TPU v7x, 32 devices: a whole 2x2x4 slice. The times are simulated.
32 devices in a mesh: fsdp: 4 (over x, core), ctx: 8 (over z, y).
Axes of the slice: x: 2, y: 2, z: 4, core: 2. Of those that a mesh axis runs over, the one named last changes fastest.
Arguments:
- prompt_in: bfloat16 [4, 1024, 1024], P('fsdp', 'ctx'), may hold values from -16 to 16
- cont_in: bfloat16 [4, 8, 512, 1024], P('fsdp', 'ctx'), may hold values from -16 to 16
- encoder: bfloat16 [4, 512, 1024], P('fsdp', 'ctx'), may hold values from -6 to 6
- prompt_start: int32 [4], P('fsdp'), may hold values from 0 to 64, as said below
- cont_start: int32 [4, 8], P('fsdp'), may hold values from 0 to 384, as said below
- self_proj: bfloat16 [1024, 3072], P(('fsdp', 'ctx')), may hold values from -0.1875 to 0.1875
- self_out: bfloat16 [1024, 1024], P(('fsdp', 'ctx')), may hold values from -1.5 to 1.5
- cross_query: bfloat16 [1024, 1024], P(('fsdp', 'ctx')), may hold values from -0.1875 to 0.1875
- cross_kv: bfloat16 [1024, 2048], P(('fsdp', 'ctx')), may hold values from -0.1875 to 0.1875
- cross_out: bfloat16 [1024, 1024], P(('fsdp', 'ctx')), may hold values from -1.5 to 1.5
- up_proj: bfloat16 [1024, 4096], P(('fsdp', 'ctx')), may hold values from -0.1875 to 0.1875
- down_proj: bfloat16 [4096, 1024], P(('fsdp', 'ctx')), may hold values from -0.09375 to 0.09375
- vec_bias: bfloat16 [7, 1024], P(None, ('fsdp', 'ctx')), may hold values from -3 to 3
- up_bias: bfloat16 [4096], P(('fsdp', 'ctx')), may hold values from -3 to 3
- ln_gain: bfloat16 [3, 1024], P(None, ('fsdp', 'ctx')), may hold values from 0.5 to 1.5
- ln_bias: bfloat16 [3, 1024], P(None, ('fsdp', 'ctx')), may hold values from -2 to 2
- prompt_cot: bfloat16 [4, 1024, 1024], P('fsdp', 'ctx'), may hold values from -6 to 6
- cont_cot: bfloat16 [4, 8, 512, 1024], P('fsdp', 'ctx'), may hold values from -6 to 6
Outputs:
- prompt_out: bfloat16 [4, 1024, 1024], P('fsdp', 'ctx')
- cont_out: bfloat16 [4, 8, 512, 1024], P('fsdp', 'ctx')
- prompt_grad: float32 [4, 1024, 1024], P('fsdp', 'ctx')
- cont_grad: float32 [4, 8, 512, 1024], P('fsdp', 'ctx')
- encoder_grad: float32 [4, 512, 1024], P('fsdp', 'ctx')
- self_proj_grad: float32 [1024, 3072], P(('fsdp', 'ctx'))
- self_out_grad: float32 [1024, 1024], P(('fsdp', 'ctx'))
- cross_query_grad: float32 [1024, 1024], P(('fsdp', 'ctx'))
- cross_kv_grad: float32 [1024, 2048], P(('fsdp', 'ctx'))
- cross_out_grad: float32 [1024, 1024], P(('fsdp', 'ctx'))
- up_proj_grad: float32 [1024, 4096], P(('fsdp', 'ctx'))
- down_proj_grad: float32 [4096, 1024], P(('fsdp', 'ctx'))
- vec_bias_grad: float32 [7, 1024], P(None, ('fsdp', 'ctx'))
- up_bias_grad: float32 [4096], P(('fsdp', 'ctx'))
- ln_gain_grad: float32 [3, 1024], P(None, ('fsdp', 'ctx'))
- ln_bias_grad: float32 [3, 1024], P(None, ('fsdp', 'ctx'))
- statistics: float32 [4, 6], P('fsdp')
Inputs may be any that keep to these rules, and one draw needn't show every extreme that they name: Prompt positions of a group before its prompt_start are left padding. Some group starts at 0 and some at 64. Places of a continuation slot before its cont_start are left padding; its tokens run to place 512 - 1. Some slot starts at 0 and some at 384.
All inputs are finite; a program needn't handle non-finite values.
Results may differ from a plain program's by a relative error of at most 0.024.
The roundings to bfloat16 on the way count: a program that leaves them out, or rounds other values in their place, can miss the bound.
Values may be sent and summed in bfloat16 or wider, within the bound.
No kernel may reach another device: no remote copies, remote signals or barrier semaphores. Data moves between devices by JAX's collectives and lax.ppermute only.
A program may use at most 320 MiB of HBM per device.

v0:
```python
from functools import partial

import jax
import jax.numpy as jnp
from jax import lax
from jax.sharding import PartitionSpec as P

HEADS = 16
HDIM = 64


def layer_norm(residual, gain_vec, shift_vec):
    row_mean = jnp.mean(residual, -1, keepdims=True)
    centred = residual - row_mean
    row_var = jnp.mean(centred * centred, -1, keepdims=True)
    return centred * lax.rsqrt(row_var + 1e-05) * gain_vec + shift_vec


def product(first_mat, second_mat):
    return jnp.dot(first_mat, second_mat, preferred_element_type=jnp.float32)


def product_tn(first_mat, second_mat):
    return lax.dot_general(
        first_mat, second_mat, (((0,), (0,)), ((), ())), preferred_element_type=jnp.float32
    )


def product_nt(first_mat, second_mat):
    return lax.dot_general(
        first_mat, second_mat, (((1,), (1,)), ((), ())), preferred_element_type=jnp.float32
    )


def split_heads(matrix):
    return matrix.reshape(matrix.shape[0], HEADS, HDIM).transpose(1, 0, 2)


def merge_heads(matrix):
    return matrix.transpose(1, 0, 2).reshape(matrix.shape[1], HEADS * HDIM)


def column_sum(matrix):
    return jnp.sum(matrix.astype(jnp.float32), 0)


def block_mask(block_index, prompt_begin, cont_begin, prompt_rows, ctx_count, slot_count, slot_len):
    prompt_len = prompt_rows * ctx_count
    positions = block_index * prompt_rows + jnp.arange(prompt_rows, dtype=jnp.int32)
    key_spots = jnp.arange(prompt_len, dtype=jnp.int32)
    prompt_part = (key_spots[None, :] <= positions[:, None]) & (
        (key_spots[None, :] >= prompt_begin) | (key_spots[None, :] == positions[:, None])
    )
    prompt_part = jnp.concatenate(
        [prompt_part, jnp.zeros((prompt_rows, slot_count * slot_len), bool)], 1
    )
    slot_index = jnp.arange(slot_count * slot_len, dtype=jnp.int32) // slot_len
    offset_in = jnp.arange(slot_count * slot_len, dtype=jnp.int32) % slot_len
    begin_at = jnp.sum(
        jnp.where(
            slot_index[:, None] == jnp.arange(slot_count, dtype=jnp.int32)[None, :],
            cont_begin[None, :],
            0,
        ),
        1,
    )
    prompt_seen = jnp.broadcast_to(
        (key_spots >= prompt_begin)[None, :], (slot_count * slot_len, prompt_len)
    )
    own_keys = (
        (slot_index[:, None] == slot_index[None, :])
        & (offset_in[None, :] <= offset_in[:, None])
        & ((offset_in[None, :] >= begin_at[:, None]) | (offset_in[None, :] == offset_in[:, None]))
    )
    cont_part = jnp.concatenate([prompt_seen, own_keys], 1)
    return jnp.concatenate([prompt_part, cont_part], 0)


def valid_mask(block_index, prompt_begin, cont_begin, prompt_rows, slot_count, slot_len):
    positions = block_index * prompt_rows + jnp.arange(prompt_rows, dtype=jnp.int32)
    slot_index = jnp.arange(slot_count * slot_len, dtype=jnp.int32) // slot_len
    offset_in = jnp.arange(slot_count * slot_len, dtype=jnp.int32) % slot_len
    begin_at = jnp.sum(
        jnp.where(
            slot_index[:, None] == jnp.arange(slot_count, dtype=jnp.int32)[None, :],
            cont_begin[None, :],
            0,
        ),
        1,
    )
    return jnp.concatenate([positions >= prompt_begin, offset_in >= begin_at]).astype(jnp.float32)


def attend_forward(queries, key_rows, value_rows, allowed):

    def one_head(per_head):
        head_query, head_key, head_value = per_head
        scores = jnp.where(allowed, product_nt(head_query, head_key), -1e30)
        row_max = jnp.max(scores, -1, keepdims=True)
        shifted = jnp.exp(scores - row_max)
        totals = jnp.sum(shifted, -1, keepdims=True)
        attn_probs = (shifted / totals).astype(jnp.bfloat16)
        return (product(attn_probs, head_value), (row_max + jnp.log(totals))[:, 0])

    mixed, log_totals = lax.map(
        one_head, (split_heads(queries), split_heads(key_rows), split_heads(value_rows))
    )
    return (merge_heads(mixed), log_totals)


def attend_backward(queries, key_rows, value_rows, grad_mixed, log_totals, allowed):

    def one_head(per_head):
        head_query, head_key, head_value, head_grad, head_log = per_head
        scores = jnp.where(allowed, product_nt(head_query, head_key), -1e30)
        attn_probs = jnp.exp(scores - head_log[:, None])
        grad_probs = product_nt(head_grad, head_value)
        row_inner = jnp.sum(attn_probs * grad_probs, -1, keepdims=True)
        grad_scores = (attn_probs * (grad_probs - row_inner)).astype(jnp.bfloat16)
        grad_query = product(grad_scores, head_key)
        grad_key = product_tn(grad_scores, head_query)
        grad_value = product_tn(attn_probs.astype(jnp.bfloat16), head_grad)
        return (grad_query, grad_key, grad_value)

    head_grads = lax.map(
        one_head,
        (
            split_heads(queries),
            split_heads(key_rows),
            split_heads(value_rows),
            split_heads(grad_mixed),
            log_totals,
        ),
    )
    return (merge_heads(head_grads[0]), merge_heads(head_grads[1]), merge_heads(head_grads[2]))


def body(
    prompt_in,
    cont_in,
    encoder,
    prompt_start,
    cont_start,
    self_proj,
    self_out,
    cross_query,
    cross_kv,
    cross_out,
    up_proj,
    down_proj,
    vec_bias,
    up_bias,
    ln_gain,
    ln_bias,
    prompt_cot,
    cont_cot,
):
    gathered = (
        lax.all_gather(self_proj, ("fsdp", "ctx"), axis=0, tiled=True),
        lax.all_gather(self_out, ("fsdp", "ctx"), axis=0, tiled=True),
        lax.all_gather(cross_query, ("fsdp", "ctx"), axis=0, tiled=True),
        lax.all_gather(cross_kv, ("fsdp", "ctx"), axis=0, tiled=True),
        lax.all_gather(cross_out, ("fsdp", "ctx"), axis=0, tiled=True),
        lax.all_gather(up_proj, ("fsdp", "ctx"), axis=0, tiled=True),
        lax.all_gather(down_proj, ("fsdp", "ctx"), axis=0, tiled=True),
        lax.all_gather(vec_bias, ("fsdp", "ctx"), axis=1, tiled=True),
        lax.all_gather(up_bias, ("fsdp", "ctx"), axis=0, tiled=True),
        lax.all_gather(ln_gain, ("fsdp", "ctx"), axis=1, tiled=True),
        lax.all_gather(ln_bias, ("fsdp", "ctx"), axis=1, tiled=True),
    )
    w_sin, w_so, w_cq, w_ckv, w_co, w_up, w_down = gathered[:7]
    biases = gathered[7].astype(jnp.float32)
    hidden_bias = gathered[8].astype(jnp.float32)
    gains = gathered[9].astype(jnp.float32)
    shifts = gathered[10].astype(jnp.float32)
    model_width = w_so.shape[0]
    scale = HDIM ** (-0.5)
    prompt_rows = prompt_in.shape[1]
    slot_count = cont_in.shape[1]
    slot_len = cont_in.shape[2]
    ctx_count = lax.axis_size("ctx")
    block_index = lax.axis_index("ctx")
    prompt_len = prompt_rows * ctx_count
    every_begin = cont_start[0]
    local_begin = lax.dynamic_slice_in_dim(every_begin, block_index * slot_count, slot_count, 0)
    tokens = jnp.concatenate(
        [prompt_in[0], cont_in[0].reshape(slot_count * slot_len, model_width)], 0
    )
    row_total = tokens.shape[0]
    allowed = block_mask(
        block_index, prompt_start[0], local_begin, prompt_rows, ctx_count, slot_count, slot_len
    )
    valid_rows = valid_mask(
        block_index, prompt_start[0], local_begin, prompt_rows, slot_count, slot_len
    )
    valid_count = (prompt_len - prompt_start[0] + jnp.sum(slot_len - every_begin)).astype(
        jnp.float32
    )
    projected = product(tokens, w_sin)
    queries = ((projected[:, :model_width] + biases[0]) * scale).astype(jnp.bfloat16)
    key_rows = projected[:, model_width : 2 * model_width].astype(jnp.bfloat16)
    value_rows = (projected[:, 2 * model_width :] + biases[1]).astype(jnp.bfloat16)
    prompt_keys, prompt_values = (
        lax.all_gather(key_rows[:prompt_rows], "ctx", axis=0, tiled=True),
        lax.all_gather(value_rows[:prompt_rows], "ctx", axis=0, tiled=True),
    )
    all_keys = jnp.concatenate([prompt_keys, key_rows[prompt_rows:]], 0)
    all_values = jnp.concatenate([prompt_values, value_rows[prompt_rows:]], 0)
    attn, self_log = attend_forward(queries, all_keys, all_values, allowed)
    attn_low = attn.astype(jnp.bfloat16)
    branch_self = product(attn_low, w_so) + biases[2]
    resid_one = tokens.astype(jnp.float32) + branch_self
    hidden_one = layer_norm(resid_one, gains[0], shifts[0]).astype(jnp.bfloat16)
    cross_queries = ((product(hidden_one, w_cq) + biases[3]) * scale).astype(jnp.bfloat16)
    local_kv = product(encoder[0], w_ckv)
    enc_keys, enc_values = (
        lax.all_gather(local_kv[:, :model_width].astype(jnp.bfloat16), "ctx", axis=0, tiled=True),
        lax.all_gather(
            (local_kv[:, model_width:] + biases[4]).astype(jnp.bfloat16), "ctx", axis=0, tiled=True
        ),
    )
    open_mask = jnp.ones((row_total, enc_keys.shape[0]), bool)
    cross_attn, cross_log = attend_forward(cross_queries, enc_keys, enc_values, open_mask)
    cross_low = cross_attn.astype(jnp.bfloat16)
    branch_cross = product(cross_low, w_co) + biases[5]
    resid_two = hidden_one.astype(jnp.float32) + branch_cross
    hidden_two = layer_norm(resid_two, gains[1], shifts[1]).astype(jnp.bfloat16)
    pre_act = product(hidden_two, w_up) + hidden_bias
    gelu_value, gelu_pull = jax.vjp(partial(jax.nn.gelu, approximate=False), pre_act)
    act_low = gelu_value.astype(jnp.bfloat16)
    branch_ffn = product(act_low, w_down) + biases[6]
    resid_three = hidden_two.astype(jnp.float32) + branch_ffn
    output = layer_norm(resid_three, gains[2], shifts[2])
    square_sums = jnp.stack(
        [
            jnp.sum(valid_rows[:, None] * member * member)
            for member in (
                tokens.astype(jnp.float32),
                branch_self,
                hidden_one.astype(jnp.float32),
                branch_cross,
                hidden_two.astype(jnp.float32),
                branch_ffn,
            )
        ]
    )
    square_sums = lax.psum(square_sums, "ctx")
    statistics = (square_sums / (valid_count * model_width))[None]
    grad_out = jnp.concatenate(
        [prompt_cot[0], cont_cot[0].reshape(slot_count * slot_len, model_width)], 0
    ).astype(jnp.float32)
    norm_value, norm_pull = jax.vjp(layer_norm, resid_three, gains[2], shifts[2])
    grad_three, gain_three, shift_three = norm_pull(grad_out)
    grad_ffn = grad_three.astype(jnp.bfloat16)
    grad_down = product_tn(act_low, grad_ffn)
    bias_six = column_sum(grad_ffn)
    grad_pre = gelu_pull(product_nt(grad_ffn, w_down))[0].astype(jnp.bfloat16)
    grad_up = product_tn(hidden_two, grad_pre)
    grad_up_bias = column_sum(grad_pre)
    down_total, up_total, up_bias_total = (grad_down, grad_up, grad_up_bias)
    grad_hidden_two = grad_three + product_nt(grad_pre, w_up)
    norm_value, norm_pull = jax.vjp(layer_norm, resid_two, gains[1], shifts[1])
    grad_two, gain_two, shift_two = norm_pull(grad_hidden_two)
    grad_cross = grad_two.astype(jnp.bfloat16)
    grad_co = product_tn(cross_low, grad_cross)
    bias_five = column_sum(grad_cross)
    grad_cattn = product_nt(grad_cross, w_co).astype(jnp.bfloat16)
    cross_gq, cross_gk, cross_gv = attend_backward(
        cross_queries, enc_keys, enc_values, grad_cattn, cross_log, open_mask
    )
    grad_cq_pre = (cross_gq.astype(jnp.bfloat16).astype(jnp.float32) * scale).astype(jnp.bfloat16)
    grad_cq = product_tn(hidden_one, grad_cq_pre)
    bias_three = column_sum(grad_cq_pre)
    enc_gk, enc_gv = (
        lax.psum_scatter(
            cross_gk.astype(jnp.bfloat16), "ctx", scatter_dimension=0, tiled=True
        ).astype(jnp.float32),
        lax.psum_scatter(
            cross_gv.astype(jnp.bfloat16), "ctx", scatter_dimension=0, tiled=True
        ).astype(jnp.float32),
    )
    enc_grad_kv = jnp.concatenate([enc_gk.astype(jnp.bfloat16), enc_gv.astype(jnp.bfloat16)], 1)
    grad_ckv = product_tn(encoder[0], enc_grad_kv)
    bias_four = column_sum(enc_grad_kv[:, model_width:])
    encoder_grad = product_nt(enc_grad_kv, w_ckv)[None]
    cq_total, ckv_total, co_total = (grad_cq, grad_ckv, grad_co)
    grad_hidden_one = grad_two + product_nt(grad_cq_pre, w_cq)
    norm_value, norm_pull = jax.vjp(layer_norm, resid_one, gains[0], shifts[0])
    grad_one, gain_one, shift_one = norm_pull(grad_hidden_one)
    grad_self = grad_one.astype(jnp.bfloat16)
    grad_so = product_tn(attn_low, grad_self)
    bias_two = column_sum(grad_self)
    grad_attn = product_nt(grad_self, w_so).astype(jnp.bfloat16)
    self_gq, self_gk, self_gv = attend_backward(
        queries, all_keys, all_values, grad_attn, self_log, allowed
    )
    prompt_gk, prompt_gv = (
        lax.psum_scatter(
            self_gk[:prompt_len].astype(jnp.bfloat16), "ctx", scatter_dimension=0, tiled=True
        ).astype(jnp.float32),
        lax.psum_scatter(
            self_gv[:prompt_len].astype(jnp.bfloat16), "ctx", scatter_dimension=0, tiled=True
        ).astype(jnp.float32),
    )
    key_grad = jnp.concatenate([prompt_gk, self_gk[prompt_len:]], 0).astype(jnp.bfloat16)
    value_grad = jnp.concatenate([prompt_gv, self_gv[prompt_len:]], 0).astype(jnp.bfloat16)
    query_grad = (self_gq.astype(jnp.bfloat16).astype(jnp.float32) * scale).astype(jnp.bfloat16)
    grad_qkv = jnp.concatenate([query_grad, key_grad, value_grad], 1)
    grad_sin = product_tn(tokens, grad_qkv)
    bias_zero = column_sum(query_grad)
    bias_one = column_sum(value_grad)
    input_grad = grad_one + product_nt(grad_qkv, w_sin)
    bias_grad = jnp.stack(
        [bias_zero, bias_one, bias_two, bias_three, bias_four, bias_five, bias_six]
    )
    gain_grad = jnp.stack([gain_one, gain_two, gain_three])
    shift_grad = jnp.stack([shift_one, shift_two, shift_three])
    (
        sin_total,
        so_total,
        cq_total,
        ckv_total,
        co_total,
        up_total,
        down_total,
        bias_total,
        up_bias_total,
        gain_total,
        shift_total,
    ) = (
        lax.psum_scatter(grad_sin, ("fsdp", "ctx"), scatter_dimension=0, tiled=True),
        lax.psum_scatter(grad_so, ("fsdp", "ctx"), scatter_dimension=0, tiled=True),
        lax.psum_scatter(cq_total, ("fsdp", "ctx"), scatter_dimension=0, tiled=True),
        lax.psum_scatter(ckv_total, ("fsdp", "ctx"), scatter_dimension=0, tiled=True),
        lax.psum_scatter(co_total, ("fsdp", "ctx"), scatter_dimension=0, tiled=True),
        lax.psum_scatter(up_total, ("fsdp", "ctx"), scatter_dimension=0, tiled=True),
        lax.psum_scatter(down_total, ("fsdp", "ctx"), scatter_dimension=0, tiled=True),
        lax.psum_scatter(bias_grad, ("fsdp", "ctx"), scatter_dimension=1, tiled=True),
        lax.psum_scatter(up_bias_total, ("fsdp", "ctx"), scatter_dimension=0, tiled=True),
        lax.psum_scatter(gain_grad, ("fsdp", "ctx"), scatter_dimension=1, tiled=True),
        lax.psum_scatter(shift_grad, ("fsdp", "ctx"), scatter_dimension=1, tiled=True),
    )
    prompt_out = output[:prompt_rows].astype(jnp.bfloat16)[None]
    cont_out = (
        output[prompt_rows:].reshape(slot_count, slot_len, model_width).astype(jnp.bfloat16)[None]
    )
    prompt_grad = input_grad[:prompt_rows][None]
    cont_grad = input_grad[prompt_rows:].reshape(slot_count, slot_len, model_width)[None]
    return (
        prompt_out,
        cont_out,
        prompt_grad,
        cont_grad,
        encoder_grad,
        sin_total,
        so_total,
        cq_total,
        ckv_total,
        co_total,
        up_total,
        down_total,
        bias_total,
        up_bias_total,
        gain_total,
        shift_total,
        statistics,
    )


def solution(mesh):
    placed = (
        P("fsdp", "ctx", None),
        P("fsdp", "ctx", None, None),
        P("fsdp", "ctx", None),
        P("fsdp"),
        P("fsdp", None),
        P(("fsdp", "ctx"), None),
        P(("fsdp", "ctx"), None),
        P(("fsdp", "ctx"), None),
        P(("fsdp", "ctx"), None),
        P(("fsdp", "ctx"), None),
        P(("fsdp", "ctx"), None),
        P(("fsdp", "ctx"), None),
        P(None, ("fsdp", "ctx")),
        P(("fsdp", "ctx")),
        P(None, ("fsdp", "ctx")),
        P(None, ("fsdp", "ctx")),
        P("fsdp", "ctx", None),
        P("fsdp", "ctx", None, None),
    )
    return jax.shard_map(
        body,
        mesh=mesh,
        in_specs=placed,
        out_specs=(
            P("fsdp", "ctx", None),
            P("fsdp", "ctx", None, None),
            P("fsdp", "ctx", None),
            P("fsdp", "ctx", None, None),
            P("fsdp", "ctx", None),
            P(("fsdp", "ctx"), None),
            P(("fsdp", "ctx"), None),
            P(("fsdp", "ctx"), None),
            P(("fsdp", "ctx"), None),
            P(("fsdp", "ctx"), None),
            P(("fsdp", "ctx"), None),
            P(("fsdp", "ctx"), None),
            P(None, ("fsdp", "ctx")),
            P(("fsdp", "ctx")),
            P(None, ("fsdp", "ctx")),
            P(None, ("fsdp", "ctx")),
            P("fsdp", None),
        ),
        check_vma=False,
    )
```

profile of v0, /device:TPU:0, one launch (start us, length us, event | category | flops | bytes accessed | tf_op | source)
XLA Modules:
  0.0 3215.1 jit_solution(13274154373689634974)
XLA Ops:
  8.7 70.8 %all-gather = bf16[32,32,7]{1,2,0:T(8,128)(2,1)S(1)} all-gather(bf16[1,32,7]{1,2,0:T(8,128)(2,1)} %bitcast.425), channel_id=1, replica_groups=mesh['fsdp'=4,'ctx'=8] {'fsdp','ctx'}, dimensions={0}, use_global_device_ids=true | all-gather | bytes 14784 | tf_op jit(solution)/shard_map/all_gather | solution.py:166
  84.9 62.0 %all-gather.16.cloned.1.call-done = bf16[1024,3072]{1,0:T(8,128)(2,1)} async-done(((bf16[32,3072]{1,0:T(8,128)(2,1)}), bf16[1024,3072]{1,0:T(8,128)(2,1)}) %all-gather.16.cloned.1.call-update) | async-done | bytes 6291472 | tf_op jit(solution)/shard_map/all_gather | solution.py:159
  146.9 9.0 fusion.125
  167.8 66.0 %all-gather.1 = bf16[32,32,3]{1,2,0:T(4,128)(2,1)S(1)} all-gather(bf16[1,32,3]{1,2,0:T(4,128)(2,1)S(1)} %bitcast.426), channel_id=1, replica_groups=mesh['fsdp'=4,'ctx'=8] {'fsdp','ctx'}, dimensions={0}, use_global_device_ids=true | all-gather | bytes 6336 | tf_op jit(solution)/shard_map/all_gather | solution.py:168
  234.5 63.8 %all-gather.2 = bf16[32,32,3]{1,2,0:T(4,128)(2,1)S(1)} all-gather(bf16[1,32,3]{1,2,0:T(4,128)(2,1)S(1)} %bitcast.427), channel_id=1, replica_groups=mesh['fsdp'=4,'ctx'=8] {'fsdp','ctx'}, dimensions={0}, use_global_device_ids=true | all-gather | bytes 6336 | tf_op jit(solution)/shard_map/all_gather | solution.py:169
  299.0 65.4 %all-gather.3 = bf16[32,1,128]{2,1,0:T(2,128)(2,1)S(1)} all-gather(bf16[1,1,128]{2,1,0:T(2,128)(2,1)S(1)} %bitcast.428), channel_id=1, replica_groups=mesh['fsdp'=4,'ctx'=8] {'fsdp','ctx'}, dimensions={0}, use_global_device_ids=true | all-gather | bytes 8448 | tf_op jit(solution)/shard_map/all_gather | solution.py:167
  385.2 4.0 pad_maximum_fusion.1
  389.3 4.6 copy.99
  393.9 6.6 copy.102
  404.5 4.6 copy.98
  409.2 6.6 copy.101
  416.9 133.8 %while.52 = (s32[]{:T(128)}, bf16[16,640,64]{1,2,0:T(8,128)(2,1)}, f32[16,640]{1,0:T(8,128)S(1)}, bf16[16,640,64]{2,1,0:T(8,128)(2,1)}, bf16[16,1536,64]{2,1,0:T...) while((s32[]{:T(128)}, bf16[16,640,64]{1,2,0:T(8,128)(2,1)}, ...), condition=%wide.region_3.4_spmd, body=%wide.region_0.3_spmd.sunk | while | flops 258538880 | bytes 29655164 | solution.py:105
  550.8 5.9 fusion.119
  559.7 4.3 multiply_convert_fusion.5
  570.4 85.5 %while.53 = (s32[]{:T(128)}, bf16[16,640,64]{1,2,0:T(8,128)(2,1)}, f32[16,640]{1,0:T(8,128)}, bf16[16,640,64]{2,1,0:T(8,128)(2,1)}, bf16[16,512,64]{2,1,0:T(8,12...) while((s32[]{:T(128)}, bf16[16,640,64]{1,2,0:T(8,128)(2,1)}, f32[16,640]{1,0:T(8,128)}, ...), condition=%wide.region_9.10_spmd, body=%wide.region_6.9_spmd.sunk | while | flops 85851520 | bytes 4554841 | solution.py:105
  657.2 5.5 fusion.118
  663.4 33.6 %multiply_convert_fusion.2 = (bf16[640,4096]{1,0:T(8,128)(2,1)}, f32[640,4096]{1,0:T(8,128)}, f32[640,4096]{1,0:T(8,128)}) fusion(f32[4096]{0:T(1024)S(1)} %bitcast.407, bf16[1024,4096]{1,0:T(8,128)(2,1)} %all-gather.34.cloned.1.call-done, f32[640,1024]{1,0:T(8,128)S(1)} %get-tuple-element.467, f32[1024]{0:T(1024)S(1)} %bitcast.387, ...), kind=kOutput, calls=%fused_computation.99 | convolution fusion | flops 5545000960 | bytes 37254144 | tf_op jit(solution)/shard_map/dot_general | solution.py:20
  697.1 13.6 fusion.88
  717.5 18.5 convert_reduce_fusion
  736.0 11.4 multiply_reduce_fusion.2
  756.0 145.5 %while.54 = (s32[]{:T(128)}, bf16[16,640,64]{1,2,0:T(8,128)(2,1)}, bf16[16,512,64]{1,2,0:T(8,128)(2,1)}, bf16[16,512,64]{1,2,0:T(8,128)(2,1)}, bf16[16,640,64]{2...) while((s32[]{:T(128)}, bf16[16,640,64]{1,2,0:T(8,128)(2,1)}, ...), condition=%wide.region_20.21_spmd, body=%wide.region_18.20_spmd.sunk | while | flops 212008320 | bytes 11159145 | solution.py:125
  904.0 5.1 multiply_reduce_fusion.3
  919.0 180.8 %while.55 = (s32[]{:T(128)}, bf16[16,640,64]{1,2,0:T(8,128)(2,1)S(1)}, bf16[16,1536,64]{1,2,0:T(8,128)(2,1)}, bf16[16,1536,64]{1,2,0:T(8,128)(2,1)}, bf16[16,640...) while((s32[]{:T(128)}, ...), condition=%wide.region_25.26_spmd, body=%wide.region_23.25_spmd.sunk | while | flops 637009280 | bytes 33113712 | solution.py:125
  1119.2 50.4 %reduce-scatter.45.cloned.1.call-done = bf16[128,1024]{1,0:T(8,128)(2,1)} async-done(((bf16[1024,1024]{1,0:T(8,128)(2,1)}), bf16[128,1024]{1,0:T(8,128)(2,1)}) %reduce-scatter.45.cloned.1.call-update) | async-done | bytes 262160
  1172.2 5.1 fusion.129
  1178.6 5.2 fusion.128
  1185.1 5.1 fusion.127
  1190.5 45.2 %reduce-scatter.47.cloned.1.call-done = bf16[64,1024]{1,0:T(8,128)(2,1)} async-done(((bf16[512,1024]{1,0:T(8,128)(2,1)}), bf16[64,1024]{1,0:T(8,128)(2,1)}) %reduce-scatter.47.cloned.1.call-update) | async-done | bytes 131088
  1236.8 4.5 convolution_bitcast_fusion.7
  1241.3 9.3 copy.130
  1253.1 52.8 %reduce-scatter.43.cloned.1.call-done = bf16[128,1024]{1,0:T(8,128)(2,1)} async-done(((bf16[1024,1024]{1,0:T(8,128)(2,1)}), bf16[128,1024]{1,0:T(8,128)(2,1)}) %reduce-scatter.43.cloned.1.call-update) | async-done | bytes 262160
  1307.1 11.3 fusion.111
  1320.1 13.0 fusion.126
  1334.3 12.7 fusion.130
  1352.9 19.1 psum.7
  1372.0 37.0 %all-reduce.1 = f32[4096]{0:T(1024)S(1)} all-reduce(f32[4096]{0:T(1024)S(1)} %copy-done.46), channel_id=14, replica_groups=mesh['fsdp'=4,'ctx'=8] {'fsdp','ctx'}, use_global_device_ids=true, to_apply=%region_46.47.clone | all-reduce | flops 4096 | bytes 32768
  1411.9 29.4 reduce-scatter.57.cloned.1.call-done
  1442.7 131.4 %reduce-scatter.55.cloned.1.call-done = f32[32,3]{1,0:T(8,128)} async-done(((f32[1024,3]{1,0:T(8,128)}), f32[32,3]{1,0:T(8,128)}) %reduce-scatter.55.cloned.1.call-update) | async-done | bytes 400
  1575.4 4.4 convolution_bitcast_fusion.8
  1579.9 7.6 add_add_fusion.3
  1589.8 116.8 %reduce-scatter.53.cloned.1.call-done = f32[32,7]{1,0:T(8,128)} async-done(((f32[1024,7]{1,0:T(8,128)}), f32[32,7]{1,0:T(8,128)}) %reduce-scatter.53.cloned.1.call-update) | async-done | bytes 912
  1708.0 142.0 %reduce-scatter.37.cloned.1.call-done = f32[32,1024]{1,0:T(8,128)} async-done(((f32[1024,1024]{1,0:T(8,128)}), f32[32,1024]{1,0:T(8,128)}) %reduce-scatter.37.cloned.1.call-update) | async-done | bytes 131088 | tf_op jit(solution)/shard_map/reduce_scatter | solution.py:335
  1849.9 145.4 %reduce-scatter.35.cloned.1.call-done = f32[32,1024]{1,0:T(8,128)} async-done(((f32[1024,1024]{1,0:T(8,128)}), f32[32,1024]{1,0:T(8,128)}) %reduce-scatter.35.cloned.1.call-update) | async-done | bytes 131088 | tf_op jit(solution)/shard_map/reduce_scatter | solution.py:333
  1995.3 144.2 %reduce-scatter.33.cloned.1.call-done = f32[32,1024]{1,0:T(8,128)} async-done(((f32[1024,1024]{1,0:T(8,128)}), f32[32,1024]{1,0:T(8,128)}) %reduce-scatter.33.cloned.1.call-update) | async-done | bytes 131088 | tf_op jit(solution)/shard_map/reduce_scatter | solution.py:332
  2139.5 185.5 %reduce-scatter.51.cloned.1.call-done = f32[32,2048]{1,0:T(8,128)} async-done(((f32[1024,2048]{1,0:T(8,128)}), f32[32,2048]{1,0:T(8,128)}) %reduce-scatter.51.cloned.1.call-update) | async-done | bytes 262160
  2325.0 163.0 %reduce-scatter.31.cloned.1.call-done = f32[32,3072]{1,0:T(8,128)} async-done(((f32[1024,3072]{1,0:T(8,128)}), f32[32,3072]{1,0:T(8,128)}) %reduce-scatter.31.cloned.1.call-update) | async-done | bytes 393232 | tf_op jit(solution)/shard_map/reduce_scatter | solution.py:331
  2488.0 359.9 %reduce-scatter.39.cloned.1.call-done = f32[32,4096]{1,0:T(8,128)} async-done(((f32[1024,4096]{1,0:T(8,128)}), f32[32,4096]{1,0:T(8,128)}) %reduce-scatter.39.cloned.1.call-update) | async-done | bytes 524304 | tf_op jit(solution)/shard_map/reduce_scatter | solution.py:336
  2847.9 360.2 %reduce-scatter.41.cloned.1.call-done = f32[128,1024]{1,0:T(8,128)} async-done(((f32[4096,1024]{1,0:T(8,128)}), f32[128,1024]{1,0:T(8,128)}) %reduce-scatter.41.cloned.1.call-update) | async-done | bytes 524304 | tf_op jit(solution)/shard_map/reduce_scatter | solution.py:337
  (762 shorter events, 675.0 us)
Async XLA Ops:
  7.2 73.1 %copy-start = (bf16[1,64,1024]{2,1,0:T(8,128)(2,1)S(1)}, bf16[1,64,1024]{2,1,0:T(8,128)(2,1)}, u32[]{:S(2)}) copy-start(bf16[1,64,1024]{2,1,0:T(8,128)(2,1)} %param.28) | copy-start | bytes 393220
  7.2 73.1 %all-gather.26.cloned.1.call-start = ((), (), s32[]{:S(2)}) async-start(), calls=%async_computation.19 | async-start | bytes 4325376 | tf_op jit(solution)/shard_map/all_gather | solution.py:162
  7.9 139.0 %all-gather.16.cloned.1.call-start = ((), (), s32[]{:S(2)}) async-start(), calls=%async_computation.14 | async-start | bytes 6488064 | tf_op jit(solution)/shard_map/all_gather | solution.py:159
  8.7 357.8 %all-gather.30.cloned.1.call-start = ((), (), s32[]{:S(2)}) async-start(), calls=%async_computation.21 | async-start | bytes 1179648 | tf_op jit(solution)/shard_map/all_gather | solution.py:218
  80.3 66.7 %copy-start.66 = (bf16[1,1,512,1024]{3,2,1,0:T(8,128)(2,1)S(1)}, bf16[1,1,512,1024]{3,2,1,0:T(8,128)(2,1)}, u32[]{:S(2)}) copy-start(bf16[1,1,512,1024]{3,2,1,0:T(8,128)(2,1)} %param.27) | copy-start | bytes 3145732
  80.3 66.7 %copy-start.67 = (bf16[1,128,1024]{2,1,0:T(8,128)(2,1)S(1)}, bf16[1,128,1024]{2,1,0:T(8,128)(2,1)}, u32[]{:S(2)}) copy-start(bf16[1,128,1024]{2,1,0:T(8,128)(2,1)} %param.26) | copy-start | bytes 786436
  84.1 286.1 %all-gather.28.cloned.1.call-start = ((), (), s32[]{:S(2)}) async-start(), calls=%async_computation.20 | async-start | bytes 1179648 | tf_op jit(solution)/shard_map/all_gather | solution.py:217
  84.9 300.4 %all-gather.20.cloned.1.call-start = ((), (), s32[]{:S(2)}) async-start(), calls=%async_computation.16 | async-start | bytes 2359296 | tf_op jit(solution)/shard_map/all_gather | solution.py:205
  156.0 78.5 %copy-start.62 = (bf16[3,32]{1,0:T(4,128)(2,1)S(1)}, bf16[3,32]{1,0:T(4,128)(2,1)}, u32[]{:S(2)}) copy-start(bf16[3,32]{1,0:T(4,128)(2,1)} %param.41) | copy-start | bytes 580
  157.9 141.1 %copy-start.63 = (bf16[128]{0:T(256)(128)(2,1)S(1)}, bf16[128]{0:T(256)(128)(2,1)}, u32[]{:S(2)}) copy-start(bf16[128]{0:T(256)(128)(2,1)} %param.39) | copy-start | bytes 772
  159.8 240.7 %all-gather.18.cloned.1.call-start = ((), (), s32[]{:S(2)}) async-start(), calls=%async_computation.15 | async-start | bytes 2359296 | tf_op jit(solution)/shard_map/all_gather | solution.py:204
  161.5 389.3 %all-gather.22.cloned.1.call-start = ((), (), s32[]{:S(2)}) async-start(), calls=%async_computation.17 | async-start | bytes 2162688 | tf_op jit(solution)/shard_map/all_gather | solution.py:160
  162.3 396.4 %all-gather.24.cloned.1.call-start = ((), (), s32[]{:S(2)}) async-start(), calls=%async_computation.18 | async-start | bytes 2162688 | tf_op jit(solution)/shard_map/all_gather | solution.py:161
  163.0 492.9 %all-gather.32.cloned.1.call-start = ((), (), s32[]{:S(2)}) async-start(), calls=%async_computation.22 | async-start | bytes 2162688 | tf_op jit(solution)/shard_map/all_gather | solution.py:163
  163.8 499.4 %all-gather.34.cloned.1.call-start = ((), (), s32[]{:S(2)}) async-start(), calls=%async_computation.23 | async-start | bytes 8650752 | tf_op jit(solution)/shard_map/all_gather | solution.py:164
  164.3 532.7 %all-gather.36.cloned.1.call-start = ((), (), s32[]{:S(2)}) async-start(), calls=%async_computation.24 | async-start | bytes 8650752 | tf_op jit(solution)/shard_map/all_gather | solution.py:165
  165.1 952.9 %reduce-scatter.49.cloned.1.call-start = ((), (), s32[]{:S(2)}) async-start(), calls=%async_computation.34 | async-start | bytes 1179648
  299.0 398.1 %copy-start.30 = (f32[1,1024]{1,0:T(1,128)}, f32[1,1024]{1,0:T(1,128)S(1)}, u32[]{:S(2)}) copy-start(f32[1,1024]{1,0:T(1,128)S(1)} %get-tuple-element.494) | copy-start | bytes 12292
  416.9 133.8 %copy-start.56 = (f32[1,1024]{1,0:T(1,128)S(1)}, f32[1,1024]{1,0:T(1,128)}, u32[]{:S(2)}) copy-start(f32[1,1024]{1,0:T(1,128)} %get-tuple-element.487) | copy-start | bytes 12292
  416.9 133.8 %copy-start.68 = (bf16[1,128,1024]{2,1,0:T(8,128)(2,1)S(1)}, bf16[1,128,1024]{2,1,0:T(8,128)(2,1)}, u32[]{:S(2)}) copy-start(bf16[1,128,1024]{2,1,0:T(8,128)(2,1)} %param.26) | copy-start | bytes 786436
  662.7 84.8 %copy-start.4 = (f32[640,1024]{1,0:T(8,128)}, f32[640,1024]{1,0:T(8,128)S(1)}, u32[]{:S(2)}) copy-start(f32[640,1024]{1,0:T(8,128)S(1)} %get-tuple-element.467) | copy-start | bytes 7864324
  663.4 33.6 %copy-start.55 = (f32[1,1024]{1,0:T(1,128)S(1)}, f32[1,1024]{1,0:T(1,128)}, u32[]{:S(2)}) copy-start(f32[1,1024]{1,0:T(1,128)} %get-tuple-element.484) | copy-start | bytes 12292
  663.4 33.6 %copy-start.57 = (f32[1,1024]{1,0:T(1,128)S(1)}, f32[1,1024]{1,0:T(1,128)}, u32[]{:S(2)}) copy-start(f32[1,1024]{1,0:T(1,128)} %get-tuple-element.487) | copy-start | bytes 12292
  663.4 33.6 %copy-start.60 = (f32[640]{0:T(1024)S(1)}, f32[640]{0:T(1024)}, u32[]{:S(2)}) copy-start(f32[640]{0:T(1024)} %add_convert_fusion.7) | copy-start | bytes 7684
  663.4 33.6 %copy-start.69 = (bf16[1,128,1024]{2,1,0:T(8,128)(2,1)S(1)}, bf16[1,128,1024]{2,1,0:T(8,128)(2,1)}, u32[]{:S(2)}) copy-start(bf16[1,128,1024]{2,1,0:T(8,128)(2,1)} %param.26) | copy-start | bytes 786436
  756.0 147.9 %copy-start.11 = (f32[640,1024]{1,0:T(8,128)S(1)}, f32[640,1024]{1,0:T(8,128)}, u32[]{:S(2)}) copy-start(f32[640,1024]{1,0:T(8,128)} %copy-done.10) | copy-start | bytes 7864324
  918.8 250.9 %reduce-scatter.45.cloned.1.call-start = ((), (), s32[]{:S(2)}) async-start(), calls=%async_computation.32 | async-start | bytes 2359296
  1104.2 131.5 %reduce-scatter.47.cloned.1.call-start = ((), (), s32[]{:S(2)}) async-start(), calls=%async_computation.33 | async-start | bytes 1179648
  1106.8 199.1 %reduce-scatter.43.cloned.1.call-start = ((), (), s32[]{:S(2)}) async-start(), calls=%async_computation.31 | async-start | bytes 2359296
  1111.3 329.9 %reduce-scatter.57.cloned.1.call-start = ((), (), s32[]{:S(2)}) async-start(), calls=%async_computation.38 | async-start | bytes 540672
  1115.2 458.8 %reduce-scatter.55.cloned.1.call-start = ((), (), s32[]{:S(2)}) async-start(), calls=%async_computation.37 | async-start | bytes 540672
  1115.3 55.7 %copy-start.51 = (f32[1024]{0:T(1024)S(1)}, f32[1024]{0:T(1024)}, u32[]{:S(2)}) copy-start(f32[1024]{0:T(1024)} %get-tuple-element.446) | copy-start | bytes 12292
  1115.3 55.7 %copy-start.52 = (f32[1024]{0:T(1024)S(1)}, f32[1024]{0:T(1024)}, u32[]{:S(2)}) copy-start(f32[1024]{0:T(1024)} %get-tuple-element.448) | copy-start | bytes 12292
  1115.3 55.7 %copy-start.53 = (f32[1024]{0:T(1024)S(1)}, f32[1024]{0:T(1024)}, u32[]{:S(2)}) copy-start(f32[1024]{0:T(1024)} %get-tuple-element.452) | copy-start | bytes 12292
  1116.7 190.3 %copy-start.15 = (bf16[512,16,64]{0,2,1:T(8,128)(2,1)}, bf16[512,16,64]{0,2,1:T(8,128)(2,1)S(1)}, u32[]{:S(2)}) copy-start(bf16[512,16,64]{0,2,1:T(8,128)(2,1)S(1)} %slice.166) | copy-start | bytes 3145732
  1116.7 55.5 %copy-start.23 = (bf16[16,640,64]{1,2,0:T(8,128)(2,1)S(1)}, bf16[16,640,64]{1,2,0:T(8,128)(2,1)}, u32[]{:S(2)}) copy-start(bf16[16,640,64]{1,2,0:T(8,128)(2,1)} %get-tuple-element.192) | copy-start | bytes 3932164
  1117.9 588.7 %reduce-scatter.53.cloned.1.call-start = ((), (), s32[]{:S(2)}) async-start(), calls=%async_computation.36 | async-start | bytes 540672
  1172.2 677.8 %reduce-scatter.37.cloned.1.call-start = ((), (), s32[]{:S(2)}) async-start(), calls=%async_computation.28 | async-start | bytes 4325376 | tf_op jit(solution)/shard_map/reduce_scatter | solution.py:335
  1177.3 818.0 %reduce-scatter.35.cloned.1.call-start = ((), (), s32[]{:S(2)}) async-start(), calls=%async_computation.27 | async-start | bytes 4325376 | tf_op jit(solution)/shard_map/reduce_scatter | solution.py:333
  1183.8 955.7 %reduce-scatter.33.cloned.1.call-start = ((), (), s32[]{:S(2)}) async-start(), calls=%async_computation.26 | async-start | bytes 4325376 | tf_op jit(solution)/shard_map/reduce_scatter | solution.py:332
  1190.3 1134.8 %reduce-scatter.51.cloned.1.call-start = ((), (), s32[]{:S(2)}) async-start(), calls=%async_computation.35 | async-start | bytes 8650752
  1250.6 56.4 %copy-start.20 = (bf16[16,640,64]{1,2,0:T(8,128)(2,1)S(1)}, bf16[16,640,64]{1,2,0:T(8,128)(2,1)}, u32[]{:S(2)}) copy-start(bf16[16,640,64]{1,2,0:T(8,128)(2,1)} %get-tuple-element.455) | copy-start | bytes 3932164
  1250.6 1237.4 %reduce-scatter.31.cloned.1.call-start = ((), (), s32[]{:S(2)}) async-start(), calls=%async_computation.25 | async-start | bytes 12976128 | tf_op jit(solution)/shard_map/reduce_scatter | solution.py:331
  1318.3 1529.6 %reduce-scatter.39.cloned.1.call-start = ((), (), s32[]{:S(2)}) async-start(), calls=%async_computation.29 | async-start | bytes 17301504 | tf_op jit(solution)/shard_map/reduce_scatter | solution.py:336
  1333.1 1875.1 %reduce-scatter.41.cloned.1.call-start = ((), (), s32[]{:S(2)}) async-start(), calls=%async_computation.30 | async-start | bytes 17301504 | tf_op jit(solution)/shard_map/reduce_scatter | solution.py:337
  1347.1 63.1 %copy-start.13 = (bf16[640,1024]{1,0:T(8,128)(2,1)S(1)}, bf16[640,1024]{1,0:T(8,128)(2,1)}, u32[]{:S(2)}) copy-start(bf16[640,1024]{1,0:T(8,128)(2,1)} %get-tuple-element.482) | copy-start | bytes 3932164
  1411.9 167.9 %copy-start.9 = (f32[640,1024]{1,0:T(8,128)S(1)}, f32[640,1024]{1,0:T(8,128)}, u32[]{:S(2)}) copy-start(f32[640,1024]{1,0:T(8,128)} %copy-done.8) | copy-start | bytes 7864324
  1411.9 167.9 %copy-start.49 = (f32[640]{0:T(1024)S(1)}, f32[640]{0:T(1024)}, u32[]{:S(2)}) copy-start(f32[640]{0:T(1024)} %copy-done.48) | copy-start | bytes 7684
  (64 other events, 228.9 us)
Sparse Core Ops, SparseCore 0:
  11.1 64.6 all-gather.25
  78.7 68.1 all-gather.15
  149.6 38.6 all-gather.29
  190.9 39.0 all-gather.27
  232.5 48.3 all-gather.19
  283.5 47.9 all-gather.17
  334.4 55.0 all-gather.21
  392.5 55.3 all-gather.23
  450.9 55.4 all-gather.31
  509.2 76.1 all-gather.33
  588.3 76.0 all-gather.35
  918.9 60.8 reduce-scatter.48
  1104.4 65.2 reduce-scatter.44
  1173.3 62.4 reduce-scatter.46
  1239.1 66.7 reduce-scatter.42
  1308.0 133.2 reduce-scatter.56
  1444.0 129.9 reduce-scatter.54
  1576.1 130.3 reduce-scatter.52
  1709.5 140.3 reduce-scatter.36
  1852.7 142.5 reduce-scatter.34
  1998.3 141.2 reduce-scatter.32
  2142.5 182.4 reduce-scatter.50
  2332.6 155.3 reduce-scatter.30
  2490.7 357.1 reduce-scatter.38
  2850.8 357.3 reduce-scatter.40
where the time goes:
time: 3230 us; the launch traced here: 3220 us
  waiting for transfers between devices  1990 us (62%)
  matrix products  616 us (19%)
  blocking collectives  322 us (10%)
  local copies, waits for them, and re-layouts  210 us (7%)
  other arithmetic  54.6 us (2%)
    unnamed x33, waiting for transfers between devices  616 us
    reduce_scatter x1, waiting for transfers between devices, body(): lax.psum_scatter(down_total, ('fsdp', 'ctx'), scatter_dimension=0, tiled=...  360 us
    reduce_scatter x1, waiting for transfers between devices, body(): lax.psum_scatter(up_total, ('fsdp', 'ctx'), scatter_dimension=0, tiled=True)  360 us
    dot_general x71, matrix products, product(): return jnp.dot(first_mat, second_mat, preferred_element_type=jnp.float32)  222 us
    dot_general x103, matrix products, product_nt(): lax.dot_general(first_mat, second_mat, (((1,), (1,)), ((), ())), preferre...  211 us
    dot_general x71, matrix products, product_tn(): lax.dot_general(first_mat, second_mat, (((0,), (0,)), ((), ())), preferre...  183 us
    reduce_scatter x1, waiting for transfers between devices, body(): lax.psum_scatter(grad_sin, ('fsdp', 'ctx'), scatter_dimension=0, tiled=True)  163 us
    reduce_scatter x1, waiting for transfers between devices, body(): lax.psum_scatter(cq_total, ('fsdp', 'ctx'), scatter_dimension=0, tiled=True)  145 us
  transfers between devices with their start and end apart: 25, of which 14 were waited for; matrix products, arithmetic and copies ran while one was open for 19% of the time, Pallas kernels for 0%

commit v1 on v0

v1 whole, which is shorter than its diff:
```python
import functools

import jax
import jax.numpy as jnp
from jax import lax
from jax.experimental import pallas as pl
from jax.experimental.pallas import tpu as pltpu
from jax.sharding import Mesh
from jax.sharding import PartitionSpec as P

HEADS = 16
HDIM = 64
MASKED = -1e30


def product(first_mat, second_mat):
    return jnp.dot(first_mat, second_mat, preferred_element_type=jnp.float32)


def product_tn(first_mat, second_mat):
    return lax.dot_general(
        first_mat, second_mat, (((0,), (0,)), ((), ())), preferred_element_type=jnp.float32
    )


def product_nt(first_mat, second_mat):
    return lax.dot_general(
        first_mat, second_mat, (((1,), (1,)), ((), ())), preferred_element_type=jnp.float32
    )


def bias_fill(sc_ref, prompt_bias, own_bias, flip):
    begin, cont_begin, block = sc_ref[0], sc_ref[1], sc_ref[2]
    q_dim, k_dim = (1, 0) if flip else (0, 1)
    shape = prompt_bias.shape
    rows = shape[q_dim]
    spot = lax.broadcasted_iota(jnp.int32, shape, q_dim) + block * rows
    key = lax.broadcasted_iota(jnp.int32, shape, k_dim)
    seen = (key <= spot) & ((key >= begin) | (key == spot))
    prompt_bias[...] = jnp.where(seen, 0.0, MASKED)
    shape = own_bias.shape
    spot = lax.broadcasted_iota(jnp.int32, shape, q_dim)
    key = lax.broadcasted_iota(jnp.int32, shape, k_dim)
    seen = (key <= spot) & ((key >= cont_begin) | (key == spot))
    own_bias[...] = jnp.where(seen, 0.0, MASKED)


def self_plan(prompt_rows, prompt_len, slot_len):
    step = slot_len // 2
    return (
        (0, prompt_rows, ((0, prompt_len, "prompt"),)),
        (prompt_rows, step, ((0, prompt_len, "start"), (1, step, "own"))),
        (prompt_rows + step, slot_len - step, ((0, prompt_len, "start"), (1, slot_len, "own"))),
    )


def cross_plan(row_total, key_total, step):
    return tuple(
        (at, min(step, row_total - at), ((0, key_total, None),)) for at in range(0, row_total, step)
    )


def head_lanes(head):
    lane = lax.broadcasted_iota(jnp.int32, (1, 2 * HDIM), 1)
    return (lane >= head * HDIM) & (lane < (head + 1) * HDIM)


def only(block, lanes):
    return jnp.where(lanes, block, jnp.zeros_like(block))


def fwd_kernel(plan, masked, slot_at, *refs):
    n_seg = 2 if masked else 1
    if masked:
        sc_ref, refs = refs[0], refs[1:]
    q_ref = refs[0]
    k_refs, v_refs = refs[1 : 1 + n_seg], refs[1 + n_seg : 1 + 2 * n_seg]
    o_ref, lse_ref = refs[1 + 2 * n_seg : 3 + 2 * n_seg]
    pair = pl.program_id(0)
    if masked:
        prompt_bias, own_bias = refs[3 + 2 * n_seg :]

        @pl.when(pair == 0)
        def _():
            bias_fill(sc_ref, prompt_bias, own_bias, False)

    out_lane = lax.broadcasted_iota(jnp.int32, (1, 128), 1)
    for q_at, q_n, parts in plan:
        rows = slice(q_at, q_at + q_n)
        q_blk = q_ref[rows, :]
        mixed_pair = None
        for head in (0, 1):
            lanes = head_lanes(head)
            q_one = only(q_blk, lanes)
            scores = []
            for seg, k_n, kind in parts:
                part = product_nt(q_one, k_refs[seg][:k_n, :])
                if kind == "prompt":
                    part = part + prompt_bias[...]
                elif kind == "own":
                    at = q_at - slot_at
                    part = part + own_bias[at : at + q_n, :k_n]
                elif kind == "start":
                    key = lax.broadcasted_iota(jnp.int32, (1, 128), 1)
                    first = jnp.where(key >= sc_ref[0], part[:, :128], MASKED)
                    part = jnp.concatenate([first, part[:, 128:]], 1)
                scores.append(part)
            row_max = functools.reduce(
                jnp.maximum, [jnp.max(part, 1, keepdims=True) for part in scores]
            )
            totals, mixed = 0.0, 0.0
            for part, (seg, k_n, _) in zip(scores, parts):
                shifted = jnp.exp(part - row_max)
                totals = totals + jnp.sum(shifted, 1, keepdims=True)
                mixed = mixed + product(shifted.astype(jnp.bfloat16), v_refs[seg][:k_n, :])
            mixed = mixed / totals
            mixed_pair = mixed if head == 0 else jnp.where(lanes, mixed, mixed_pair)
            lse = row_max + jnp.log(totals)
            lse_ref[rows, :] = jnp.where(out_lane == 2 * pair + head, lse, lse_ref[rows, :])
        o_ref[rows, :] = mixed_pair.astype(jnp.bfloat16)


def accumulate(total_ref, keys, done, part):
    known = min(max(done - keys.start, 0), keys.stop - keys.start)
    if known:
        total_ref[keys.start : keys.start + known, :] += part[:known]
    if known < keys.stop - keys.start:
        total_ref[keys.start + known : keys.stop, :] = part[known:]


def bwd_kernel(plan, masked, slot_at, key_step, *refs):
    n_seg = 2 if masked else 1
    if masked:
        sc_ref, refs = refs[0], refs[1:]
    q_ref, g_ref, o_ref, lse_ref = refs[:4]
    k_refs, v_refs = refs[4 : 4 + n_seg], refs[4 + n_seg : 4 + 2 * n_seg]
    outs = refs[4 + 2 * n_seg :]
    dq_ref, dk_refs, dv_refs = outs[0], outs[1 : 1 + n_seg], outs[1 + n_seg : 1 + 2 * n_seg]
    scratch = outs[1 + 2 * n_seg :]
    dk_acc, dv_acc = scratch[:n_seg], scratch[n_seg : 2 * n_seg]
    pair = pl.program_id(0)
    if masked:
        prompt_bias, own_bias = scratch[2 * n_seg :]

        @pl.when(pair == 0)
        def _():
            bias_fill(sc_ref, prompt_bias, own_bias, True)

    done = [0] * n_seg
    picks = jnp.concatenate(
        [only(jnp.ones((1, 2 * HDIM), jnp.float32), head_lanes(h)) for h in (0, 1)]
        + [jnp.zeros((6, 2 * HDIM), jnp.float32)],
        0,
    )
    for q_at, q_n, parts in plan:
        rows = slice(q_at, q_at + q_n)
        q_blk, g_blk = q_ref[rows, :], g_ref[rows, :]
        inner = lax.dot_general(
            picks,
            g_blk.astype(jnp.float32) * o_ref[rows, :].astype(jnp.float32),
            (((1,), (1,)), ((), ())),
            precision=lax.Precision.HIGHEST,
            preferred_element_type=jnp.float32,
        )
        dq = 0.0
        for head in (0, 1):
            lanes = head_lanes(head)
            q_one, g_one = only(q_blk, lanes), only(g_blk, lanes)
            lse = lse_ref[0, head : head + 1, rows]
            row_inner = inner[head : head + 1, :]
            for seg, k_n, kind in parts:
                for at in range(0, k_n, key_step):
                    keys = slice(at, min(at + key_step, k_n))
                    k_one = only(k_refs[seg][keys, :], lanes)
                    scores = product_nt(k_one, q_blk)
                    if kind == "prompt":
                        scores = scores + prompt_bias[keys, :]
                    elif kind == "own":
                        q_off = q_at - slot_at
                        scores = scores + own_bias[keys, q_off : q_off + q_n]
                    elif kind == "start" and at == 0:
                        key = lax.broadcasted_iota(jnp.int32, (128, 1), 0)
                        first = jnp.where(key >= sc_ref[0], scores[:128, :], MASKED)
                        scores = jnp.concatenate([first, scores[128:, :]], 0)
                    probs = jnp.exp(scores - lse)
                    grad_probs = product_nt(v_refs[seg][keys, :], g_one)
                    grad_scores = (probs * (grad_probs - row_inner)).astype(jnp.bfloat16)
                    add_v = product(probs.astype(jnp.bfloat16), g_one)
                    add_k = product(grad_scores, q_one)
                    accumulate(dv_acc[seg], keys, done[seg], add_v)
                    accumulate(dk_acc[seg], keys, done[seg], add_k)
                    dq = dq + product_tn(grad_scores, k_one)
                done[seg] = max(done[seg], k_n)
        dq_ref[rows, :] = dq.astype(jnp.bfloat16)
    for seg in range(n_seg):
        dk_refs[seg][...] = dk_acc[seg][...].astype(jnp.bfloat16)
        dv_refs[seg][...] = dv_acc[seg][...].astype(jnp.bfloat16)


VMEM_LIMIT = 48 * 1024 * 1024


def pair_spec(rows, shift=0):
    return pl.BlockSpec((rows, 2 * HDIM), lambda i: (0, i + shift))


def attend_forward(scalars, queries, kv_list, plan, slot_at):
    masked = scalars is not None
    row_total, width = queries.shape
    pairs = width // (2 * HDIM)
    scratch = []
    if masked:
        prompt_len, slot_len = kv_list[0].shape[0], kv_list[1].shape[0]
        scratch = [
            pltpu.VMEM((slot_at, prompt_len), jnp.float32),
            pltpu.VMEM((slot_len, slot_len), jnp.float32),
        ]
    area = sum(q_n * k_n for _, q_n, parts in plan for _, k_n, _ in parts)
    return pl.pallas_call(
        functools.partial(fwd_kernel, plan, masked, slot_at),
        grid=(pairs,),
        in_specs=([pl.BlockSpec(memory_space=pltpu.SMEM)] if masked else [])
        + [pair_spec(row_total)]
        + [pair_spec(kv.shape[0]) for kv in kv_list]
        + [pair_spec(kv.shape[0], pairs) for kv in kv_list],
        out_specs=[pair_spec(row_total), pl.BlockSpec((row_total, 128), lambda i: (0, 0))],
        out_shape=[
            jax.ShapeDtypeStruct((row_total, width), jnp.bfloat16),
            jax.ShapeDtypeStruct((row_total, 128), jnp.float32),
        ],
        scratch_shapes=scratch,
        compiler_params=pltpu.CompilerParams(
            dimension_semantics=("arbitrary",), vmem_limit_bytes=VMEM_LIMIT
        ),
        cost_estimate=pl.CostEstimate(
            flops=4 * area * HEADS * 128,
            bytes_accessed=4 * row_total * width + sum(2 * kv.size for kv in kv_list),
            transcendentals=area * HEADS,
        ),
        name="attend_forward",
    )(*([scalars] if masked else []), queries, *kv_list, *kv_list)


def attend_backward(scalars, queries, grads, mixed, log_totals, kv_list, plan, slot_at, key_step):
    masked = scalars is not None
    row_total, width = queries.shape
    pairs = width // (2 * HDIM)
    lse = log_totals[:, :HEADS].T.reshape(pairs, 2, row_total)
    scratch = [pltpu.VMEM((kv.shape[0], 2 * HDIM), jnp.float32) for kv in kv_list] * 2
    if masked:
        prompt_len, slot_len = kv_list[0].shape[0], kv_list[1].shape[0]
        scratch += [
            pltpu.VMEM((prompt_len, slot_at), jnp.float32),
            pltpu.VMEM((slot_len, slot_len), jnp.float32),
        ]
    area = sum(q_n * k_n for _, q_n, parts in plan for _, k_n, _ in parts)
    n_seg = len(kv_list)
    outs = pl.pallas_call(
        functools.partial(bwd_kernel, plan, masked, slot_at, key_step),
        grid=(pairs,),
        in_specs=([pl.BlockSpec(memory_space=pltpu.SMEM)] if masked else [])
        + [pair_spec(row_total)] * 3
        + [pl.BlockSpec((1, 2, row_total), lambda i: (i, 0, 0))]
        + [pair_spec(kv.shape[0]) for kv in kv_list]
        + [pair_spec(kv.shape[0], pairs) for kv in kv_list],
        out_specs=[pair_spec(row_total)] + [pair_spec(kv.shape[0]) for kv in kv_list] * 2,
        out_shape=[jax.ShapeDtypeStruct((row_total, width), jnp.bfloat16)]
        + [jax.ShapeDtypeStruct((kv.shape[0], width), jnp.bfloat16) for kv in kv_list] * 2,
        scratch_shapes=scratch,
        compiler_params=pltpu.CompilerParams(
            dimension_semantics=("arbitrary",), vmem_limit_bytes=VMEM_LIMIT
        ),
        cost_estimate=pl.CostEstimate(
            flops=10 * area * HEADS * 128,
            bytes_accessed=8 * row_total * width + sum(4 * kv.size for kv in kv_list),
            transcendentals=area * HEADS,
        ),
        name="attend_backward",
    )(*([scalars] if masked else []), queries, grads, mixed, lse, *kv_list, *kv_list)
    return outs[0], outs[1 : 1 + n_seg], outs[1 + n_seg :]


def column_sum(matrix):
    return jnp.sum(matrix.astype(jnp.float32), 0)


def layer_norm(residual, gain_vec, shift_vec):
    row_mean = jnp.mean(residual, -1, keepdims=True)
    centred = residual - row_mean
    row_var = jnp.mean(centred * centred, -1, keepdims=True)
    return centred * lax.rsqrt(row_var + 1e-05) * gain_vec + shift_vec


def layer_norm_back(residual, gain_vec, grad):
    row_mean = jnp.mean(residual, -1, keepdims=True)
    centred = residual - row_mean
    row_var = jnp.mean(centred * centred, -1, keepdims=True)
    inverse = lax.rsqrt(row_var + 1e-05)
    xhat = centred * inverse
    dx = grad * gain_vec
    inner = dx - jnp.mean(dx, -1, keepdims=True) - xhat * jnp.mean(dx * xhat, -1, keepdims=True)
    return inner * inverse, jnp.sum(grad * xhat, 0), jnp.sum(grad, 0)


SWAP = ((0, 1), (1, 0))


def swap(value, axis):
    return lax.ppermute(value, axis, SWAP)


def xor_perm(count, shift):
    return tuple((i, i ^ shift) for i in range(count))


def reduce_stages(part, names, order):
    names = list(names)
    for axis in order:
        dim = names.index(axis)
        count = part.shape[dim]
        here = lax.axis_index(axis)
        total = lax.dynamic_index_in_dim(part, here, dim, keepdims=False).astype(jnp.float32)
        for shift in range(1, count):
            other = lax.dynamic_index_in_dim(part, here ^ shift, dim, keepdims=False)
            came = lax.ppermute(other, axis, xor_perm(count, shift))
            total = total + came.astype(jnp.float32)
        names.pop(dim)
        part = total if not names else total.astype(jnp.bfloat16)
    return part


class Links:
    def __init__(self, mesh):
        self.fast = dict(mesh.shape) == {"fsdp": 4, "ctx": 8}
        if self.fast:
            self.mesh = Mesh(mesh.devices.reshape(2, 2, 4, 2), ("x", "c", "z", "y"))
            self.rows, self.ctx = ("x", "c"), ("z", "y")
        else:
            self.mesh, self.rows, self.ctx = mesh, ("fsdp",), ("ctx",)
        self.every = self.rows + self.ctx

    def gather(self, value, axes):
        return lax.all_gather(value, axes, axis=0, tiled=True)

    def scatter(self, part, order):
        part = part.astype(jnp.bfloat16)
        if not self.fast:
            return lax.psum_scatter(part, self.every, scatter_dimension=0, tiled=True).astype(
                jnp.float32
            )
        part = part.reshape(2, 2, 4, 2, part.shape[0] // 32, part.shape[1])
        return reduce_stages(part, "xczy", order)

    def scatter_ctx(self, part, order):
        part = part.astype(jnp.bfloat16)
        if not self.fast:
            return lax.psum_scatter(part, self.ctx, scatter_dimension=0, tiled=True).astype(
                jnp.float32
            )
        part = part.reshape(4, 2, part.shape[0] // 8, part.shape[1])
        return reduce_stages(part, "zy", order)

    def total(self, value, axes):
        if not self.fast:
            return lax.psum(value, axes)
        for axis in axes:
            count = 4 if axis == "z" else 2
            value = value + sum(
                lax.ppermute(value, axis, xor_perm(count, shift)) for shift in range(1, count)
            )
        return value


def body(
    links,
    prompt_in,
    cont_in,
    encoder,
    prompt_start,
    cont_start,
    self_proj,
    self_out,
    cross_query,
    cross_kv,
    cross_out,
    up_proj,
    down_proj,
    vec_bias,
    up_bias,
    ln_gain,
    ln_bias,
    prompt_cot,
    cont_cot,
):
    f32, bf16 = jnp.float32, jnp.bfloat16
    shard, width = self_out.shape
    prompt_rows, slot_len = prompt_in.shape[1], cont_in.shape[2]
    block_index = lax.axis_index(links.ctx)
    ctx_count = lax.axis_size(links.ctx)
    prompt_len = prompt_rows * ctx_count
    enc_rows = encoder.shape[1]
    hidden = up_bias.shape[0] // shard
    scale = HDIM ** (-0.5)

    small = jnp.concatenate(
        [vec_bias.T, ln_gain.T, ln_bias.T, up_bias.reshape(hidden, shard).T], 1
    )
    small = jnp.pad(small, ((0, 0), (0, 128 - small.shape[1])))
    inputs_all = links.gather(jnp.concatenate([prompt_in[0], encoder[0]], 0), links.ctx)
    inputs_all = inputs_all.reshape(ctx_count, prompt_rows + enc_rows, width)
    prompt_all = inputs_all[:, :prompt_rows].reshape(prompt_len, width)
    enc_all = inputs_all[:, prompt_rows:].reshape(enc_rows * ctx_count, width)
    first = links.gather(jnp.concatenate([self_proj, small], 1), links.every)
    second = links.gather(
        jnp.concatenate([self_out, cross_query, cross_kv, cross_out], 1), links.every
    )
    w_up = links.gather(up_proj, links.every)
    w_down = links.gather(down_proj, links.every)
    w_q, w_kv = first[:, :width], first[:, width : 3 * width]
    w_so, w_cq = second[:, :width], second[:, width : 2 * width]
    w_ckv, w_co = second[:, 2 * width : 4 * width], second[:, 4 * width :]
    small = first[:, 3 * width :].astype(f32).T
    biases, gains, shifts = small[:7], small[7:10], small[10:13]
    hidden_bias = (
        small[13 : 13 + hidden]
        .reshape(hidden, width // shard, shard)
        .transpose(1, 0, 2)
        .reshape(hidden * width)
    )

    every_begin = cont_start[0]
    own_begin = lax.dynamic_index_in_dim(every_begin, block_index, 0, keepdims=False)
    scalars = jnp.stack([prompt_start[0], own_begin, block_index.astype(jnp.int32)])
    cont_rows = cont_in[0, 0]
    tokens = jnp.concatenate([prompt_in[0], cont_rows], 0)
    row_total = tokens.shape[0]
    row_spot = jnp.arange(row_total, dtype=jnp.int32)
    valid_rows = jnp.where(
        row_spot < prompt_rows,
        block_index * prompt_rows + row_spot >= prompt_start[0],
        row_spot - prompt_rows >= own_begin,
    ).astype(f32)[:, None]
    valid_count = (prompt_len - prompt_start[0] + jnp.sum(slot_len - every_begin)).astype(f32)

    kv_bias = jnp.concatenate([jnp.zeros((width,), f32), biases[1]])
    queries = ((product(tokens, w_q) + biases[0]) * scale).astype(bf16)
    prompt_kv = (product(prompt_all, w_kv) + kv_bias).astype(bf16)
    cont_kv = (product(cont_rows, w_kv) + kv_bias).astype(bf16)
    plan = self_plan(prompt_rows, prompt_len, slot_len)
    attn, self_log = attend_forward(scalars, queries, [prompt_kv, cont_kv], plan, prompt_rows)
    branch_self = product(attn, w_so) + biases[2]
    resid_one = tokens.astype(f32) + branch_self
    hidden_one = layer_norm(resid_one, gains[0], shifts[0]).astype(bf16)

    enc_bias = jnp.concatenate([jnp.zeros((width,), f32), biases[4]])
    enc_kv = (product(enc_all, w_ckv) + enc_bias).astype(bf16)
    cross_queries = ((product(hidden_one, w_cq) + biases[3]) * scale).astype(bf16)
    enc_len = enc_all.shape[0]
    cross_attn, cross_log = attend_forward(
        None, cross_queries, [enc_kv], cross_plan(row_total, enc_len, 320), 0
    )
    branch_cross = product(cross_attn, w_co) + biases[5]
    resid_two = hidden_one.astype(f32) + branch_cross
    hidden_two = layer_norm(resid_two, gains[1], shifts[1]).astype(bf16)

    pre_act = product(hidden_two, w_up) + hidden_bias
    half = 0.5 * (1.0 + lax.erf(pre_act * (0.5**0.5)))
    act = (pre_act * half).astype(bf16)
    slope = (half + pre_act * jnp.exp(-0.5 * pre_act * pre_act) * 0.3989422804014327).astype(bf16)
    branch_ffn = product(act, w_down) + biases[6]
    resid_three = hidden_two.astype(f32) + branch_ffn
    output = layer_norm(resid_three, gains[2], shifts[2]).astype(bf16)

    members = (tokens, branch_self, hidden_one, branch_cross, hidden_two, branch_ffn)
    squares = jnp.stack(
        [jnp.sum(valid_rows * jnp.square(member.astype(f32))) for member in members]
    )
    squares = links.total(jnp.pad(squares[None], ((0, 7), (0, 122))), links.ctx)[0, :6]
    statistics = (squares / (valid_count * width))[None]

    grad_out = jnp.concatenate([prompt_cot[0], cont_cot[0, 0]], 0).astype(f32)
    grad_three, gain_three, shift_three = layer_norm_back(resid_three, gains[2], grad_out)
    grad_ffn = grad_three.astype(bf16)
    down_total = links.scatter(product_tn(act, grad_ffn), "cxyz")
    grad_pre = (product_nt(grad_ffn, w_down) * slope.astype(f32)).astype(bf16)
    up_total = links.scatter(product_tn(hidden_two, grad_pre), "cyxz")
    grad_hidden_two = grad_three + product_nt(grad_pre, w_up)
    grad_two, gain_two, shift_two = layer_norm_back(resid_two, gains[1], grad_hidden_two)
    grad_cross = grad_two.astype(bf16)
    co_total = links.scatter(product_tn(cross_attn, grad_cross), "czxy")
    grad_cattn = product_nt(grad_cross, w_co).astype(bf16)
    cross_gq, cross_gk, cross_gv = attend_backward(
        None,
        cross_queries,
        grad_cattn,
        cross_attn,
        cross_log,
        [enc_kv],
        cross_plan(row_total, enc_len, 384),
        0,
        512,
    )
    grad_cq = (cross_gq.astype(f32) * scale).astype(bf16)
    enc_gkv = jnp.concatenate([cross_gk[0], cross_gv[0]], 1)
    cq_total = links.scatter(product_tn(hidden_one, grad_cq), "cxyz")
    ckv_total = links.scatter(product_tn(enc_all, enc_gkv), "cyxz")
    encoder_grad = links.scatter_ctx(product_nt(enc_gkv, w_ckv), "zy")[None]
    grad_hidden_one = grad_two + product_nt(grad_cq, w_cq)
    grad_one, gain_one, shift_one = layer_norm_back(resid_one, gains[0], grad_hidden_one)
    grad_self = grad_one.astype(bf16)
    so_total = links.scatter(product_tn(attn, grad_self), "cxyz")
    grad_attn = product_nt(grad_self, w_so).astype(bf16)
    self_gq, self_gk, self_gv = attend_backward(
        scalars,
        queries,
        grad_attn,
        attn,
        self_log,
        [prompt_kv, cont_kv],
        plan,
        prompt_rows,
        1024,
    )
    grad_q = (self_gq.astype(f32) * scale).astype(bf16)
    prompt_gkv = jnp.concatenate([self_gk[0], self_gv[0]], 1)
    cont_gkv = jnp.concatenate([self_gk[1], self_gv[1]], 1)
    prompt_back = product_nt(prompt_gkv, w_kv)
    half_width = width // 2
    prompt_back = jnp.concatenate(
        [
            links.scatter_ctx(prompt_back[:, :half_width], "yz"),
            links.scatter_ctx(prompt_back[:, half_width:], "zy"),
        ],
        1,
    )
    sin_q = product_tn(tokens, grad_q)
    sin_kv = product_tn(prompt_all, prompt_gkv) + product_tn(cont_rows, cont_gkv)
    sin_total = jnp.concatenate(
        [
            links.scatter(sin_q, "cxyz"),
            links.scatter(sin_kv[:, :width], "cyxz"),
            links.scatter(sin_kv[:, width:], "czxy"),
        ],
        1,
    )
    input_grad = grad_one + product_nt(grad_q, w_q)
    prompt_grad = (input_grad[:prompt_rows] + prompt_back)[None]
    cont_grad = (input_grad[prompt_rows:] + product_nt(cont_gkv, w_kv))[None, None]

    up_bias_part = column_sum(grad_pre).reshape(width // shard, hidden, shard)
    small_part = jnp.concatenate(
        [
            jnp.stack(
                [
                    column_sum(grad_q),
                    column_sum(self_gv[0]) + column_sum(self_gv[1]),
                    column_sum(grad_self),
                    column_sum(grad_cq),
                    column_sum(cross_gv[0]),
                    column_sum(grad_cross),
                    column_sum(grad_ffn),
                    gain_one,
                    gain_two,
                    gain_three,
                    shift_one,
                    shift_two,
                    shift_three,
                ]
            ),
            up_bias_part.transpose(1, 0, 2).reshape(hidden, width),
        ],
        0,
    )
    small_total = links.total(small_part, links.every)
    at = lax.axis_index(links.every) * shard
    small_total = lax.dynamic_slice_in_dim(small_total, at, shard, 1)
    bias_total, gain_total, shift_total = small_total[:7], small_total[7:10], small_total[10:13]
    up_bias_total = small_total[13 : 13 + hidden].reshape(hidden * shard)
    return (
        output[:prompt_rows][None],
        output[prompt_rows:][None, None],
        prompt_grad,
        cont_grad,
        encoder_grad,
        sin_total,
        so_total,
        cq_total,
        ckv_total,
        co_total,
        up_total,
        down_total,
        bias_total,
        up_bias_total,
        gain_total,
        shift_total,
        statistics,
    )


def solution(mesh):
    links = Links(mesh)
    fs, ctx, every = links.rows, links.ctx, links.every
    group = P(fs, ctx, None)
    slots = P(fs, ctx, None, None)
    weight = P(every, None)
    vectors = P(None, every)
    return jax.shard_map(
        functools.partial(body, links),
        mesh=links.mesh,
        in_specs=(group, slots, group, P(fs), P(fs, None))
        + (weight,) * 7
        + (vectors, P(every), vectors, vectors, group, slots),
        out_specs=(group, slots, group, slots, group)
        + (weight,) * 7
        + (vectors, P(every), vectors, vectors, P(fs, None)),
        check_vma=False,
    )
```

time: 3230 us -> 1040 us (0.32)
  waiting for transfers between devices: 1990 us -> 520 us
  matrix products: 616 us -> 151 us
  blocking collectives: 322 us -> 0 us
  local copies, waits for them, and re-layouts: 210 us -> 80.8 us
  Pallas kernels: 0 us -> 109 us
  starting transfers between devices: 1.48 us -> 99.5 us
    reduce_scatter x6 -> x0, waiting for transfers between devices: 1310 us -> none  [the longest x1 360 us: body(): lax.psum_scatter(down_total, ('fsdp', 'ctx'), scatter_dimension=0, tiled=...]
    unnamed x33 -> x5, waiting for transfers between devices: 616 us -> 1.1 us
    all_gather x4 -> x0, blocking collectives: 266 us -> none  [the longest x1 70.8 us: body(): lax.all_gather(vec_bias, ('fsdp', 'ctx'), axis=1, tiled=True)]
    ppermute x0 -> x76, waiting for transfers between devices: none -> 234 us  [the longest x66 232 us: reduce_stages(): came = lax.ppermute(other, axis, xor_perm(count, shift))]
    all_gather x11 -> x5, waiting for transfers between devices: 62.1 us -> 284 us  [gather(): return lax.all_gather(value, axes, axis=0, tiled=True)]
    dot_general x71 -> x9, matrix products: 222 us -> 51.2 us  [product(): return jnp.dot(first_mat, second_mat, preferred_element_type=jnp.float32)]
    dot_general x103 -> x9, matrix products: 211 us -> 52.7 us  [product_nt(): lax.dot_general(first_mat, second_mat, (((1,), (1,)), ((), ())), preferre...]
    dot_general x71 -> x9, matrix products: 183 us -> 47.3 us  [product_tn(): lax.dot_general(first_mat, second_mat, (((0,), (0,)), ((), ())), preferre...]
  transfers between devices with their start and end apart: 25 -> 81, of which waited for: 14 -> 39; matrix products, arithmetic and copies ran while one was open for 19% -> 24% of each run, Pallas kernels for 0% -> 11%
where the time goes in v1:
time: 1040 us; the launch traced here: 1030 us
  waiting for transfers between devices  520 us (50%)
  matrix products  151 us (15%)
  Pallas kernels  109 us (10%)
  starting transfers between devices  99.5 us (10%)
  local copies, waits for them, and re-layouts  80.8 us (8%)
  other arithmetic  52.4 us (5%)
  between operations  17.3 us (2%)
    all_gather x5, waiting for transfers between devices, gather(): return lax.all_gather(value, axes, axis=0, tiled=True)  284 us
    ppermute x66, waiting for transfers between devices, reduce_stages(): came = lax.ppermute(other, axis, xor_perm(count, shift))  232 us
    ppermute x66, starting transfers between devices, reduce_stages(): came = lax.ppermute(other, axis, xor_perm(count, shift))  77.2 us
    pallas_call x2, Pallas kernels, attend_backward(): pl.pallas_call(functools.partial(bwd_kernel, plan, masked, slot_at, key_s...  68.4 us
    dot_general x9, matrix products, product_nt(): lax.dot_general(first_mat, second_mat, (((1,), (1,)), ((), ())), preferre...  52.7 us
    dot_general x9, matrix products, product(): return jnp.dot(first_mat, second_mat, preferred_element_type=jnp.float32)  51.2 us
    dot_general x9, matrix products, product_tn(): lax.dot_general(first_mat, second_mat, (((0,), (0,)), ((), ())), preferre...  47.3 us
    pallas_call x2, Pallas kernels, attend_forward(): pl.pallas_call(functools.partial(fwd_kernel, plan, masked, slot_at), grid...  40.3 us
  transfers between devices with their start and end apart: 81, of which 39 were waited for; matrix products, arithmetic and copies ran while one was open for 24% of the time, Pallas kernels for 11%

profile of v1, /device:TPU:0, one launch (start us, length us, event | category | flops | bytes accessed | tf_op | source)
XLA Modules:
  0.0 1029.5 jit_solution(3037901226038200206)
XLA Ops:
  19.2 54.7 %all-gather.8.cloned.1.call-done = bf16[1536,1024]{1,0:T(8,128)(2,1)} async-done(((bf16[192,1024]{1,0:T(8,128)(2,1)}), bf16[1536,1024]{1,0:T(8,128)(2,1)}) %all-gather.8.cloned.1.call-update) | async-done | bytes 3145744 | tf_op jit(solution)/shard_map/all_gather | solution.py:343
  78.1 68.7 %all-gather.6.cloned.1.call-done = bf16[1024,3200]{1,0:T(8,128)(2,1)} async-done(((bf16[32,3200]{1,0:T(8,128)(2,1)}), bf16[1024,3200]{1,0:T(8,128)(2,1)}) %all-gather.6.cloned.1.call-update) | async-done | bytes 6553616 | tf_op jit(solution)/shard_map/all_gather | solution.py:343
  157.1 6.3 add_convert_fusion.refs_2_.refs_4_.refs_5_.refs_7_
  163.4 29.3 %attend_forward.2 = (bf16[640,1024]{1,0:T(8,128)(2,1)S(1)}, f32[640,128]{1,0:T(8,128)S(1)}) custom-call(s32[3]{0:T(128)S(1)} %pad_add_fusion.refs_0_, bf16[640,1024]{1,0:T(8,128)(2,1)S(1)} %multiply_convert_fusion.5.refs_1_, bf16[1024,2048]{1,0:T(8,128)(2,1)} %add_convert_fusion.refs_2_.refs_4_.refs_5_.refs_7_, ...), custom_call_target="tpu_custom_call" | custom-call | flops 6979321856 | bytes 8912896 | tf_op jit(solution)/shard_map/attend_forward/pallas_call | solution.py:219
  193.0 42.7 %all-gather.10.cloned.1.call-done = bf16[1024,5120]{1,0:T(8,128)(2,1)} async-done(((bf16[32,5120]{1,0:T(8,128)(2,1)}), bf16[1024,5120]{1,0:T(8,128)(2,1)}) %all-gather.10.cloned.1.call-update) | async-done | bytes 10485776 | tf_op jit(solution)/shard_map/all_gather | solution.py:343
  235.6 4.9 fusion.149
  246.1 11.0 %attend_forward.3 = (bf16[640,1024]{1,0:T(8,128)(2,1)S(1)}, f32[640,128]{1,0:T(8,128)S(1)}) custom-call(bf16[640,1024]{1,0:T(8,128)(2,1)S(1)} %multiply_convert_fusion.4.refs_0_, bf16[512,2048]{1,0:T(8,128)(2,1)S(1)} %add_convert_fusion.1.refs_1_.refs_2_.refs_4_.refs_5_, bf16[512,2048]{1,0:T(8,128)(2,1)S(1)} %add_convert_fusion.1.refs_1_.refs_2_.refs_4_.refs_5_), custom_call_target="tpu_custom_call" | custom-call | flops 2684354560 | bytes 4718592 | tf_op jit(solution)/shard_map/attend_forward/pallas_call | solution.py:219
  257.1 5.2 fusion.148
  262.7 51.6 %all-gather.12.cloned.1.call-done = bf16[1024,4096]{1,0:T(8,128)(2,1)} async-done(((bf16[32,4096]{1,0:T(8,128)(2,1)}), bf16[1024,4096]{1,0:T(8,128)(2,1)}) %all-gather.12.cloned.1.call-update) | async-done | bytes 8388624 | tf_op jit(solution)/shard_map/all_gather | solution.py:343
  314.3 12.4 %multiply_convert_fusion.1 = (bf16[640,4096]{1,0:T(8,128)(2,1)}, f32[640,4096]{1,0:T(8,128)}) fusion(f32[4096]{0:T(1024)S(1)} %add.647, bf16[1024,4096]{1,0:T(8,128)(2,1)} %all-gather.12.cloned.1.call-done, f32[640,1024]{1,0:T(8,128)S(1)} %get-tuple-element.81, f32[1024]{0:T(1024)S(1)} %get-tuple-element.56, f32[1024]{0:T(1024)S(1)} %get-tuple-element.57, ...), kind=kOutput, calls=%fused_computation.8 | convolution fusion | flops 5387714560 | bytes 26768384 | tf_op jit(solution)/shard_map/dot_general | solution.py:17
  326.7 66.4 %all-gather.14.cloned.1.call-done = bf16[4096,1024]{1,0:T(8,128)(2,1)} async-done(((bf16[128,1024]{1,0:T(8,128)(2,1)}), bf16[4096,1024]{1,0:T(8,128)(2,1)}) %all-gather.14.cloned.1.call-update) | async-done | bytes 8388624 | tf_op jit(solution)/shard_map/all_gather | solution.py:343
  393.2 13.5 %multiply_reduce_fusion = (f32[]{:T(128)}, f32[]{:T(128)}, f32[]{:T(128)}, f32[]{:T(128)}, f32[]{:T(128)}, /*index=5*/f32[]{:T(128)}, f32[640]{0:T(1024)S(1)}, f32[640,1024]{1,0:T(8,128)S(1)}) fusion(f32[640]{0:T(1024)S(1)} %fusion.133, f32[1024]{0:T(1024)S(1)} %get-tuple-element.55, f32[640,1024]{1,0:T(8,128)} %get-tuple-element.147, ...), kind=kOutput, calls=%fused_computation.66 | convolution fusion | flops 5390990848 | bytes 26769432 | tf_op jit(solution)/shard_map/dot_general | solution.py:17
  406.6 4.0 stack.85
  423.2 13.5 %convert_reduce_fusion = (f32[4096]{0:T(1024)S(1)}, bf16[640,4096]{1,0:T(8,128)(2,1)S(1)}) fusion(f32[640,4096]{1,0:T(8,128)} %get-tuple-element.150, f32[4096]{0:T(1024)S(1)} %add.647, bf16[4096,1024]{1,0:T(8,128)(2,1)} %all-gather.14.cloned.1.call-done, f32[640,1024]{1,0:T(8,128)S(1)} %copy-done.39), kind=kOutput, calls=%fused_computation.6 | convolution fusion | flops 5408681984 | bytes 26771456 | tf_op jit(solution)/shard_map/dot_general | solution.py:27
  439.0 9.3 convolution_convert_fusion
  448.3 11.0 %multiply_reduce_fusion.3 = (f32[1024]{0:T(1024)}, f32[640]{0:T(1024)S(1)}, f32[640]{0:T(1024)S(1)}, f32[1024]{0:T(1024)}, f32[640,1024]{1,0:T(8,128)S(1)}) fusion(f32[640,1024]{1,0:T(8,128)S(1)} %copy-done.20, f32[640]{0:T(1024)S(1)} %add_rsqrt_fusion.1, f32[640]{0:T(1024)S(1)} %broadcast_multiply_fusion.7, f32[1024]{0:T(1024)S(1)} %get-tuple-element.57, ...), kind=kOutput, calls=%fused_computation.69 | convolution fusion | flops 5375259648 | bytes 21518336 | tf_op jit(solution)/shard_map/dot_general | solution.py:27
  464.0 21.3 %attend_backward.2 = (bf16[640,1024]{1,0:T(8,128)(2,1)S(1)}, bf16[512,1024]{1,0:T(8,128)(2,1)S(1)}, bf16[512,1024]{1,0:T(8,128)(2,1)S(1)}) custom-call(bf16[640,1024]{1,0:T(8,128)(2,1)S(1)} %copy-done.10, bf16[640,1024]{1,0:T(8,128)(2,1)S(1)} %fusion.75.refs_1_, bf16[640,1024]{1,0:T(8,128)(2,1)} %copy-done.4, f32[8,2,640]{2,1,0:T(2,128)S(1)} %reshape.280.refs_3_, ...), custom_call_target="tpu_custom_call" | custom-call | flops 6710886400 | bytes 9437184 | tf_op jit(solution)/shard_map/attend_backward/pallas_call | solution.py:258
  492.8 4.3 multiply_reduce_fusion.4
  505.1 47.1 %attend_backward.3 = (bf16[640,1024]{1,0:T(8,128)(2,1)S(1)}, bf16[1024,1024]{1,0:T(8,128)(2,1)}, bf16[512,1024]{1,0:T(8,128)(2,1)S(1)}, bf16[1024,1024]{1,0:T(8,128)(2,1)}, bf16[512,1024]{1,0:T(8,128)(2,1)S(1)}) custom-call(s32[3]{0:T(128)S(1)} %pad_add_fusion.refs_0_, bf16[640,1024]{1,0:T(8,128)(2,1)S(1)} %copy-done.13, ...), custom_call_target="tpu_custom_call" | custom-call | flops 17448304640 | bytes 17825792 | tf_op jit(solution)/shard_map/attend_backward/pallas_call | solution.py:258
  556.4 9.4 convolution_convert_fusion.1
  568.2 7.9 constant_dynamic-slice_fusion.5
  598.1 6.8 fusion.153
  604.9 4.9 fusion.47
  612.6 6.5 fusion.7
  622.1 6.9 constant_dynamic-slice_fusion.3
  629.0 5.3 fusion.80
  637.8 3.7 fusion.37
  666.0 11.5 %collective-permute-start.68 = (f32[17,1024]{1,0:T(8,128)S(1)}, f32[17,1024]{1,0:T(8,128)S(1)}, u32[]{:S(2)}, u32[]{:S(2)}) collective-permute-start(f32[17,1024]{1,0:T(8,128)S(1)} %add.746), channel_id=1, source_target_pairs={{0,2},{2,0},{4,6},{6,4},{1,3},{3,1},{5,7},{7,5},{8,10},{10,8},{12,... | collective-permute-start | bytes 208904 | tf_op jit(solution)/shard_map/ppermute | solution.py:369
  684.3 4.9 collective-permute-done.4
  690.0 6.9 collective-permute-done.6
  697.7 9.6 collective-permute-done.5
  723.8 4.9 collective-permute-done.2
  745.6 5.6 collective-permute-done.51
  753.1 16.9 %collective-permute-done.50 = bf16[2,2,32,1024]{3,2,1,0:T(8,128)(2,1)S(1)} collective-permute-done((bf16[2,2,32,1024]{3,2,1,0:T(8,128)(2,1)S(1)}, bf16[2,2,32,1024]{3,2,1,0:T(8,128)(2,1)S(1)}, u32[]{:S(2)}, u32[]{:S(2)}) %collective-permute-start.50) | collective-permute-done | bytes 262176 | tf_op jit(solution)/shard_map/ppermute | solution.py:325
  772.4 13.6 %collective-permute-done.26 = bf16[2,2,32,1024]{3,2,1,0:T(8,128)(2,1)S(1)} collective-permute-done((bf16[2,2,32,1024]{3,2,1,0:T(8,128)(2,1)S(1)}, bf16[2,2,32,1024]{3,2,1,0:T(8,128)(2,1)S(1)}, u32[]{:S(2)}, u32[]{:S(2)}) %collective-permute-start.26) | collective-permute-done | bytes 262176 | tf_op jit(solution)/shard_map/ppermute | solution.py:325
  787.0 9.5 collective-permute-done.52
  797.3 4.1 collective-permute-done.28
  814.2 5.7 collective-permute-done.37
  821.0 5.5 collective-permute-done.19
  871.6 7.0 collective-permute-done.44
  884.2 24.4 %collective-permute-done.55 = bf16[2,4,32,4096]{3,2,1,0:T(8,128)(2,1)} collective-permute-done((bf16[2,4,32,4096]{3,2,1,0:T(8,128)(2,1)}, bf16[2,4,32,4096]{3,2,1,0:T(8,128)(2,1)}, u32[]{:S(2)}, u32[]{:S(2)}) %collective-permute-start.55) | collective-permute-done | bytes 2097184 | tf_op jit(solution)/shard_map/ppermute | solution.py:325
  918.8 4.0 collective-permute-done.46
  923.6 33.6 %collective-permute-done.61 = bf16[4,2,128,1024]{3,2,0,1:T(8,128)(2,1)S(1)} collective-permute-done((bf16[4,2,128,1024]{3,2,0,1:T(8,128)(2,1)S(1)}, bf16[4,2,128,1024]{3,2,0,1:T(8,128)(2,1)S(1)}, u32[]{:S(2)}, u32[]{:S(2)}) %collective-permute-start.61) | collective-permute-done | bytes 2097184 | tf_op jit(solution)/shard_map/ppermute | solution.py:325
  958.9 13.7 %collective-permute-done.56 = bf16[4,32,4096]{2,1,0:T(8,128)(2,1)S(1)} collective-permute-done((bf16[4,32,4096]{2,1,0:T(8,128)(2,1)S(1)}, bf16[4,32,4096]{2,1,0:T(8,128)(2,1)S(1)}, u32[]{:S(2)}, u32[]{:S(2)}) %collective-permute-start.56) | collective-permute-done | bytes 1048608 | tf_op jit(solution)/shard_map/ppermute | solution.py:325
  973.0 5.5 collective-permute-start.57
  984.7 7.3 collective-permute-done.57
  992.8 20.0 %collective-permute-done.58 = bf16[32,4096]{1,0:T(8,128)(2,1)S(1)} collective-permute-done((bf16[32,4096]{1,0:T(8,128)(2,1)S(1)}, bf16[32,4096]{1,0:T(8,128)(2,1)S(1)}, u32[]{:S(2)}, u32[]{:S(2)}) %collective-permute-start.58) | collective-permute-done | bytes 262176 | tf_op jit(solution)/shard_map/ppermute | solution.py:325
  1013.8 7.8 collective-permute-done.64
  (509 shorter events, 261.3 us)
Async XLA Ops:
  7.2 66.8 %all-gather.8.cloned.1.call-start = ((), (), s32[]{:S(2)}) async-start(), calls=%async_computation.1 | async-start | bytes 3538944 | tf_op jit(solution)/shard_map/all_gather | solution.py:343
  9.1 137.8 %all-gather.6.cloned.1.call-start = ((), (), s32[]{:S(2)}) async-start(), calls=%async_computation | async-start | bytes 6758400 | tf_op jit(solution)/shard_map/all_gather | solution.py:343
  12.3 223.3 %all-gather.10.cloned.1.call-start = ((), (), s32[]{:S(2)}) async-start(), calls=%async_computation.2 | async-start | bytes 10813440 | tf_op jit(solution)/shard_map/all_gather | solution.py:343
  14.1 300.2 %all-gather.12.cloned.1.call-start = ((), (), s32[]{:S(2)}) async-start(), calls=%async_computation.3 | async-start | bytes 8650752 | tf_op jit(solution)/shard_map/all_gather | solution.py:343
  14.7 378.5 %all-gather.14.cloned.1.call-start = ((), (), s32[]{:S(2)}) async-start(), calls=%async_computation.4 | async-start | bytes 8650752 | tf_op jit(solution)/shard_map/all_gather | solution.py:343
  411.2 236.4 %collective-permute-start.74 = (f32[8,128]{1,0:T(8,128)}, f32[8,128]{1,0:T(8,128)}, u32[]{:S(2)}, u32[]{:S(2)}) collective-permute-start(f32[8,128]{1,0:T(8,128)} %pad.11), channel_id=1, source_target_pairs={{0,6},{2,4},{4,2},{6,0},{1,7},{3,5},{5,3},{7,1},{8,14},{10,12},{12... | collective-permute-start | bytes 12296 | tf_op jit(solution)/shard_map/ppermute | solution.py:369
  413.1 235.5 %collective-permute-start.73 = (f32[8,128]{1,0:T(8,128)}, f32[8,128]{1,0:T(8,128)}, u32[]{:S(2)}, u32[]{:S(2)}) collective-permute-start(f32[8,128]{1,0:T(8,128)} %pad.11), channel_id=1, source_target_pairs={{0,4},{2,6},{4,0},{6,2},{1,5},{3,7},{5,1},{7,3},{8,12},{10,14},{12... | collective-permute-start | bytes 12296 | tf_op jit(solution)/shard_map/ppermute | solution.py:369
  414.2 234.5 %collective-permute-start.72 = (f32[8,128]{1,0:T(8,128)}, f32[8,128]{1,0:T(8,128)}, u32[]{:S(2)}, u32[]{:S(2)}) collective-permute-start(f32[8,128]{1,0:T(8,128)} %pad.11), channel_id=1, source_target_pairs={{0,2},{2,0},{4,6},{6,4},{1,3},{3,1},{5,7},{7,5},{8,10},{10,8},{12,... | collective-permute-start | bytes 12296 | tf_op jit(solution)/shard_map/ppermute | solution.py:369
  583.3 61.5 %collective-permute-start.66 = (f32[17,1024]{1,0:T(8,128)S(1)}, f32[17,1024]{1,0:T(8,128)}, u32[]{:S(2)}, u32[]{:S(2)}) collective-permute-start(f32[17,1024]{1,0:T(8,128)S(1)} %concatenate.55), channel_id=1, source_target_pairs={{0,16},{16,0},{1,17},{17,1},{2,18},{18,2},{3,19},{19,3},{4,20},{20... | collective-permute-start | bytes 208904 | tf_op jit(solution)/shard_map/ppermute | solution.py:369
  644.2 35.9 %collective-permute-start.8 = (bf16[2,64,1024]{2,1,0:T(8,128)(2,1)S(1)}, bf16[2,64,1024]{2,1,0:T(8,128)(2,1)S(1)}, u32[]{:S(2)}, u32[]{:S(2)}) collective-permute-start(bf16[2,64,1024]{2,1,0:T(8,128)(2,1)S(1)} %get-tuple-element.121), channel_id=1, source_target_pairs={{0,2},{2,0},{4,6},{6,4},{1,3},{3,1},{5,7},{7,5},{8,10},{10,8},{12,... | collective-permute-start | bytes 786440 | tf_op jit(solution)/shard_map/ppermute | solution.py:325
  644.8 37.4 %collective-permute-start.10 = (bf16[2,64,1024]{2,1,0:T(8,128)(2,1)S(1)}, bf16[2,64,1024]{2,1,0:T(8,128)(2,1)S(1)}, u32[]{:S(2)}, u32[]{:S(2)}) collective-permute-start(bf16[2,64,1024]{2,1,0:T(8,128)(2,1)S(1)} %get-tuple-element.122), channel_id=1, source_target_pairs={{0,6},{2,4},{4,2},{6,0},{1,7},{3,5},{5,3},{7,1},{8,14},{10,12},{12... | collective-permute-start | bytes 786440 | tf_op jit(solution)/shard_map/ppermute | solution.py:325
  647.6 36.6 %collective-permute-start.9 = (bf16[2,64,1024]{2,1,0:T(8,128)(2,1)S(1)}, bf16[2,64,1024]{2,1,0:T(8,128)(2,1)S(1)}, u32[]{:S(2)}, u32[]{:S(2)}) collective-permute-start(bf16[2,64,1024]{2,1,0:T(8,128)(2,1)S(1)} %get-tuple-element.123), channel_id=1, source_target_pairs={{0,4},{2,6},{4,0},{6,2},{1,5},{3,7},{5,1},{7,3},{8,12},{10,14},{12... | collective-permute-start | bytes 786440 | tf_op jit(solution)/shard_map/ppermute | solution.py:325
  649.4 15.3 %collective-permute-start.75 = (f32[8,128]{1,0:T(8,128)S(1)}, f32[8,128]{1,0:T(8,128)S(1)}, u32[]{:S(2)}, u32[]{:S(2)}) collective-permute-start(f32[8,128]{1,0:T(8,128)S(1)} %add_add_fusion.1), channel_id=1, source_target_pairs={{0,1},{1,0},{2,3},{3,2},{4,5},{5,4},{6,7},{7,6},{8,9},{9,8},{10,11... | collective-permute-start | bytes 12296 | tf_op jit(solution)/shard_map/ppermute | solution.py:369
  650.0 16.0 %collective-permute-start.70 = (f32[17,1024]{1,0:T(8,128)S(1)}, f32[17,1024]{1,0:T(8,128)S(1)}, u32[]{:S(2)}, u32[]{:S(2)}) collective-permute-start(f32[17,1024]{1,0:T(8,128)S(1)} %add.746), channel_id=1, source_target_pairs={{0,6},{2,4},{4,2},{6,0},{1,7},{3,5},{5,3},{7,1},{8,14},{10,12},{12... | collective-permute-start | bytes 208904 | tf_op jit(solution)/shard_map/ppermute | solution.py:369
  666.0 14.1 %collective-permute-start.68 = (f32[17,1024]{1,0:T(8,128)S(1)}, f32[17,1024]{1,0:T(8,128)S(1)}, u32[]{:S(2)}, u32[]{:S(2)}) collective-permute-start(f32[17,1024]{1,0:T(8,128)S(1)} %add.746), channel_id=1, source_target_pairs={{0,2},{2,0},{4,6},{6,4},{1,3},{3,1},{5,7},{7,5},{8,10},{10,8},{12,... | collective-permute-start | bytes 208904 | tf_op jit(solution)/shard_map/ppermute | solution.py:369
  678.0 52.8 %collective-permute-start.30 = (bf16[2,4,2,32,1024]{4,3,1,2,0:T(8,128)(2,1)}, bf16[2,4,2,32,1024]{4,3,1,2,0:T(8,128)(2,1)}, u32[]{:S(2)}, u32[]{:S(2)}) collective-permute-start(bf16[2,4,2,32,1024]{4,3,1,2,0:T(8,128)(2,1)} %bitcast.384), channel_id=1, source_target_pairs={{0,8},{8,0},{1,9},{9,1},{2,10},{10,2},{3,11},{11,3},{4,12},{12,4},... | collective-permute-start | bytes 3145736 | tf_op jit(solution)/shard_map/ppermute | solution.py:325
  680.1 52.7 %collective-permute-start.12 = (bf16[2,4,2,32,1024]{4,3,1,2,0:T(8,128)(2,1)}, bf16[2,4,2,32,1024]{4,3,1,2,0:T(8,128)(2,1)}, u32[]{:S(2)}, u32[]{:S(2)}) collective-permute-start(bf16[2,4,2,32,1024]{4,3,1,2,0:T(8,128)(2,1)} %bitcast.387), channel_id=1, source_target_pairs={{0,8},{8,0},{1,9},{9,1},{2,10},{10,2},{3,11},{11,3},{4,12},{12,4},... | collective-permute-start | bytes 3145736 | tf_op jit(solution)/shard_map/ppermute | solution.py:325
  682.2 14.7 %collective-permute-start.6 = (bf16[2,128,512]{2,1,0:T(8,128)(2,1)S(1)}, bf16[2,128,512]{2,1,0:T(8,128)(2,1)S(1)}, u32[]{:S(2)}, u32[]{:S(2)}) collective-permute-start(bf16[2,128,512]{2,1,0:T(8,128)(2,1)S(1)} %get-tuple-element.125), channel_id=1, source_target_pairs={{0,6},{2,4},{4,2},{6,0},{1,7},{3,5},{5,3},{7,1},{8,14},{10,12},{12... | collective-permute-start | bytes 786440 | tf_op jit(solution)/shard_map/ppermute | solution.py:325
  684.1 23.2 %collective-permute-start.5 = (bf16[2,128,512]{2,1,0:T(8,128)(2,1)S(1)}, bf16[2,128,512]{2,1,0:T(8,128)(2,1)S(1)}, u32[]{:S(2)}, u32[]{:S(2)}) collective-permute-start(bf16[2,128,512]{2,1,0:T(8,128)(2,1)S(1)} %get-tuple-element.126), channel_id=1, source_target_pairs={{0,4},{2,6},{4,0},{6,2},{1,5},{3,7},{5,1},{7,3},{8,12},{10,14},{12... | collective-permute-start | bytes 786440 | tf_op jit(solution)/shard_map/ppermute | solution.py:325
  689.2 25.3 %collective-permute-start = (bf16[4,128,512]{2,1,0:T(8,128)(2,1)}, bf16[4,128,512]{2,1,0:T(8,128)(2,1)}, u32[]{:S(2)}, u32[]{:S(2)}) collective-permute-start(bf16[4,128,512]{2,1,0:T(8,128)(2,1)} %dynamic-slice_bitcast_fusion.10), channel_id=1, source_target_pairs={{0,1},{1,0},{2,3},{3,2},{4,5},{5,4},{6,7},{7,6},{8,9},{9,8},{10,11... | collective-permute-start | bytes 1572872 | tf_op jit(solution)/shard_map/ppermute | solution.py:325
  721.2 15.2 %collective-permute-start.36 = (bf16[2,4,2,32,1024]{4,3,1,2,0:T(8,128)(2,1)S(1)}, bf16[2,4,2,32,1024]{4,3,1,2,0:T(8,128)(2,1)S(1)}, u32[]{:S(2)}, u32[]{:S(2)}) collective-permute-start(bf16[2,4,2,32,1024]{4,3,1,2,0:T(8,128)(2,1)S(1)} %bitcast.419), channel_id=1, source_target_pairs={{0,8},{8,0},{1,9},{9,1},{2,10},{10,2},{3,11},{11,3},{4,12},{12,4},... | collective-permute-start | bytes 3145736 | tf_op jit(solution)/shard_map/ppermute | solution.py:325
  732.8 106.9 %collective-permute-start.42 = (bf16[2,4,2,32,2048]{4,3,1,0,2:T(8,128)(2,1)S(1)}, bf16[2,4,2,32,2048]{4,3,1,0,2:T(8,128)(2,1)S(1)}, u32[]{:S(2)}, u32[]{:S(2)}) collective-permute-start(bf16[2,4,2,32,2048]{4,3,1,0,2:T(8,128)(2,1)S(1)} %bitcast.409), channel_id=1, source_target_pairs={{0,8},{8,0},{1,9},{9,1},{2,10},{10,2},{3,11},{11,3},{4,12},{12,4},... | collective-permute-start | bytes 6291464 | tf_op jit(solution)/shard_map/ppermute | solution.py:325
  735.5 126.7 %collective-permute-start.54 = (bf16[2,4,2,32,4096]{4,3,1,0,2:T(8,128)(2,1)S(1)}, bf16[2,4,2,32,4096]{4,3,1,0,2:T(8,128)(2,1)S(1)}, u32[]{:S(2)}, u32[]{:S(2)}) collective-permute-start(bf16[2,4,2,32,4096]{4,3,1,0,2:T(8,128)(2,1)S(1)} %bitcast.397), channel_id=1, source_target_pairs={{0,8},{8,0},{1,9},{9,1},{2,10},{10,2},{3,11},{11,3},{4,12},{12,4},... | collective-permute-start | bytes 12582920 | tf_op jit(solution)/shard_map/ppermute | solution.py:325
  736.9 14.3 %collective-permute-start.51 = (bf16[2,2,32,1024]{3,2,1,0:T(8,128)(2,1)S(1)}, bf16[2,2,32,1024]{3,2,1,0:T(8,128)(2,1)S(1)}, u32[]{:S(2)}, u32[]{:S(2)}) collective-permute-start(bf16[2,2,32,1024]{3,2,1,0:T(8,128)(2,1)S(1)} %get-tuple-element.116), channel_id=1, source_target_pairs={{0,6},{2,4},{4,2},{6,0},{1,7},{3,5},{5,3},{7,1},{8,14},{10,12},{12... | collective-permute-start | bytes 786440 | tf_op jit(solution)/shard_map/ppermute | solution.py:325
  739.3 30.8 %collective-permute-start.50 = (bf16[2,2,32,1024]{3,2,1,0:T(8,128)(2,1)S(1)}, bf16[2,2,32,1024]{3,2,1,0:T(8,128)(2,1)S(1)}, u32[]{:S(2)}, u32[]{:S(2)}) collective-permute-start(bf16[2,2,32,1024]{3,2,1,0:T(8,128)(2,1)S(1)} %get-tuple-element.117), channel_id=1, source_target_pairs={{0,4},{2,6},{4,0},{6,2},{1,5},{3,7},{5,1},{7,3},{8,12},{10,14},{12... | collective-permute-start | bytes 786440 | tf_op jit(solution)/shard_map/ppermute | solution.py:325
  745.1 25.2 %collective-permute-start.25 = (bf16[2,2,32,1024]{3,2,1,0:T(8,128)(2,1)S(1)}, bf16[2,2,32,1024]{3,2,1,0:T(8,128)(2,1)S(1)}, u32[]{:S(2)}, u32[]{:S(2)}) collective-permute-start(bf16[2,2,32,1024]{3,2,1,0:T(8,128)(2,1)S(1)} %get-tuple-element.118), channel_id=1, source_target_pairs={{0,2},{2,0},{4,6},{6,4},{1,3},{3,1},{5,7},{7,5},{8,10},{10,8},{12,... | collective-permute-start | bytes 786440 | tf_op jit(solution)/shard_map/ppermute | solution.py:325
  751.2 20.0 %collective-permute-start.27 = (bf16[2,2,32,1024]{3,2,1,0:T(8,128)(2,1)S(1)}, bf16[2,2,32,1024]{3,2,1,0:T(8,128)(2,1)S(1)}, u32[]{:S(2)}, u32[]{:S(2)}) collective-permute-start(bf16[2,2,32,1024]{3,2,1,0:T(8,128)(2,1)S(1)} %get-tuple-element.119), channel_id=1, source_target_pairs={{0,6},{2,4},{4,2},{6,0},{1,7},{3,5},{5,3},{7,1},{8,14},{10,12},{12... | collective-permute-start | bytes 786440 | tf_op jit(solution)/shard_map/ppermute | solution.py:325
  770.1 15.9 %collective-permute-start.26 = (bf16[2,2,32,1024]{3,2,1,0:T(8,128)(2,1)S(1)}, bf16[2,2,32,1024]{3,2,1,0:T(8,128)(2,1)S(1)}, u32[]{:S(2)}, u32[]{:S(2)}) collective-permute-start(bf16[2,2,32,1024]{3,2,1,0:T(8,128)(2,1)S(1)} %get-tuple-element.120), channel_id=1, source_target_pairs={{0,4},{2,6},{4,0},{6,2},{1,5},{3,7},{5,1},{7,3},{8,12},{10,14},{12... | collective-permute-start | bytes 786440 | tf_op jit(solution)/shard_map/ppermute | solution.py:325
  770.3 41.3 %collective-permute-start.31 = (bf16[4,2,32,1024]{3,2,0,1:T(8,128)(2,1)S(1)}, bf16[4,2,32,1024]{3,2,0,1:T(8,128)(2,1)S(1)}, u32[]{:S(2)}, u32[]{:S(2)}) collective-permute-start(bf16[4,2,32,1024]{3,2,0,1:T(8,128)(2,1)S(1)} %dynamic-slice_bitcast_fusion.7), channel_id=1, source_target_pairs={{0,16},{16,0},{1,17},{17,1},{2,18},{18,2},{3,19},{19,3},{4,20},{20... | collective-permute-start | bytes 1572872 | tf_op jit(solution)/shard_map/ppermute | solution.py:325
  771.1 42.0 %collective-permute-start.13 = (bf16[4,2,32,1024]{3,2,0,1:T(8,128)(2,1)S(1)}, bf16[4,2,32,1024]{3,2,0,1:T(8,128)(2,1)S(1)}, u32[]{:S(2)}, u32[]{:S(2)}) collective-permute-start(bf16[4,2,32,1024]{3,2,0,1:T(8,128)(2,1)S(1)} %dynamic-slice_bitcast_fusion.9), channel_id=1, source_target_pairs={{0,16},{16,0},{1,17},{17,1},{2,18},{18,2},{3,19},{19,3},{4,20},{20... | collective-permute-start | bytes 1572872 | tf_op jit(solution)/shard_map/ppermute | solution.py:325
  811.6 14.9 %collective-permute-start.19 = (bf16[2,4,32,1024]{3,2,1,0:T(8,128)(2,1)S(1)}, bf16[2,4,32,1024]{3,2,1,0:T(8,128)(2,1)S(1)}, u32[]{:S(2)}, u32[]{:S(2)}) collective-permute-start(bf16[2,4,32,1024]{3,2,1,0:T(8,128)(2,1)S(1)} %dynamic-slice_bitcast_fusion.8), channel_id=1, source_target_pairs={{0,1},{1,0},{2,3},{3,2},{4,5},{5,4},{6,7},{7,6},{8,9},{9,8},{10,11... | collective-permute-start | bytes 1572872 | tf_op jit(solution)/shard_map/ppermute | solution.py:325
  813.2 17.4 %collective-permute-start.32 = (bf16[4,32,1024]{2,1,0:T(8,128)(2,1)S(1)}, bf16[4,32,1024]{2,1,0:T(8,128)(2,1)S(1)}, u32[]{:S(2)}, u32[]{:S(2)}) collective-permute-start(bf16[4,32,1024]{2,1,0:T(8,128)(2,1)S(1)} %dynamic-slice_bitcast_fusion.21), channel_id=1, source_target_pairs={{0,1},{1,0},{2,3},{3,2},{4,5},{5,4},{6,7},{7,6},{8,9},{9,8},{10,11... | collective-permute-start | bytes 786440 | tf_op jit(solution)/shard_map/ppermute | solution.py:325
  840.8 17.9 %collective-permute-start.43 = (bf16[2,4,32,2048]{3,2,1,0:T(8,128)(2,1)S(1)}, bf16[2,4,32,2048]{3,2,1,0:T(8,128)(2,1)S(1)}, u32[]{:S(2)}, u32[]{:S(2)}) collective-permute-start(bf16[2,4,32,2048]{3,2,1,0:T(8,128)(2,1)S(1)} %dynamic-slice_bitcast_fusion.4), channel_id=1, source_target_pairs={{0,1},{1,0},{2,3},{3,2},{4,5},{5,4},{6,7},{7,6},{8,9},{9,8},{10,11... | collective-permute-start | bytes 3145736 | tf_op jit(solution)/shard_map/ppermute | solution.py:325
  846.3 33.7 %collective-permute-start.60 = (bf16[2,4,2,128,1024]{4,3,1,2,0:T(8,128)(2,1)S(1)}, bf16[2,4,2,128,1024]{4,3,1,2,0:T(8,128)(2,1)S(1)}, u32[]{:S(2)}, u32[]{:S(2)}) collective-permute-start(bf16[2,4,2,128,1024]{4,3,1,2,0:T(8,128)(2,1)S(1)} %bitcast.396), channel_id=1, source_target_pairs={{0,8},{8,0},{1,9},{9,1},{2,10},{10,2},{3,11},{11,3},{4,12},{12,4},... | collective-permute-start | bytes 12582920 | tf_op jit(solution)/shard_map/ppermute | solution.py:325
  865.7 42.9 %collective-permute-start.55 = (bf16[2,4,32,4096]{3,2,1,0:T(8,128)(2,1)}, bf16[2,4,32,4096]{3,2,1,0:T(8,128)(2,1)}, u32[]{:S(2)}, u32[]{:S(2)}) collective-permute-start(bf16[2,4,32,4096]{3,2,1,0:T(8,128)(2,1)} %dynamic-slice_bitcast_fusion.1), channel_id=1, source_target_pairs={{0,1},{1,0},{2,3},{3,2},{4,5},{5,4},{6,7},{7,6},{8,9},{9,8},{10,11... | collective-permute-start | bytes 6291464 | tf_op jit(solution)/shard_map/ppermute | solution.py:325
  867.1 44.7 %collective-permute-start.39 = (bf16[32,1024]{1,0:T(8,128)(2,1)}, bf16[32,1024]{1,0:T(8,128)(2,1)}, u32[]{:S(2)}, u32[]{:S(2)}) collective-permute-start(bf16[32,1024]{1,0:T(8,128)(2,1)} %get-tuple-element.133), channel_id=1, source_target_pairs={{0,2},{2,0},{4,6},{6,4},{1,3},{3,1},{5,7},{7,5},{8,10},{10,8},{12,... | collective-permute-start | bytes 196616 | tf_op jit(solution)/shard_map/ppermute | solution.py:325
  867.2 46.9 %collective-permute-start.41 = (bf16[32,1024]{1,0:T(8,128)(2,1)}, bf16[32,1024]{1,0:T(8,128)(2,1)}, u32[]{:S(2)}, u32[]{:S(2)}) collective-permute-start(bf16[32,1024]{1,0:T(8,128)(2,1)} %get-tuple-element.134), channel_id=1, source_target_pairs={{0,6},{2,4},{4,2},{6,0},{1,7},{3,5},{5,3},{7,1},{8,14},{10,12},{12... | collective-permute-start | bytes 196616 | tf_op jit(solution)/shard_map/ppermute | solution.py:325
  878.6 37.2 %collective-permute-start.40 = (bf16[32,1024]{1,0:T(8,128)(2,1)}, bf16[32,1024]{1,0:T(8,128)(2,1)}, u32[]{:S(2)}, u32[]{:S(2)}) collective-permute-start(bf16[32,1024]{1,0:T(8,128)(2,1)} %get-tuple-element.135), channel_id=1, source_target_pairs={{0,4},{2,6},{4,0},{6,2},{1,5},{3,7},{5,1},{7,3},{8,12},{10,14},{12... | collective-permute-start | bytes 196616 | tf_op jit(solution)/shard_map/ppermute | solution.py:325
  880.0 38.8 %collective-permute-start.45 = (bf16[32,2048]{1,0:T(8,128)(2,1)S(1)}, bf16[32,2048]{1,0:T(8,128)(2,1)S(1)}, u32[]{:S(2)}, u32[]{:S(2)}) collective-permute-start(bf16[32,2048]{1,0:T(8,128)(2,1)S(1)} %get-tuple-element.127), channel_id=1, source_target_pairs={{0,2},{2,0},{4,6},{6,4},{1,3},{3,1},{5,7},{7,5},{8,10},{10,8},{12,... | collective-permute-start | bytes 393224 | tf_op jit(solution)/shard_map/ppermute | solution.py:325
  908.6 48.6 %collective-permute-start.61 = (bf16[4,2,128,1024]{3,2,0,1:T(8,128)(2,1)S(1)}, bf16[4,2,128,1024]{3,2,0,1:T(8,128)(2,1)S(1)}, u32[]{:S(2)}, u32[]{:S(2)}) collective-permute-start(bf16[4,2,128,1024]{3,2,0,1:T(8,128)(2,1)S(1)} %dynamic-slice_bitcast_fusion), channel_id=1, source_target_pairs={{0,16},{16,0},{1,17},{17,1},{2,18},{18,2},{3,19},{19,3},{4,20},{20... | collective-permute-start | bytes 6291464 | tf_op jit(solution)/shard_map/ppermute | solution.py:325
  915.8 56.9 %collective-permute-start.56 = (bf16[4,32,4096]{2,1,0:T(8,128)(2,1)S(1)}, bf16[4,32,4096]{2,1,0:T(8,128)(2,1)S(1)}, u32[]{:S(2)}, u32[]{:S(2)}) collective-permute-start(bf16[4,32,4096]{2,1,0:T(8,128)(2,1)S(1)} %dynamic-slice_bitcast_fusion.3), channel_id=1, source_target_pairs={{0,16},{16,0},{1,17},{17,1},{2,18},{18,2},{3,19},{19,3},{4,20},{20... | collective-permute-start | bytes 3145736 | tf_op jit(solution)/shard_map/ppermute | solution.py:325
  958.2 21.8 %collective-permute-start.62 = (bf16[4,128,1024]{2,1,0:T(8,128)(2,1)S(1)}, bf16[4,128,1024]{2,1,0:T(8,128)(2,1)S(1)}, u32[]{:S(2)}, u32[]{:S(2)}) collective-permute-start(bf16[4,128,1024]{2,1,0:T(8,128)(2,1)S(1)} %dynamic-slice_bitcast_fusion.2), channel_id=1, source_target_pairs={{0,1},{1,0},{2,3},{3,2},{4,5},{5,4},{6,7},{7,6},{8,9},{9,8},{10,11... | collective-permute-start | bytes 3145736 | tf_op jit(solution)/shard_map/ppermute | solution.py:325
  973.0 19.1 %collective-permute-start.57 = (bf16[32,4096]{1,0:T(8,128)(2,1)S(1)}, bf16[32,4096]{1,0:T(8,128)(2,1)S(1)}, u32[]{:S(2)}, u32[]{:S(2)}) collective-permute-start(bf16[32,4096]{1,0:T(8,128)(2,1)S(1)} %get-tuple-element.112), channel_id=1, source_target_pairs={{0,2},{2,0},{4,6},{6,4},{1,3},{3,1},{5,7},{7,5},{8,10},{10,8},{12,... | collective-permute-start | bytes 786440 | tf_op jit(solution)/shard_map/ppermute | solution.py:325
  978.5 14.3 %collective-permute-start.59 = (bf16[32,4096]{1,0:T(8,128)(2,1)S(1)}, bf16[32,4096]{1,0:T(8,128)(2,1)S(1)}, u32[]{:S(2)}, u32[]{:S(2)}) collective-permute-start(bf16[32,4096]{1,0:T(8,128)(2,1)S(1)} %get-tuple-element.113), channel_id=1, source_target_pairs={{0,6},{2,4},{4,2},{6,0},{1,7},{3,5},{5,3},{7,1},{8,14},{10,12},{12... | collective-permute-start | bytes 786440 | tf_op jit(solution)/shard_map/ppermute | solution.py:325
  979.8 33.1 %collective-permute-start.58 = (bf16[32,4096]{1,0:T(8,128)(2,1)S(1)}, bf16[32,4096]{1,0:T(8,128)(2,1)S(1)}, u32[]{:S(2)}, u32[]{:S(2)}) collective-permute-start(bf16[32,4096]{1,0:T(8,128)(2,1)S(1)} %get-tuple-element.114), channel_id=1, source_target_pairs={{0,4},{2,6},{4,0},{6,2},{1,5},{3,7},{5,1},{7,3},{8,12},{10,14},{12... | collective-permute-start | bytes 786440 | tf_op jit(solution)/shard_map/ppermute | solution.py:325
  980.5 33.3 %collective-permute-start.63 = (bf16[128,1024]{1,0:T(8,128)(2,1)S(1)}, bf16[128,1024]{1,0:T(8,128)(2,1)S(1)}, u32[]{:S(2)}, u32[]{:S(2)}) collective-permute-start(bf16[128,1024]{1,0:T(8,128)(2,1)S(1)} %get-tuple-element.109), channel_id=1, source_target_pairs={{0,2},{2,0},{4,6},{6,4},{1,3},{3,1},{5,7},{7,5},{8,10},{10,8},{12,... | collective-permute-start | bytes 786440 | tf_op jit(solution)/shard_map/ppermute | solution.py:325
  983.4 30.4 %collective-permute-start.65 = (bf16[128,1024]{1,0:T(8,128)(2,1)S(1)}, bf16[128,1024]{1,0:T(8,128)(2,1)S(1)}, u32[]{:S(2)}, u32[]{:S(2)}) collective-permute-start(bf16[128,1024]{1,0:T(8,128)(2,1)S(1)} %get-tuple-element.110), channel_id=1, source_target_pairs={{0,6},{2,4},{4,2},{6,0},{1,7},{3,5},{5,3},{7,1},{8,14},{10,12},{12... | collective-permute-start | bytes 786440 | tf_op jit(solution)/shard_map/ppermute | solution.py:325
  992.1 29.5 %collective-permute-start.64 = (bf16[128,1024]{1,0:T(8,128)(2,1)S(1)}, bf16[128,1024]{1,0:T(8,128)(2,1)S(1)}, u32[]{:S(2)}, u32[]{:S(2)}) collective-permute-start(bf16[128,1024]{1,0:T(8,128)(2,1)S(1)} %get-tuple-element.111), channel_id=1, source_target_pairs={{0,4},{2,6},{4,0},{6,2},{1,5},{3,7},{5,1},{7,3},{8,12},{10,14},{12... | collective-permute-start | bytes 786440 | tf_op jit(solution)/shard_map/ppermute | solution.py:325
  (125 other events, 1216.1 us)
Sparse Core Ops, SparseCore 0:
  10.8 63.1 all-gather.7
  77.4 69.3 all-gather.5
  150.3 85.2 all-gather.9
  238.5 75.7 all-gather.11
  317.1 75.9 all-gather.13

commit v2 on v1

--- a/solution.py
+++ b/solution.py
@@ -1,4 +1,5 @@
 import functools
+import itertools
 
 import jax
 import jax.numpy as jnp
@@ -29,20 +30,22 @@
     )
 
 
-def bias_fill(sc_ref, prompt_bias, own_bias, flip):
+def bias_fill(sc_ref, prompt_bias, own_bias, flip, segs=(0, 1)):
     begin, cont_begin, block = sc_ref[0], sc_ref[1], sc_ref[2]
     q_dim, k_dim = (1, 0) if flip else (0, 1)
-    shape = prompt_bias.shape
-    rows = shape[q_dim]
-    spot = lax.broadcasted_iota(jnp.int32, shape, q_dim) + block * rows
-    key = lax.broadcasted_iota(jnp.int32, shape, k_dim)
-    seen = (key <= spot) & ((key >= begin) | (key == spot))
-    prompt_bias[...] = jnp.where(seen, 0.0, MASKED)
-    shape = own_bias.shape
-    spot = lax.broadcasted_iota(jnp.int32, shape, q_dim)
-    key = lax.broadcasted_iota(jnp.int32, shape, k_dim)
-    seen = (key <= spot) & ((key >= cont_begin) | (key == spot))
-    own_bias[...] = jnp.where(seen, 0.0, MASKED)
+    if 0 in segs:
+        shape = prompt_bias.shape
+        rows = shape[q_dim]
+        spot = lax.broadcasted_iota(jnp.int32, shape, q_dim) + block * rows
+        key = lax.broadcasted_iota(jnp.int32, shape, k_dim)
+        seen = (key <= spot) & ((key >= begin) | (key == spot))
+        prompt_bias[...] = jnp.where(seen, 0.0, MASKED)
+    if 1 in segs:
+        shape = own_bias.shape
+        spot = lax.broadcasted_iota(jnp.int32, shape, q_dim)
+        key = lax.broadcasted_iota(jnp.int32, shape, k_dim)
+        seen = (key <= spot) & ((key >= cont_begin) | (key == spot))
+        own_bias[...] = jnp.where(seen, 0.0, MASKED)
 
 
 def self_plan(prompt_rows, prompt_len, slot_len):
@@ -128,13 +131,17 @@
         total_ref[keys.start + known : keys.stop, :] = part[known:]
 
 
-def bwd_kernel(plan, masked, slot_at, key_step, *refs):
-    n_seg = 2 if masked else 1
+def bwd_kernel(plan, masked, slot_at, key_step, segs, onto, *refs):
+    n_seg = len(segs)
     if masked:
         sc_ref, refs = refs[0], refs[1:]
     q_ref, g_ref, o_ref, lse_ref = refs[:4]
     k_refs, v_refs = refs[4 : 4 + n_seg], refs[4 + n_seg : 4 + 2 * n_seg]
     outs = refs[4 + 2 * n_seg :]
+    if onto:
+        dq_in, outs = outs[0], outs[1:]
+        dq_in_rows = slice(0, plan[0][0])
+        outs[0][dq_in_rows, :] = dq_in[dq_in_rows, :].astype(outs[0].dtype)
     dq_ref, dk_refs, dv_refs = outs[0], outs[1 : 1 + n_seg], outs[1 + n_seg : 1 + 2 * n_seg]
     scratch = outs[1 + 2 * n_seg :]
     dk_acc, dv_acc = scratch[:n_seg], scratch[n_seg : 2 * n_seg]
@@ -144,7 +151,7 @@
 
         @pl.when(pair == 0)
         def _():
-            bias_fill(sc_ref, prompt_bias, own_bias, True)
+            bias_fill(sc_ref, prompt_bias, own_bias, True, segs)
 
     done = [0] * n_seg
     picks = jnp.concatenate(
@@ -162,13 +169,14 @@
             precision=lax.Precision.HIGHEST,
             preferred_element_type=jnp.float32,
         )
-        dq = 0.0
+        dq = dq_in[rows, :] if onto else 0.0
         for head in (0, 1):
             lanes = head_lanes(head)
             q_one, g_one = only(q_blk, lanes), only(g_blk, lanes)
             lse = lse_ref[0, head : head + 1, rows]
             row_inner = inner[head : head + 1, :]
-            for seg, k_n, kind in parts:
+            for which, k_n, kind in parts:
+                seg = segs.index(which)
                 for at in range(0, k_n, key_step):
                     keys = slice(at, min(at + key_step, k_n))
                     k_one = only(k_refs[seg][keys, :], lanes)
@@ -191,7 +199,7 @@
                     accumulate(dk_acc[seg], keys, done[seg], add_k)
                     dq = dq + product_tn(grad_scores, k_one)
                 done[seg] = max(done[seg], k_n)
-        dq_ref[rows, :] = dq.astype(jnp.bfloat16)
+        dq_ref[rows, :] = dq.astype(dq_ref.dtype)
     for seg in range(n_seg):
         dk_refs[seg][...] = dk_acc[seg][...].astype(jnp.bfloat16)
         dv_refs[seg][...] = dv_acc[seg][...].astype(jnp.bfloat16)
@@ -232,52 +240,200 @@
         compiler_params=pltpu.CompilerParams(
             dimension_semantics=("arbitrary",), vmem_limit_bytes=VMEM_LIMIT
         ),
-        cost_estimate=pl.CostEstimate(
-            flops=4 * area * HEADS * 128,
-            bytes_accessed=4 * row_total * width + sum(2 * kv.size for kv in kv_list),
-            transcendentals=area * HEADS,
-        ),
+        cost_estimate=pl.CostEstimate(flops=1, bytes_accessed=1, transcendentals=0),
         name="attend_forward",
     )(*([scalars] if masked else []), queries, *kv_list, *kv_list)
 
 
-def attend_backward(scalars, queries, grads, mixed, log_totals, kv_list, plan, slot_at, key_step):
+def attend_backward(
+    scalars, queries, grads, mixed, log_totals, kv_list, plan, slot_at, key_step, segs, onto=None
+):
     masked = scalars is not None
     row_total, width = queries.shape
     pairs = width // (2 * HDIM)
     lse = log_totals[:, :HEADS].T.reshape(pairs, 2, row_total)
+    plan = tuple(
+        (q_at, q_n, kept)
+        for q_at, q_n, parts in plan
+        if (kept := tuple(part for part in parts if part[0] in segs))
+    )
+    prompt_len, slot_len = kv_list[0].shape[0], kv_list[-1].shape[0]
+    kv_list = [kv_list[seg] for seg in segs]
     scratch = [pltpu.VMEM((kv.shape[0], 2 * HDIM), jnp.float32) for kv in kv_list] * 2
     if masked:
-        prompt_len, slot_len = kv_list[0].shape[0], kv_list[1].shape[0]
         scratch += [
-            pltpu.VMEM((prompt_len, slot_at), jnp.float32),
-            pltpu.VMEM((slot_len, slot_len), jnp.float32),
+            pltpu.VMEM((prompt_len if 0 in segs else 8, slot_at), jnp.float32),
+            pltpu.VMEM((slot_len, slot_len) if 1 in segs else (8, 128), jnp.float32),
         ]
     area = sum(q_n * k_n for _, q_n, parts in plan for _, k_n, _ in parts)
     n_seg = len(kv_list)
+    partial = masked and 1 not in segs
+    given = [] if onto is None else [onto]
     outs = pl.pallas_call(
-        functools.partial(bwd_kernel, plan, masked, slot_at, key_step),
+        functools.partial(bwd_kernel, plan, masked, slot_at, key_step, segs, bool(given)),
         grid=(pairs,),
         in_specs=([pl.BlockSpec(memory_space=pltpu.SMEM)] if masked else [])
         + [pair_spec(row_total)] * 3
         + [pl.BlockSpec((1, 2, row_total), lambda i: (i, 0, 0))]
         + [pair_spec(kv.shape[0]) for kv in kv_list]
-        + [pair_spec(kv.shape[0], pairs) for kv in kv_list],
+        + [pair_spec(kv.shape[0], pairs) for kv in kv_list]
+        + [pair_spec(row_total)] * len(given),
         out_specs=[pair_spec(row_total)] + [pair_spec(kv.shape[0]) for kv in kv_list] * 2,
-        out_shape=[jax.ShapeDtypeStruct((row_total, width), jnp.bfloat16)]
+        out_shape=[
+            jax.ShapeDtypeStruct((row_total, width), jnp.float32 if partial else jnp.bfloat16)
+        ]
         + [jax.ShapeDtypeStruct((kv.shape[0], width), jnp.bfloat16) for kv in kv_list] * 2,
         scratch_shapes=scratch,
         compiler_params=pltpu.CompilerParams(
             dimension_semantics=("arbitrary",), vmem_limit_bytes=VMEM_LIMIT
         ),
-        cost_estimate=pl.CostEstimate(
-            flops=10 * area * HEADS * 128,
-            bytes_accessed=8 * row_total * width + sum(4 * kv.size for kv in kv_list),
-            transcendentals=area * HEADS,
+        cost_estimate=pl.CostEstimate(flops=1, bytes_accessed=1, transcendentals=0),
+        name="attend_backward",
+    )(*([scalars] if masked else []), queries, grads, mixed, lse, *kv_list, *kv_list, *given)
+    return outs[0], outs[1 : 1 + n_seg], outs[1 + n_seg :]
+def ffn_backward_kernel(
+    core_ref,
+    g_ref,
+    h_ref,
+    act_ref,
+    slope_ref,
+    down_ref,
+    up_ref,
+    down_other,
+    down_mine,
+    up_other,
+    up_mine,
+    bias_ref,
+    out_ref,
+    turned,
+):
+    step, steps = pl.program_id(0), pl.num_programs(0)
+    core = core_ref[0]
+    quarter = h_ref.shape[1] // 4
+
+    @pl.when(step == 0)
+    def _():
+        for at, flip in ((0, 1), (1, 0)):
+            for x in (0, 1):
+                first = pl.multiple_of((2 * x + (core ^ flip)) * quarter, quarter)
+                spot = (2 * at + x) * quarter
+                turned[spot : spot + quarter, :] = h_ref[:, pl.ds(first, quarter)].T
+
+    grad = g_ref[...]
+    pre = product_nt(grad, down_ref[...]) * slope_ref[...].astype(jnp.float32)
+    bias_ref[...] = jnp.sum(pre, 0, keepdims=True)
+    pre = pre.astype(jnp.bfloat16)
+    add = product_nt(pre, up_ref[...])
+
+    @pl.when(step == 0)
+    def _():
+        out_ref[...] = add
+
+    @pl.when(step > 0)
+    def _():
+        out_ref[...] += add
+
+    up_other[...] = product(turned[: 2 * quarter, :], pre).astype(jnp.bfloat16)
+    up_mine[...] = product(turned[2 * quarter :, :], pre).astype(jnp.bfloat16)
+    down = product_tn(act_ref[...], grad).astype(jnp.bfloat16)
+
+    @pl.when(step < steps // 2)
+    def _():
+        down_other[...] = down
+
+    @pl.when(step >= steps // 2)
+    def _():
+        down_mine[...] = down
+
+
+def ffn_backward(core, grad_ffn, hidden_two, act, slope, w_down, w_up, step=1024):
+    rows, width = hidden_two.shape
+    units = w_up.shape[1]
+    steps = units // step
+    inner = steps // 4
+    half = steps // 2
+
+    def unit(i, core_ref):
+        other = i < half
+        j = jnp.where(other, i, i - half)
+        c = jnp.where(other, 1 - core_ref[0], core_ref[0])
+        return ((j // inner) * 2 + c) * inner + j % inner
+
+    whole = pl.BlockSpec((rows, width), lambda i, core_ref: (0, 0))
+    block = pl.BlockSpec((rows, step), lambda i, core_ref: (0, unit(i, core_ref)))
+    up_block = pl.BlockSpec((width // 2, step), lambda i, core_ref: (0, unit(i, core_ref)))
+    return pl.pallas_call(
+        ffn_backward_kernel,
+        grid_spec=pltpu.PrefetchScalarGridSpec(
+            num_scalar_prefetch=1,
+            grid=(steps,),
+            in_specs=[
+                whole,
+                whole,
+                block,
+                block,
+                pl.BlockSpec((step, width), lambda i, core_ref: (unit(i, core_ref), 0)),
+                pl.BlockSpec((width, step), lambda i, core_ref: (0, unit(i, core_ref))),
+            ],
+            out_specs=[
+                pl.BlockSpec((step, width), lambda i, core_ref: (jnp.minimum(i, half - 1), 0)),
+                pl.BlockSpec((step, width), lambda i, core_ref: (jnp.maximum(i - half, 0), 0)),
+                up_block,
+                up_block,
+                pl.BlockSpec((1, step), lambda i, core_ref: (0, unit(i, core_ref))),
+                whole,
+            ],
+            scratch_shapes=[pltpu.VMEM((width, rows), jnp.bfloat16)],
         ),
-        name="attend_backward",
-    )(*([scalars] if masked else []), queries, grads, mixed, lse, *kv_list, *kv_list)
-    return outs[0], outs[1 : 1 + n_seg], outs[1 + n_seg :]
+        out_shape=[
+            jax.ShapeDtypeStruct((units // 2, width), jnp.bfloat16),
+            jax.ShapeDtypeStruct((units // 2, width), jnp.bfloat16),
+            jax.ShapeDtypeStruct((width // 2, units), jnp.bfloat16),
+            jax.ShapeDtypeStruct((width // 2, units), jnp.bfloat16),
+            jax.ShapeDtypeStruct((1, units), jnp.float32),
+            jax.ShapeDtypeStruct((rows, width), jnp.float32),
+        ],
+        compiler_params=pltpu.CompilerParams(
+            dimension_semantics=("arbitrary",), vmem_limit_bytes=VMEM_LIMIT
+        ),
+        cost_estimate=pl.CostEstimate(flops=1, bytes_accessed=1, transcendentals=0),
+        name="ffn_backward",
+    )(core, grad_ffn, hidden_two, act, slope, w_down, w_up)
+
+
+def half_products_kernel(counts, has_came, core_ref, *refs):
+    out_ref = refs[-1]
+    came_ref = refs[-2] if has_came else None
+    at = 0
+    for term, count in enumerate(counts):
+        pairs = [(refs[at + 2 * i], refs[at + 2 * i + 1]) for i in range(count)]
+        at += 2 * count
+        quarter = pairs[0][0].shape[1] // 4
+        for x in (0, 1):
+            rows = slice(x * quarter, (x + 1) * quarter)
+            first = pl.multiple_of((2 * x + core_ref[0]) * quarter, quarter)
+            total = sum(product_tn(left[:, pl.ds(first, quarter)], right[...]) for left, right in pairs)
+            if has_came:
+                total = total + came_ref[term, rows, :].astype(jnp.float32)
+            out_ref[term, rows, :] = total.astype(jnp.bfloat16)
+
+
+def half_products(core, terms, came=None):
+    arrays = [matrix for pairs in terms for pair in pairs for matrix in pair]
+    shape = (len(terms), arrays[0].shape[1] // 2, arrays[1].shape[1])
+    given = [] if came is None else [came]
+    return pl.pallas_call(
+        functools.partial(
+            half_products_kernel, tuple(len(pairs) for pairs in terms), came is not None
+        ),
+        in_specs=[pl.BlockSpec(memory_space=pltpu.SMEM)]
+        + [pl.BlockSpec(memory_space=pltpu.VMEM)] * (len(arrays) + len(given)),
+        out_specs=pl.BlockSpec(memory_space=pltpu.VMEM),
+        out_shape=jax.ShapeDtypeStruct(shape, jnp.bfloat16),
+        compiler_params=pltpu.CompilerParams(vmem_limit_bytes=VMEM_LIMIT),
+        cost_estimate=pl.CostEstimate(flops=1, bytes_accessed=1, transcendentals=0),
+        name="half_products",
+    )(core, *arrays, *given)
 
 
 def column_sum(matrix):
@@ -309,66 +465,334 @@
     return lax.ppermute(value, axis, SWAP)
 
 
-def xor_perm(count, shift):
-    return tuple((i, i ^ shift) for i in range(count))
-
-
-def reduce_stages(part, names, order):
-    names = list(names)
-    for axis in order:
-        dim = names.index(axis)
-        count = part.shape[dim]
-        here = lax.axis_index(axis)
-        total = lax.dynamic_index_in_dim(part, here, dim, keepdims=False).astype(jnp.float32)
-        for shift in range(1, count):
-            other = lax.dynamic_index_in_dim(part, here ^ shift, dim, keepdims=False)
-            came = lax.ppermute(other, axis, xor_perm(count, shift))
-            total = total + came.astype(jnp.float32)
-        names.pop(dim)
-        part = total if not names else total.astype(jnp.bfloat16)
-    return part
+class RowSum:
+    def __init__(self, part):
+        self.part, self.names, self.coming = part, ["y", "z", "w"], None
+
+    def pick(self, flip):
+        axis = self.names[0]
+        return lax.dynamic_index_in_dim(
+            self.part, lax.axis_index(axis) ^ flip, "wzy".index(axis), keepdims=False
+        )
+
+    def operands(self):
+        return [self.pick(1)]
+
+    def launch(self, operands):
+        self.coming = swap(operands[0], self.names[0])
+
+    def add(self):
+        total = self.pick(0).astype(jnp.float32) + self.coming.astype(jnp.float32)
+        self.names.pop(0)
+        self.part = total.astype(jnp.bfloat16) if self.names else total
+        self.coming = None
+
+    def finish(self):
+        while self.names:
+            if self.coming is None:
+                self.launch(self.operands())
+            self.add()
+        return self.part
+
+
+class WeightSum:
+    def __init__(self, other, mine):
+        self.other, self.mine = other, mine
+        self.names, self.coming = ["c", "xy", "yx", "z", "w"], None
+
+    def operands(self):
+        if self.names[0] == "c":
+            return [self.other]
+        return [self.pick(side, 1) for side in range(len(self.sides))]
+
+    def pick(self, side, flip):
+        stage = self.names[0]
+        dim = {"xy": (1, 4), "yx": (3, 1), "z": (2,), "w": (1,)}[stage][side]
+        here = lax.axis_index(stage[side]) ^ flip
+        return lax.dynamic_index_in_dim(self.sides[side], here, dim, keepdims=False)
+
+    def launch(self, operands):
+        self.coming = [swap(operand, axis) for operand, axis in zip(operands, self.names[0])]
+
+    def add(self):
+        f32, bf16 = jnp.float32, jnp.bfloat16
+        stage, coming = self.names[0], self.coming
+        if stage == "c":
+            total = self.mine(coming[0])
+            terms, rows, width = total.shape
+            total = total.reshape(terms, 2, 2, 2, 2, rows // 16, width)
+            self.sides = [total[..., : width // 2], total[..., width // 2 :]]
+        else:
+            self.sides = [
+                self.pick(side, 0).astype(f32) + came.astype(f32)
+                for side, came in enumerate(coming)
+            ]
+            if stage != "w":
+                self.sides = [side.astype(bf16) for side in self.sides]
+            if stage == "yx":
+                self.sides = [jnp.concatenate(self.sides, -1)]
+        self.names.pop(0)
+        self.coming = None
+
+    def finish(self):
+        while self.names:
+            if self.coming is None:
+                self.launch(self.operands())
+            self.add()
+        return self.sides[0]
+
+
+class Whole:
+    def __init__(self, axes, parts):
+        self.names, self.coming = [], None
+        self.parts = [
+            lax.psum_scatter(part.astype(jnp.bfloat16), axes, scatter_dimension=0, tiled=True)
+            for part in parts
+        ]
+
+    def finish(self):
+        return jnp.stack(self.parts).astype(jnp.float32)
+
+
+def begin(value, *transfers):
+    live = [t for t in transfers if t.names]
+    if not live:
+        return value
+    value, operands = lax.optimization_barrier((value, [t.operands() for t in live]))
+    for t, ready in zip(live, operands):
+        t.launch(ready)
+    return value
+
+
+def advance(value, *transfers):
+    live = [t for t in transfers if t.coming is not None]
+    if not live:
+        return value
+    value, arrived = lax.optimization_barrier((value, [t.coming for t in live]))
+    for t, coming in zip(live, arrived):
+        t.coming = coming
+        t.add()
+    return begin(value, *live)
+
+
+class Rows:
+    def __init__(self, part):
+        self.part, self.names, self.coming = part, (), None
+
+    def finish(self):
+        return self.part.astype(jnp.float32)
+
+
+class Known:
+    def __init__(self, parts):
+        self.parts, self.names, self.coming = parts, (), None
+
+    def finish(self, place):
+        return self.parts
+
+
+class RowGathering:
+    def __init__(self, block, cuts):
+        self.block, self.cuts, self.names = block, cuts, ["w", "z", "y"]
+        self.coming = None
+
+    def operands(self):
+        return [self.block]
+
+    def launch(self, operands):
+        (self.block,) = operands
+        self.coming = swap(self.block, self.names[0])
+
+    def add(self):
+        self.names.pop(0)
+        self.block = jnp.stack([self.block, self.coming])
+        self.coming = None
+
+    def finish(self, place):
+        while self.names:
+            if self.coming is None:
+                self.launch(self.operands())
+            self.add()
+        return assemble_rows(place, self.cuts, self.block)
+
+
+def put_blocks(own, source, spans, outs, lead):
+    shard = source.shape[-2]
+    for y, z, w in itertools.product(range(2), range(2), range(2)):
+        place = ((own[0] ^ w) * 2 + (own[1] ^ z)) * 2 + (own[2] ^ y)
+        rows = pl.ds(pl.multiple_of(place * shard, shard), shard)
+        for first, out, column, count in spans:
+            outs[out][rows, column : column + count] = source[
+                (*lead(y), z, w, slice(None), slice(first, first + count))
+            ]
+
+
+def assemble_kernel(spans, place_ref, left_own, right_own, left_came, right_came, *outs):
+    own = (place_ref[2], place_ref[3], place_ref[4])
+    core = pl.program_id(0)
+    for which, left, right in ((0, left_own, right_own), (1, left_came, right_came)):
+
+        @pl.when(core == which)
+        def _(left=left, right=right):
+            put_blocks(own, left, spans[0], outs, lambda y: (0, y))
+            put_blocks(own, right, spans[1], outs, lambda y: (y, 0))
+
+
+def assemble(place, spans, arrays, shapes):
+    left_own, right_own, _, _ = arrays
+    shard = left_own.shape[-2]
+
+    def left_spec(which):
+        def at(core, x, _):
+            return (jnp.where(core == which, x, 1 - which), 0, 0, 0, 0, 0)
+
+        return pl.BlockSpec((1, 2, 2, 2, shard, left_own.shape[-1]), at)
+
+    def right_spec(which):
+        def at(core, x, _):
+            return (0, jnp.where(core == which, x, 1 - which), 0, 0, 0, 0)
+
+        return pl.BlockSpec((2, 1, 2, 2, shard, right_own.shape[-1]), at)
+
+    def out_at(core, x, place_ref):
+        return ((place_ref[0] ^ x) * 2 + (place_ref[1] ^ core), 0)
+
+    return pl.pallas_call(
+        functools.partial(assemble_kernel, spans),
+        grid_spec=pltpu.PrefetchScalarGridSpec(
+            num_scalar_prefetch=1,
+            grid=(2, 2),
+            in_specs=[left_spec(0), right_spec(0), left_spec(1), right_spec(1)],
+            out_specs=[pl.BlockSpec((8 * shard, shape[1]), out_at) for shape in shapes],
+        ),
+        out_shape=[jax.ShapeDtypeStruct(shape, jnp.bfloat16) for shape in shapes],
+        compiler_params=pltpu.CompilerParams(
+            dimension_semantics=("arbitrary", "arbitrary"), vmem_limit_bytes=VMEM_LIMIT
+        ),
+        cost_estimate=pl.CostEstimate(
+            flops=0, transcendentals=0, bytes_accessed=sum(4 * array.size for array in arrays)
+        ),
+        name="assemble",
+    )(place, *arrays)
+
+
+def assemble_rows_kernel(cuts, place_ref, source, *outs):
+    own = (place_ref[2], place_ref[3], place_ref[4])
+    for out, (first, count) in zip(outs, cuts):
+        for y, z, w in itertools.product(range(2), range(2), range(2)):
+            block = ((own[0] ^ w) * 2 + (own[1] ^ z)) * 2 + (own[2] ^ y)
+            rows = pl.ds(pl.multiple_of(block * count, count), count)
+            out[rows, :] = source[y, z, w, first : first + count, :]
+
+
+def assemble_rows(place, cuts, gathered):
+    width = gathered.shape[-1]
+    return pl.pallas_call(
+        functools.partial(assemble_rows_kernel, cuts),
+        in_specs=[pl.BlockSpec(memory_space=pltpu.SMEM), pl.BlockSpec(memory_space=pltpu.VMEM)],
+        out_specs=[pl.BlockSpec(memory_space=pltpu.VMEM) for _ in cuts],
+        out_shape=[jax.ShapeDtypeStruct((8 * count, width), jnp.bfloat16) for _, count in cuts],
+        compiler_params=pltpu.CompilerParams(vmem_limit_bytes=VMEM_LIMIT),
+        cost_estimate=pl.CostEstimate(
+            flops=0, transcendentals=0, bytes_accessed=4 * gathered.size
+        ),
+        name="assemble_rows",
+    )(place, gathered)
+
+
+class Gathering:
+    def __init__(self, block, cut, spans, shapes):
+        self.sides, self.cut = [block], cut
+        self.spans, self.shapes = spans, shapes
+        self.names, self.coming = ["w", "z", "yx", "xy", "cc"], None
+
+    def operands(self):
+        return self.sides
+
+    def launch(self, operands):
+        self.sides = operands
+        self.coming = [swap(side, axis) for side, axis in zip(operands, self.names[0])]
+
+    def add(self):
+        stage = self.names.pop(0)
+        coming, self.coming = self.coming, None
+        if stage == "cc":
+            self.arrived = coming
+        elif stage == "z":
+            pair = [self.sides[0], coming[0]]
+            self.sides = [
+                jnp.stack([block[..., : self.cut] for block in pair]),
+                jnp.stack([block[..., self.cut :] for block in pair]),
+            ]
+        else:
+            self.sides = [jnp.stack(pair) for pair in zip(self.sides, coming)]
+
+    def finish(self, place):
+        while self.names:
+            if self.coming is None:
+                self.launch(self.operands())
+            self.add()
+        return assemble(place, self.spans, [*self.sides, *self.arrived], self.shapes)
 
 
 class Links:
     def __init__(self, mesh):
         self.fast = dict(mesh.shape) == {"fsdp": 4, "ctx": 8}
         if self.fast:
-            self.mesh = Mesh(mesh.devices.reshape(2, 2, 4, 2), ("x", "c", "z", "y"))
-            self.rows, self.ctx = ("x", "c"), ("z", "y")
+            self.mesh = Mesh(mesh.devices.reshape(2, 2, 2, 2, 2), ("x", "c", "w", "z", "y"))
+            self.rows, self.ctx = ("x", "c"), ("w", "z", "y")
         else:
             self.mesh, self.rows, self.ctx = mesh, ("fsdp",), ("ctx",)
         self.every = self.rows + self.ctx
 
-    def gather(self, value, axes):
-        return lax.all_gather(value, axes, axis=0, tiled=True)
-
-    def scatter(self, part, order):
+    def place(self):
+        axes = self.every if self.fast else ()
+        return jnp.stack([lax.axis_index(axis).astype(jnp.int32) for axis in axes or self.rows])
+
+    def gather(self, weights, cut):
+        if not self.fast:
+            return Known([lax.all_gather(w, self.every, axis=0, tiled=True) for w in weights])
+        shapes = tuple((32 * w.shape[0], w.shape[1]) for w in weights)
+        block = weights[0] if len(weights) == 1 else jnp.concatenate(weights, 1)
+        first, left, right = 0, [], []
+        for out, weight in enumerate(weights):
+            count = weight.shape[1]
+            low = min(max(cut - first, 0), count)
+            if low:
+                left.append((first, out, 0, low))
+            if low < count:
+                right.append((first + low - cut, out, low, count - low))
+            first += count
+        return Gathering(block, cut, (tuple(left), tuple(right)), shapes)
+
+    def gather_once(self, weights):
+        return lax.all_gather(jnp.concatenate(weights, 1), self.every, axis=0, tiled=True)
+
+    def gather_rows(self, parts):
+        if not self.fast:
+            return Known([lax.all_gather(part, self.ctx, axis=0, tiled=True) for part in parts])
+        cuts, first = [], 0
+        for part in parts:
+            cuts.append((first, part.shape[0]))
+            first += part.shape[0]
+        return RowGathering(jnp.concatenate(parts, 0), tuple(cuts))
+
+    def weight_sum(self, terms):
+        if not self.fast:
+            return Whole(
+                self.every,
+                [sum(product_tn(left, right) for left, right in pairs) for pairs in terms],
+            )
+        core = lax.axis_index("c").astype(jnp.int32).reshape(1)
+        return WeightSum(
+            half_products(1 - core, terms), lambda came: half_products(core, terms, came)
+        )
+
+    def row_sum(self, part):
         part = part.astype(jnp.bfloat16)
         if not self.fast:
-            return lax.psum_scatter(part, self.every, scatter_dimension=0, tiled=True).astype(
-                jnp.float32
-            )
-        part = part.reshape(2, 2, 4, 2, part.shape[0] // 32, part.shape[1])
-        return reduce_stages(part, "xczy", order)
-
-    def scatter_ctx(self, part, order):
-        part = part.astype(jnp.bfloat16)
-        if not self.fast:
-            return lax.psum_scatter(part, self.ctx, scatter_dimension=0, tiled=True).astype(
-                jnp.float32
-            )
-        part = part.reshape(4, 2, part.shape[0] // 8, part.shape[1])
-        return reduce_stages(part, "zy", order)
-
-    def total(self, value, axes):
-        if not self.fast:
-            return lax.psum(value, axes)
-        for axis in axes:
-            count = 4 if axis == "z" else 2
-            value = value + sum(
-                lax.ppermute(value, axis, xor_perm(count, shift)) for shift in range(1, count)
-            )
-        return value
+            return Rows(lax.psum_scatter(part, self.ctx, scatter_dimension=0, tiled=True))
+        return RowSum(part.reshape(2, 2, 2, part.shape[0] // 8, part.shape[1]))
 
 
 def body(
@@ -406,20 +830,25 @@
         [vec_bias.T, ln_gain.T, ln_bias.T, up_bias.reshape(hidden, shard).T], 1
     )
     small = jnp.pad(small, ((0, 0), (0, 128 - small.shape[1])))
-    inputs_all = links.gather(jnp.concatenate([prompt_in[0], encoder[0]], 0), links.ctx)
-    inputs_all = inputs_all.reshape(ctx_count, prompt_rows + enc_rows, width)
-    prompt_all = inputs_all[:, :prompt_rows].reshape(prompt_len, width)
-    enc_all = inputs_all[:, prompt_rows:].reshape(enc_rows * ctx_count, width)
-    first = links.gather(jnp.concatenate([self_proj, small], 1), links.every)
-    second = links.gather(
-        jnp.concatenate([self_out, cross_query, cross_kv, cross_out], 1), links.every
-    )
-    w_up = links.gather(up_proj, links.every)
-    w_down = links.gather(down_proj, links.every)
-    w_q, w_kv = first[:, :width], first[:, width : 3 * width]
-    w_so, w_cq = second[:, :width], second[:, width : 2 * width]
-    w_ckv, w_co = second[:, 2 * width : 4 * width], second[:, 4 * width :]
-    small = first[:, 3 * width :].astype(f32).T
+    place = links.place()
+    rows_in = links.gather_rows([prompt_in[0], encoder[0]])
+    first = links.gather([self_proj, small], 13 * 128)
+    second = links.gather([self_out, cross_query, cross_kv, cross_out], 20 * 128)
+    up = links.gather([up_proj], 16 * 128)
+    tokens = jnp.concatenate([prompt_in[0], cont_in[0, 0]], 0)
+    tokens = begin(tokens, first, rows_in)
+    tokens = advance(tokens, first)
+    tokens = advance(tokens, first, rows_in)
+    tokens = begin(tokens, second)
+    tokens = advance(tokens, first)
+    tokens = advance(tokens, rows_in, second)
+    tokens = advance(tokens, first)
+    tokens, down_proj = begin((tokens, down_proj), up)
+    w_down = lax.all_gather(down_proj, links.every, axis=0, tiled=True)
+    tokens = advance(tokens, first)
+    self_w, small = first.finish(place)
+    w_q, w_kv = self_w[:, :width], self_w[:, width:]
+    small = small.astype(f32).T
     biases, gains, shifts = small[:7], small[7:10], small[10:13]
     hidden_bias = (
         small[13 : 13 + hidden]
@@ -431,8 +860,7 @@
     every_begin = cont_start[0]
     own_begin = lax.dynamic_index_in_dim(every_begin, block_index, 0, keepdims=False)
     scalars = jnp.stack([prompt_start[0], own_begin, block_index.astype(jnp.int32)])
-    cont_rows = cont_in[0, 0]
-    tokens = jnp.concatenate([prompt_in[0], cont_rows], 0)
+    cont_rows = tokens[prompt_rows:]
     row_total = tokens.shape[0]
     row_spot = jnp.arange(row_total, dtype=jnp.int32)
     valid_rows = jnp.where(
@@ -444,10 +872,17 @@
 
     kv_bias = jnp.concatenate([jnp.zeros((width,), f32), biases[1]])
     queries = ((product(tokens, w_q) + biases[0]) * scale).astype(bf16)
+    cont_kv = (product(cont_rows, w_kv) + kv_bias).astype(bf16)
+    (queries, cont_kv) = advance((queries, cont_kv), second, up)
+    queries = advance(queries, rows_in)
+    prompt_all, enc_all = rows_in.finish(place)
     prompt_kv = (product(prompt_all, w_kv) + kv_bias).astype(bf16)
-    cont_kv = (product(cont_rows, w_kv) + kv_bias).astype(bf16)
     plan = self_plan(prompt_rows, prompt_len, slot_len)
+    prompt_kv = advance(prompt_kv, second)
     attn, self_log = attend_forward(scalars, queries, [prompt_kv, cont_kv], plan, prompt_rows)
+    attn = advance(attn, second, up)
+    attn = advance(attn, second)
+    w_so, w_cq, w_ckv, w_co = second.finish(place)
     branch_self = product(attn, w_so) + biases[2]
     resid_one = tokens.astype(f32) + branch_self
     hidden_one = layer_norm(resid_one, gains[0], shifts[0]).astype(bf16)
@@ -456,9 +891,12 @@
     enc_kv = (product(enc_all, w_ckv) + enc_bias).astype(bf16)
     cross_queries = ((product(hidden_one, w_cq) + biases[3]) * scale).astype(bf16)
     enc_len = enc_all.shape[0]
+    cross_queries = advance(cross_queries, up)
     cross_attn, cross_log = attend_forward(
         None, cross_queries, [enc_kv], cross_plan(row_total, enc_len, 320), 0
     )
+    cross_attn = advance(cross_attn, up)
+    (w_up,) = up.finish(place)
     branch_cross = product(cross_attn, w_co) + biases[5]
     resid_two = hidden_one.astype(f32) + branch_cross
     hidden_two = layer_norm(resid_two, gains[1], shifts[1]).astype(bf16)
@@ -473,22 +911,35 @@
 
     members = (tokens, branch_self, hidden_one, branch_cross, hidden_two, branch_ffn)
     squares = jnp.stack(
-        [jnp.sum(valid_rows * jnp.square(member.astype(f32))) for member in members]
-    )
-    squares = links.total(jnp.pad(squares[None], ((0, 7), (0, 122))), links.ctx)[0, :6]
-    statistics = (squares / (valid_count * width))[None]
-
+        [jnp.sum(valid_rows * jnp.square(member.astype(f32)), 0) for member in members]
+    )
     grad_out = jnp.concatenate([prompt_cot[0], cont_cot[0, 0]], 0).astype(f32)
     grad_three, gain_three, shift_three = layer_norm_back(resid_three, gains[2], grad_out)
     grad_ffn = grad_three.astype(bf16)
-    down_total = links.scatter(product_tn(act, grad_ffn), "cxyz")
-    grad_pre = (product_nt(grad_ffn, w_down) * slope.astype(f32)).astype(bf16)
-    up_total = links.scatter(product_tn(hidden_two, grad_pre), "cyxz")
-    grad_hidden_two = grad_three + product_nt(grad_pre, w_up)
+    half_width = width // 2
+    if links.fast:
+        core = lax.axis_index("c").astype(jnp.int32).reshape(1)
+        down_other, down_mine, up_other, up_mine, up_bias_part, back_ffn = ffn_backward(
+            core, grad_ffn, hidden_two, act, slope, w_down, w_up
+        )
+
+        def add_to(mine):
+            return lambda came: (mine.astype(f32) + came[0].astype(f32)).astype(bf16)[None]
+
+        down_sum = WeightSum(down_other[None], add_to(down_mine))
+        up_sum = WeightSum(up_other[None], add_to(up_mine))
+    else:
+        grad_pre = (product_nt(grad_ffn, w_down) * slope.astype(f32)).astype(bf16)
+        down_sum = links.weight_sum([[(act, grad_ffn)]])
+        up_sum = links.weight_sum([[(hidden_two, grad_pre)]])
+        up_bias_part = column_sum(grad_pre)
+        back_ffn = product_nt(grad_pre, w_up)
+    back_ffn = begin(back_ffn, down_sum, up_sum)
+    grad_hidden_two = grad_three + back_ffn
     grad_two, gain_two, shift_two = layer_norm_back(resid_two, gains[1], grad_hidden_two)
     grad_cross = grad_two.astype(bf16)
-    co_total = links.scatter(product_tn(cross_attn, grad_cross), "czxy")
     grad_cattn = product_nt(grad_cross, w_co).astype(bf16)
+    grad_cattn = advance(grad_cattn, down_sum)
     cross_gq, cross_gk, cross_gv = attend_backward(
         None,
         cross_queries,
@@ -499,61 +950,34 @@
         cross_plan(row_total, enc_len, 384),
         0,
         512,
-    )
+        (0,),
+    )
+    cross_gq = advance(cross_gq, down_sum, up_sum)
     grad_cq = (cross_gq.astype(f32) * scale).astype(bf16)
-    enc_gkv = jnp.concatenate([cross_gk[0], cross_gv[0]], 1)
-    cq_total = links.scatter(product_tn(hidden_one, grad_cq), "cxyz")
-    ckv_total = links.scatter(product_tn(enc_all, enc_gkv), "cyxz")
-    encoder_grad = links.scatter_ctx(product_nt(enc_gkv, w_ckv), "zy")[None]
+    enc_back = product_nt(cross_gk[0], w_ckv[:, :width]) + product_nt(
+        cross_gv[0], w_ckv[:, width:]
+    )
+    enc_sum = links.row_sum(enc_back)
+    grad_cq = begin(grad_cq, enc_sum)
     grad_hidden_one = grad_two + product_nt(grad_cq, w_cq)
     grad_one, gain_one, shift_one = layer_norm_back(resid_one, gains[0], grad_hidden_one)
     grad_self = grad_one.astype(bf16)
-    so_total = links.scatter(product_tn(attn, grad_self), "cxyz")
+    mid_sum = links.weight_sum(
+        [
+            [(cross_attn, grad_cross)],
+            [(hidden_one, grad_cq)],
+            [(attn, grad_self)],
+            [(enc_all, cross_gk[0])],
+            [(enc_all, cross_gv[0])],
+        ]
+    )
+    grad_self = begin(grad_self, mid_sum)
     grad_attn = product_nt(grad_self, w_so).astype(bf16)
-    self_gq, self_gk, self_gv = attend_backward(
-        scalars,
-        queries,
-        grad_attn,
-        attn,
-        self_log,
-        [prompt_kv, cont_kv],
-        plan,
-        prompt_rows,
-        1024,
-    )
-    grad_q = (self_gq.astype(f32) * scale).astype(bf16)
-    prompt_gkv = jnp.concatenate([self_gk[0], self_gv[0]], 1)
-    cont_gkv = jnp.concatenate([self_gk[1], self_gv[1]], 1)
-    prompt_back = product_nt(prompt_gkv, w_kv)
-    half_width = width // 2
-    prompt_back = jnp.concatenate(
-        [
-            links.scatter_ctx(prompt_back[:, :half_width], "yz"),
-            links.scatter_ctx(prompt_back[:, half_width:], "zy"),
-        ],
-        1,
-    )
-    sin_q = product_tn(tokens, grad_q)
-    sin_kv = product_tn(prompt_all, prompt_gkv) + product_tn(cont_rows, cont_gkv)
-    sin_total = jnp.concatenate(
-        [
-            links.scatter(sin_q, "cxyz"),
-            links.scatter(sin_kv[:, :width], "cyxz"),
-            links.scatter(sin_kv[:, width:], "czxy"),
-        ],
-        1,
-    )
-    input_grad = grad_one + product_nt(grad_q, w_q)
-    prompt_grad = (input_grad[:prompt_rows] + prompt_back)[None]
-    cont_grad = (input_grad[prompt_rows:] + product_nt(cont_gkv, w_kv))[None, None]
-
-    up_bias_part = column_sum(grad_pre).reshape(width // shard, hidden, shard)
     small_part = jnp.concatenate(
         [
+            squares,
             jnp.stack(
                 [
-                    column_sum(grad_q),
-                    column_sum(self_gv[0]) + column_sum(self_gv[1]),
                     column_sum(grad_self),
                     column_sum(grad_cq),
                     column_sum(cross_gv[0]),
@@ -567,15 +991,62 @@
                     shift_three,
                 ]
             ),
-            up_bias_part.transpose(1, 0, 2).reshape(hidden, width),
+            up_bias_part.reshape(width // shard, hidden, shard)
+            .transpose(1, 0, 2)
+            .reshape(hidden, width),
         ],
         0,
     )
-    small_total = links.total(small_part, links.every)
+    grad_attn, small_part = lax.optimization_barrier((grad_attn, small_part))
+    grad_attn = advance(grad_attn, down_sum, up_sum)
+    grad_attn = advance(grad_attn, mid_sum)
+    self_args = (queries, grad_attn, attn, self_log, [prompt_kv, cont_kv], plan, prompt_rows)
+    part_gq, prompt_gk, prompt_gv = attend_backward(scalars, *self_args, 1024, (0,))
+    prompt_gk, prompt_gv = prompt_gk[0], prompt_gv[0]
+    w_k, w_v = w_kv[:, :width], w_kv[:, width:]
+    part_gq = advance(part_gq, up_sum, mid_sum, enc_sum, down_sum)
+    prompt_sum = links.row_sum(product_nt(prompt_gk, w_k) + product_nt(prompt_gv, w_v))
+    part_gq = begin(part_gq, prompt_sum)
+    self_gq, cont_gk, cont_gv = attend_backward(scalars, *self_args, 512, (1,), part_gq)
+    cont_gk, cont_gv = cont_gk[0], cont_gv[0]
+    self_gq = advance(self_gq, down_sum, up_sum, mid_sum, prompt_sum, enc_sum)
+    grad_q = (self_gq.astype(f32) * scale).astype(bf16)
+
+    last_part = jnp.stack([column_sum(grad_q), column_sum(prompt_gv) + column_sum(cont_gv)])
+    small_part = jnp.concatenate(
+        [small_part, last_part, jnp.zeros((32 - small_part.shape[0] - 2, width), f32)], 0
+    )
+    small_all = lax.all_gather(small_part, links.every, axis=0, tiled=True)
+    self_sum = links.weight_sum(
+        [
+            [(tokens, grad_q)],
+            [(prompt_all, prompt_gk), (cont_rows, cont_gk)],
+            [(prompt_all, prompt_gv), (cont_rows, cont_gv)],
+        ]
+    )
+    grad_q = begin(grad_q, self_sum)
+    input_grad = grad_one + product_nt(grad_q, w_q)
+    cont_grad = input_grad[prompt_rows:] + product_nt(cont_gk, w_k) + product_nt(cont_gv, w_v)
+    cont_grad = advance(cont_grad, self_sum)
+    cont_grad = advance(cont_grad, mid_sum, prompt_sum)
+    cont_grad = advance(cont_grad, self_sum, up_sum)
+    cont_grad = advance(cont_grad, self_sum)
+    cont_grad = advance(cont_grad, self_sum, mid_sum, prompt_sum, enc_sum)[None, None]
+    prompt_grad = (input_grad[:prompt_rows] + prompt_sum.finish())[None]
+    encoder_grad = enc_sum.finish()[None]
+    up_total, down_total = up_sum.finish()[0], down_sum.finish()[0]
+    co_total, cq_total, so_total, ck_total, cv_total = mid_sum.finish()
+    ckv_total = jnp.concatenate([ck_total, cv_total], 1)
+    sin_total = jnp.concatenate([*self_sum.finish()], 1)
+    small_all = small_all.reshape(-1, ctx_count, 32, width)
+    group = lax.axis_index(links.rows)
+    squares = jnp.sum(lax.dynamic_index_in_dim(small_all, group, 0, keepdims=False)[:, :6], (0, 2))
+    statistics = (squares / (valid_count * width))[None]
     at = lax.axis_index(links.every) * shard
-    small_total = lax.dynamic_slice_in_dim(small_total, at, shard, 1)
-    bias_total, gain_total, shift_total = small_total[:7], small_total[7:10], small_total[10:13]
-    up_bias_total = small_total[13 : 13 + hidden].reshape(hidden * shard)
+    sums = jnp.sum(lax.dynamic_slice_in_dim(small_all, at, shard, 3), (0, 1))
+    bias_total = jnp.concatenate([sums[21:23], sums[6:11]])
+    gain_total, shift_total = sums[11:14], sums[14:17]
+    up_bias_total = sums[17 : 17 + hidden].reshape(hidden * shard)
     return (
         output[:prompt_rows][None],
         output[prompt_rows:][None, None],

time: 1040 us -> 748 us (0.72)
  waiting for transfers between devices: 520 us -> 198 us
  Pallas kernels: 109 us -> 213 us
  matrix products: 151 us -> 82.3 us
  other arithmetic: 52.4 us -> 93.7 us
  starting transfers between devices: 99.5 us -> 71.4 us
  local copies, waits for them, and re-layouts: 80.8 us -> 66.8 us
    all_gather x5 -> x2, waiting for transfers between devices: 284 us -> 0.01 us  [the longest x1 0.01 us: body(): w_down = lax.all_gather(down_proj, links.every, axis=0, tiled=True)]
    pallas_call x0 -> x9, Pallas kernels: none -> 98.2 us  [the longest x4 39.5 us: half_products(): pl.pallas_call(functools.partial(half_products_kernel, tuple((len(pairs)...]
    dot_general x9 -> x0, matrix products: 47.3 us -> none  [product_tn(): lax.dot_general(first_mat, second_mat, (((0,), (0,)), ((), ())), preferre...]
    ppermute x76 -> x61, waiting for transfers between devices: 234 us -> 198 us  [swap(): return lax.ppermute(value, axis, SWAP)]
    dynamic_slice x18 -> x12, local copies, waits for them, and re-layouts: 39.5 us -> 8.61 us  [the longest x8 5.69 us: pick(): return lax.dynamic_index_in_dim(self.sides[side], here, dim, keepdims=False)]
    ppermute x76 -> x61, starting transfers between devices: 99.3 us -> 70.8 us  [swap(): return lax.ppermute(value, axis, SWAP)]
    another operation x0 -> x23, other arithmetic: none -> 21.6 us  [the longest x15 16.6 us: add(): self.sides = [jnp.stack(pair) for pair in zip(self.sides, coming)]]
    dot_general x9 -> x10, matrix products: 52.7 us -> 31.1 us  [product_nt(): lax.dot_general(first_mat, second_mat, (((1,), (1,)), ((), ())), preferre...]
  transfers between devices with their start and end apart: 81 -> 63, of which waited for: 39 -> 28; matrix products, arithmetic and copies ran while one was open for 24% -> 22% of each run, Pallas kernels for 11% -> 22%
where the time goes in v2:
time: 748 us; the launch traced here: 743 us
  Pallas kernels  213 us (28%)
  waiting for transfers between devices  198 us (26%)
  other arithmetic  93.7 us (13%)
  matrix products  82.3 us (11%)
  starting transfers between devices  71.4 us (10%)
  local copies, waits for them, and re-layouts  66.8 us (9%)
  between operations  17.7 us (2%)
    ppermute x61, waiting for transfers between devices, swap(): return lax.ppermute(value, axis, SWAP)  198 us
    pallas_call x3, Pallas kernels, attend_backward(): pl.pallas_call(functools.partial(bwd_kernel, plan, masked, slot_at, key_s...  74.8 us
    ppermute x61, starting transfers between devices, swap(): return lax.ppermute(value, axis, SWAP)  70.8 us
    dot_general x9, matrix products, product(): return jnp.dot(first_mat, second_mat, preferred_element_type=jnp.float32)  51.1 us
    pallas_call x2, Pallas kernels, attend_forward(): pl.pallas_call(functools.partial(fwd_kernel, plan, masked, slot_at), grid...  40.4 us
    pallas_call x4, Pallas kernels, half_products(): pl.pallas_call(functools.partial(half_products_kernel, tuple((len(pairs)...  39.5 us
    pallas_call x1, Pallas kernels, ffn_backward(): pl.pallas_call(ffn_backward_kernel, grid_spec=pltpu.PrefetchScalarGridSpe...  33.6 us
    dot_general x10, matrix products, product_nt(): lax.dot_general(first_mat, second_mat, (((1,), (1,)), ((), ())), preferre...  31.1 us
  transfers between devices with their start and end apart: 63, of which 28 were waited for; matrix products, arithmetic and copies ran while one was open for 22% of the time, Pallas kernels for 22%

profile of v2, /device:TPU:0, one launch (start us, length us, event | category | flops | bytes accessed | tf_op | source)
XLA Modules:
  0.0 743.2 jit_solution(17228025204848472510)
XLA Ops:
  9.5 4.1 collective-permute-start
  13.7 18.6 %collective-permute-done = bf16[32,3200]{1,0:T(8,128)(2,1)S(1)} collective-permute-done((bf16[32,3200]{1,0:T(8,128)(2,1)S(1)}, bf16[32,3200]{1,0:T(8,128)(2,1)S(1)}, u32[]{:S(2)}, u32[]{:S(2)}) %collective-permute-start) | collective-permute-done | bytes 204832 | tf_op jit(solution)/shard_map/ppermute | solution.py:465
  32.6 7.5 %collective-permute-done.2 = bf16[192,1024]{1,0:T(8,128)(2,1)S(1)} collective-permute-done((bf16[192,1024]{1,0:T(8,128)(2,1)S(1)}, bf16[192,1024]{1,0:T(8,128)(2,1)S(1)}, u32[]{:S(2)}, u32[]{:S(2)}) %collective-permute-start.2) | collective-permute-done | bytes 393248 | tf_op jit(solution)/shard_map/ppermute | solution.py:465
  40.1 8.7 %collective-permute-done.1 = bf16[2,32,3200]{2,1,0:T(8,128)(2,1)S(1)} collective-permute-done((bf16[2,32,3200]{2,1,0:T(8,128)(2,1)S(1)}, bf16[2,32,3200]{2,1,0:T(8,128)(2,1)S(1)}, u32[]{:S(2)}, u32[]{:S(2)}) %collective-permute-start.1) | collective-permute-done | bytes 409632 | tf_op jit(solution)/shard_map/ppermute | solution.py:465
  52.2 4.1 collective-permute-start.6
  56.3 5.1 collective-permute-done.4
  64.1 11.7 %collective-permute-done.6 = bf16[32,5120]{1,0:T(8,128)(2,1)S(1)} collective-permute-done((bf16[32,5120]{1,0:T(8,128)(2,1)S(1)}, bf16[32,5120]{1,0:T(8,128)(2,1)S(1)}, u32[]{:S(2)}, u32[]{:S(2)}) %collective-permute-start.6) | collective-permute-done | bytes 327712 | tf_op jit(solution)/shard_map/ppermute | solution.py:465
  87.1 3.6 collective-permute-start.12
  91.3 6.8 assemble.3
  98.2 3.5 slice_reduce_fusion.1
  106.8 4.4 collective-permute-done.11
  114.4 12.4 %collective-permute-done.13 = bf16[2,2,192,1024]{3,2,1,0:T(8,128)(2,1)} collective-permute-done((bf16[2,2,192,1024]{3,2,1,0:T(8,128)(2,1)}, bf16[2,2,192,1024]{3,2,1,0:T(8,128)(2,1)}, u32[]{:S(2)}, u32[]{:S(2)}) %collective-permute-start.13) | collective-permute-done | bytes 1572896 | tf_op jit(solution)/shard_map/ppermute | solution.py:465
  134.2 6.1 add_convert_fusion.refs_2_.refs_4_.refs_5_.refs_6_
  140.3 15.0 %collective-permute-done.14 = bf16[2,2,32,2560]{3,2,1,0:T(8,128)(2,1)S(1)} collective-permute-done((bf16[2,2,32,2560]{3,2,1,0:T(8,128)(2,1)S(1)}, bf16[2,2,32,2560]{3,2,1,0:T(8,128)(2,1)S(1)}, u32[]{:S(2)}, u32[]{:S(2)}) %collective-permute-start.14) | collective-permute-done | bytes 655392 | tf_op jit(solution)/shard_map/ppermute | solution.py:465
  167.4 29.4 %attend_forward.2 = (bf16[640,1024]{1,0:T(8,128)(2,1)S(1)}, f32[640,128]{1,0:T(8,128)S(1)}) custom-call(s32[3]{0:T(128)S(1)} %pad_add_fusion.refs_0_, bf16[640,1024]{1,0:T(8,128)(2,1)S(1)} %copy-done.18, bf16[1024,2048]{1,0:T(8,128)(2,1)} %add_convert_fusion.refs_2_.refs_4_.refs_5_.refs_6_, bf16[512,2048]{1,0:T(8,128)(2,1)S(1)} %add_convert_fusion.3.refs_3_.refs_5_.refs_6_, ...), custom_call_target="tpu_custom_call" | custom-call | flops 1 | bytes 1 | tf_op jit(solution)/shard_map/attend_forward/pallas_call | solution.py:227
  204.5 5.2 collective-permute-done.19.left_came
  211.3 8.2 %assemble.4 = (bf16[1024,1024]{1,0:T(8,128)(2,1)S(1)}, bf16[1024,1024]{1,0:T(8,128)(2,1)S(1)}, bf16[1024,2048]{1,0:T(8,128)(2,1)}, bf16[1024,1024]{1,0:T(8,128)(2,1)}) custom-call(s32[5]{0:T(128)S(1)} %stack.333.place_ref, bf16[2,2,2,2,32,2560]{5,4,3,2,1,0:T(8,128)(2,1)} %copy-done.50, bf16[2,2,2,2,32,2560]{5,4,3,2,1,0:T(8,128)(2,1)} %copy-done.49, ...), custom_call_target="tpu_custom_call" | custom-call | bytes 20971520 | tf_op jit(solution)/shard_map/assemble/pallas_call | solution.py:660
  233.2 11.0 %attend_forward.3 = (bf16[640,1024]{1,0:T(8,128)(2,1)S(1)}, f32[640,128]{1,0:T(8,128)S(1)}) custom-call(bf16[640,1024]{1,0:T(8,128)(2,1)S(1)} %multiply_convert_fusion.3.refs_0_, bf16[512,2048]{1,0:T(8,128)(2,1)S(1)} %add_convert_fusion.2.refs_1_.refs_2_.refs_4_.refs_5_, bf16[512,2048]{1,0:T(8,128)(2,1)S(1)} %add_convert_fusion.2.refs_1_.refs_2_.refs_4_.refs_5_), custom_call_target="tpu_custom_call" | custom-call | flops 1 | bytes 1 | tf_op jit(solution)/shard_map/attend_forward/pallas_call | solution.py:227
  244.2 9.7 %collective-permute-done.23 = bf16[2,2,2,32,2048]{4,3,2,1,0:T(8,128)(2,1)S(1)} collective-permute-done((bf16[2,2,2,32,2048]{4,3,2,1,0:T(8,128)(2,1)S(1)}, bf16[2,2,2,32,2048]{4,3,2,1,0:T(8,128)(2,1)S(1)}, u32[]{:S(2)}, u32[]{:S(2)}) %collective-permute-start.23) | collective-permute-done | bytes 1048608 | tf_op jit(solution)/shard_map/ppermute | solution.py:465
  260.9 5.1 fusion.110
  267.6 8.0 %assemble.5.up_ref = bf16[1024,4096]{1,0:T(8,128)(2,1)} custom-call(s32[5]{0:T(128)S(1)} %stack.333.place_ref, bf16[2,2,2,2,32,2048]{5,4,3,2,1,0:T(8,128)(2,1)} %pad_maximum_fusion.3.left_own, bf16[2,2,2,2,32,2048]{5,4,3,2,1,0:T(8,128)(2,1)} %pad_maximum_fusion.4.right_own, bf16[2,2,2,2,32,2048]{5,4,3,2,1,0:T(8,128)(2,1)} %collective-permute-done.25.left_came, ...), custom_call_target="tpu_custom_call" | custom-call | bytes 16777216 | tf_op jit(solution)/shard_map/assemble/pallas_call | solution.py:660
  275.6 13.9 %fusion.4 = (bf16[640,4096]{1,0:T(8,128)(2,1)}, bf16[640,4096]{1,0:T(8,128)(2,1)}) fusion(f32[4096]{0:T(1024)S(1)} %add.481, bf16[640,1024]{1,0:T(8,128)(2,1)S(1)} %add_convert_fusion.5.h_ref, bf16[1024,4096]{1,0:T(8,128)(2,1)} %assemble.5.up_ref), kind=kOutput, calls=%fused_computation.5 | convolution fusion | flops 5400166400 | bytes 20201472 | tf_op jit(solution)/shard_map/dot_general | solution.py:18
  289.4 14.1 %multiply_reduce_fusion.2 = (f32[1024]{0:T(1024)}, f32[1024]{0:T(1024)}, f32[1024]{0:T(1024)}, f32[1024]{0:T(1024)}, f32[1024]{0:T(1024)}, /*index=5*/f32[1024]{0:T(1024)}, f32[640]{0:T(1024)S(1)}, f32[640,1024]{1,0:T(8,128)S(1)}) fusion(f32[640]{0:T(1024)S(1)} %fusion.102, f32[1024]{0:T(1024)S(1)} %get-tuple-element.439, ...), kind=kOutput, calls=%fused_computation.57 | convolution fusion | flops 5385741824 | bytes 25469952 | tf_op jit(solution)/shard_map/dot_general | solution.py:18
  308.9 33.6 %ffn_backward.1 = (bf16[2048,1024]{1,0:T(8,128)(2,1)}, bf16[2048,1024]{1,0:T(8,128)(2,1)}, bf16[512,4096]{1,0:T(8,128)(2,1)}, bf16[512,4096]{1,0:T(8,128)(2,1)},...) custom-call(s32[1]{0:T(128)} %bitcast.30.core_ref, bf16[640,1024]{1,0:T(8,128)(2,1)S(1)} %get-tuple-element.457.g_ref, ...), custom_call_target="tpu_custom_call" | custom-call | flops 1 | bytes 1 | tf_op jit(solution)/shard_map/ffn_backward/pallas_call | solution.py:365
  344.6 7.8 %multiply_reduce_fusion = (f32[1024]{0:T(1024)}, f32[640]{0:T(1024)S(1)}, f32[640]{0:T(1024)S(1)}, f32[1024]{0:T(1024)}, f32[640,1024]{1,0:T(8,128)S(1)}, /*index=5*/bf16[640,1024]{1,0:T(8,128)(2,1)}) fusion(f32[640,1024]{1,0:T(8,128)} %copy-done.41, f32[640]{0:T(1024)S(1)} %add_rsqrt_fusion.1, f32[640]{0:T(1024)S(1)} %broadcast_multiply_fusion.7, ...), kind=kLoop, calls=%fused_computation.51 | loop fusion | flops 15725312 | bytes 13148160 | tf_op jit(solution)/shard_map/reduce_sum | solution.py:458
  358.1 4.3 fusion.6
  373.9 21.6 %attend_backward.3 = (bf16[640,1024]{1,0:T(8,128)(2,1)S(1)}, bf16[512,1024]{1,0:T(8,128)(2,1)S(1)}, bf16[512,1024]{1,0:T(8,128)(2,1)S(1)}) custom-call(bf16[640,1024]{1,0:T(8,128)(2,1)S(1)} %copy-done.27, bf16[640,1024]{1,0:T(8,128)(2,1)S(1)} %copy-done.31, bf16[640,1024]{1,0:T(8,128)(2,1)} %copy-done.10, f32[8,2,640]{2,1,0:T(2,128)S(1)} %reshape.384.refs_3_, ...), custom_call_target="tpu_custom_call" | custom-call | flops 1 | bytes 1 | tf_op jit(solution)/shard_map/attend_backward/pallas_call | solution.py:272
  399.8 3.7 fusion.5
  420.9 8.7 %half_products.4 = bf16[5,512,1024]{2,1,0:T(8,128)(2,1)} custom-call(s32[1]{0:T(128)S(6)} %sub.98.core_ref, bf16[640,1024]{1,0:T(8,128)(2,1)S(1)} %copy-done.11, bf16[640,1024]{1,0:T(8,128)(2,1)S(1)} %copy-done.14, bf16[640,1024]{1,0:T(8,128)(2,1)} %copy-done.48, bf16[640,1024]{1,0:T(8,128)(2,1)} %copy-done.45, bf16[640,1024]{1,0:T(8,128)(2,1)} %copy-done.3, ...), custom_call_target="tpu_custom_call" | custom-call | flops 1 | bytes 1 | tf_op jit(solution)/shard_map/half_products/pallas_call | solution.py:425
  446.2 3.7 convolution_convert_fusion.refs_2_
  449.9 16.8 %collective-permute-done.31 = bf16[1,2,2,128,512]{4,3,1,2,0:T(8,128)(2,1)} collective-permute-done((bf16[1,2,2,128,512]{4,3,1,2,0:T(8,128)(2,1)}, bf16[1,2,2,128,512]{4,3,1,2,0:T(8,128)(2,1)}, u32[]{:S(2)}, u32[]{:S(2)}) %collective-permute-start.31) | collective-permute-done | bytes 524320 | tf_op jit(solution)/shard_map/ppermute | solution.py:465
  479.6 10.2 %half_products.5 = bf16[5,512,1024]{2,1,0:T(8,128)(2,1)} custom-call(s32[1]{0:T(128)} %bitcast.30.core_ref, bf16[640,1024]{1,0:T(8,128)(2,1)S(1)} %copy-done.12, bf16[640,1024]{1,0:T(8,128)(2,1)S(1)} %copy-done.15, bf16[640,1024]{1,0:T(8,128)(2,1)} %copy-done.48, bf16[640,1024]{1,0:T(8,128)(2,1)} %copy-done.45, bf16[640,1024]{1,0:T(8,128)(2,1)} %copy-done.3, ...), custom_call_target="tpu_custom_call" | custom-call | flops 1 | bytes 1 | tf_op jit(solution)/shard_map/half_products/pallas_call | solution.py:425
  497.2 35.5 %attend_backward.4 = (f32[640,1024]{1,0:T(8,128)}, bf16[1024,1024]{1,0:T(8,128)(2,1)S(1)}, bf16[1024,1024]{1,0:T(8,128)(2,1)}) custom-call(s32[3]{0:T(128)S(1)} %copy-done.34, bf16[640,1024]{1,0:T(8,128)(2,1)S(1)} %copy-done.19, bf16[640,1024]{1,0:T(8,128)(2,1)S(1)} %convolution_convert_fusion.refs_2_, bf16[640,1024]{1,0:T(8,128)(2,1)S(1)} %copy-done.4, ...), custom_call_target="tpu_custom_call" | custom-call | flops 1 | bytes 1 | tf_op jit(solution)/shard_map/attend_backward/pallas_call | solution.py:272
  532.7 4.8 fusion.42
  537.9 4.0 add_convert_fusion.1
  543.2 6.8 collective-permute-done.41
  569.3 7.0 collective-permute-done.42
  577.1 17.7 %attend_backward.5 = (bf16[640,1024]{1,0:T(8,128)(2,1)S(1)}, bf16[512,1024]{1,0:T(8,128)(2,1)S(1)}, bf16[512,1024]{1,0:T(8,128)(2,1)S(1)}) custom-call(s32[3]{0:T(128)S(1)} %copy-done.34, bf16[640,1024]{1,0:T(8,128)(2,1)S(1)} %copy-done.19, bf16[640,1024]{1,0:T(8,128)(2,1)S(1)} %convolution_convert_fusion.refs_2_, bf16[640,1024]{1,0:T(8,128)(2,1)} %copy-done.3, ...), custom_call_target="tpu_custom_call" | custom-call | flops 1 | bytes 1 | tf_op jit(solution)/shard_map/attend_backward/pallas_call | solution.py:272
  594.9 3.4 collective-permute-done.44
  606.8 10.0 %half_products.6 = bf16[3,512,1024]{2,1,0:T(8,128)(2,1)} custom-call(s32[1]{0:T(128)S(6)} %sub.98.core_ref, bf16[640,1024]{1,0:T(8,128)(2,1)S(1)} %copy-done.7, bf16[640,1024]{1,0:T(8,128)(2,1)S(1)} %get-tuple-element.387.refs_1_, bf16[1024,1024]{1,0:T(8,128)(2,1)} %copy-done.1, bf16[1024,1024]{1,0:T(8,128)(2,1)} %copy-done.23, ...), custom_call_target="tpu_custom_call" | custom-call | flops 1 | bytes 1 | tf_op jit(solution)/shard_map/half_products/pallas_call | solution.py:425
  629.8 4.3 fusion.27
  634.2 10.7 %half_products.7 = bf16[3,512,1024]{2,1,0:T(8,128)(2,1)} custom-call(s32[1]{0:T(128)} %bitcast.30.core_ref, bf16[640,1024]{1,0:T(8,128)(2,1)S(1)} %copy-done.7, bf16[640,1024]{1,0:T(8,128)(2,1)S(1)} %copy-done.17, bf16[1024,1024]{1,0:T(8,128)(2,1)} %copy-done.1, bf16[1024,1024]{1,0:T(8,128)(2,1)} %copy-done.23, ...), custom_call_target="tpu_custom_call" | custom-call | flops 1 | bytes 1 | tf_op jit(solution)/shard_map/half_products/pallas_call | solution.py:425
  650.6 3.7 collective-permute-start.53
  654.3 12.7 %collective-permute-done.50 = bf16[2,128,1024]{2,1,0:T(8,128)(2,1)S(1)} collective-permute-done((bf16[2,128,1024]{2,1,0:T(8,128)(2,1)S(1)}, bf16[2,128,1024]{2,1,0:T(8,128)(2,1)S(1)}, u32[]{:S(2)}, u32[]{:S(2)}) %collective-permute-start.50) | collective-permute-done | bytes 524320 | tf_op jit(solution)/shard_map/ppermute | solution.py:465
  680.8 8.7 %collective-permute-done.54 = bf16[3,2,2,32,512]{4,3,0,1,2:T(8,128)(2,1)S(1)} collective-permute-done((bf16[3,2,2,32,512]{4,3,0,1,2:T(8,128)(2,1)S(1)}, bf16[3,2,2,32,512]{4,3,0,1,2:T(8,128)(2,1)S(1)}, u32[]{:S(2)}, u32[]{:S(2)}) %collective-permute-start.54) | collective-permute-done | bytes 393248 | tf_op jit(solution)/shard_map/ppermute | solution.py:465
  691.1 12.7 %collective-permute-done.59 = bf16[64,1024]{1,0:T(8,128)(2,1)S(1)} collective-permute-done((bf16[64,1024]{1,0:T(8,128)(2,1)S(1)}, bf16[64,1024]{1,0:T(8,128)(2,1)S(1)}, u32[]{:S(2)}, u32[]{:S(2)}) %collective-permute-start.59) | collective-permute-done | bytes 131104 | tf_op jit(solution)/shard_map/ppermute | solution.py:465
  703.8 14.5 %collective-permute-done.58 = bf16[128,1024]{1,0:T(8,128)(2,1)S(1)} collective-permute-done((bf16[128,1024]{1,0:T(8,128)(2,1)S(1)}, bf16[128,1024]{1,0:T(8,128)(2,1)S(1)}, u32[]{:S(2)}, u32[]{:S(2)}) %collective-permute-start.58) | collective-permute-done | bytes 262176 | tf_op jit(solution)/shard_map/ppermute | solution.py:465
  723.8 6.4 collective-permute-done.60
  (536 shorter events, 236.1 us)
Async XLA Ops:
  7.3 282.2 %all-gather.3.cloned.1.call-start = ((), (), s32[]{:S(2)}) async-start(), calls=%async_computation | async-start | bytes 8650752 | tf_op jit(solution)/shard_map/all_gather | solution.py:847
  9.5 22.8 %collective-permute-start = (bf16[32,3200]{1,0:T(8,128)(2,1)S(1)}, bf16[32,3200]{1,0:T(8,128)(2,1)S(1)}, u32[]{:S(2)}, u32[]{:S(2)}) collective-permute-start(bf16[32,3200]{1,0:T(8,128)(2,1)S(1)} %pad_maximum_fusion.30), channel_id=1, source_target_pairs={{0,4},{4,0},{1,5},{5,1},{2,6},{6,2},{3,7},{7,3},{8,12},{12,8},{9,1... | collective-permute-start | bytes 614408 | tf_op jit(solution)/shard_map/ppermute | solution.py:465
  13.6 26.4 %collective-permute-start.2 = (bf16[192,1024]{1,0:T(8,128)(2,1)S(1)}, bf16[192,1024]{1,0:T(8,128)(2,1)S(1)}, u32[]{:S(2)}, u32[]{:S(2)}) collective-permute-start(bf16[192,1024]{1,0:T(8,128)(2,1)S(1)} %pad_maximum_fusion.25), channel_id=1, source_target_pairs={{0,4},{4,0},{1,5},{5,1},{2,6},{6,2},{3,7},{7,3},{8,12},{12,8},{9,1... | collective-permute-start | bytes 1179656 | tf_op jit(solution)/shard_map/ppermute | solution.py:465
  52.1 25.9 %collective-permute-start.5 = (bf16[2,192,1024]{2,1,0:T(8,128)(2,1)S(1)}, bf16[2,192,1024]{2,1,0:T(8,128)(2,1)S(1)}, u32[]{:S(2)}, u32[]{:S(2)}) collective-permute-start(bf16[2,192,1024]{2,1,0:T(8,128)(2,1)S(1)} %pad_maximum_fusion.15), channel_id=1, source_target_pairs={{0,2},{2,0},{1,3},{3,1},{4,6},{6,4},{5,7},{7,5},{8,10},{10,8},{9,1... | collective-permute-start | bytes 2359304 | tf_op jit(solution)/shard_map/ppermute | solution.py:465
  52.2 23.7 %collective-permute-start.6 = (bf16[32,5120]{1,0:T(8,128)(2,1)S(1)}, bf16[32,5120]{1,0:T(8,128)(2,1)S(1)}, u32[]{:S(2)}, u32[]{:S(2)}) collective-permute-start(bf16[32,5120]{1,0:T(8,128)(2,1)S(1)} %pad_maximum_fusion.28), channel_id=1, source_target_pairs={{0,4},{4,0},{1,5},{5,1},{2,6},{6,2},{3,7},{7,3},{8,12},{12,8},{9,1... | collective-permute-start | bytes 983048 | tf_op jit(solution)/shard_map/ppermute | solution.py:465
  61.5 19.8 %collective-permute-start.7 = (bf16[2,2,2,32,1664]{4,3,2,1,0:T(8,128)(2,1)S(1)}, bf16[2,2,2,32,1664]{4,3,2,1,0:T(8,128)(2,1)S(1)}, u32[]{:S(2)}, u32[]{:S(2)}) collective-permute-start(bf16[2,2,2,32,1664]{4,3,2,1,0:T(8,128)(2,1)S(1)} %pad_maximum_fusion.14), channel_id=1, source_target_pairs={{0,16},{16,0},{1,17},{17,1},{2,18},{18,2},{3,19},{19,3},{4,20},{20... | collective-permute-start | bytes 2555912 | tf_op jit(solution)/shard_map/ppermute | solution.py:465
  63.1 18.0 %collective-permute-start.8 = (bf16[2,2,2,32,1536]{4,3,2,1,0:T(8,128)(2,1)S(1)}, bf16[2,2,2,32,1536]{4,3,2,1,0:T(8,128)(2,1)S(1)}, u32[]{:S(2)}, u32[]{:S(2)}) collective-permute-start(bf16[2,2,2,32,1536]{4,3,2,1,0:T(8,128)(2,1)S(1)} %pad_maximum_fusion.16), channel_id=1, source_target_pairs={{0,1},{1,0},{2,3},{3,2},{4,5},{5,4},{6,7},{7,6},{8,9},{9,8},{10,11... | collective-permute-start | bytes 2359304 | tf_op jit(solution)/shard_map/ppermute | solution.py:465
  83.4 27.8 %collective-permute-start.11 = (bf16[2,32,5120]{2,1,0:T(8,128)(2,1)}, bf16[2,32,5120]{2,1,0:T(8,128)(2,1)}, u32[]{:S(2)}, u32[]{:S(2)}) collective-permute-start(bf16[2,32,5120]{2,1,0:T(8,128)(2,1)} %pad_maximum_fusion.17), channel_id=1, source_target_pairs={{0,2},{2,0},{1,3},{3,1},{4,6},{6,4},{5,7},{7,5},{8,10},{10,8},{9,1... | collective-permute-start | bytes 1966088 | tf_op jit(solution)/shard_map/ppermute | solution.py:465
  84.7 42.1 %collective-permute-start.13 = (bf16[2,2,192,1024]{3,2,1,0:T(8,128)(2,1)}, bf16[2,2,192,1024]{3,2,1,0:T(8,128)(2,1)}, u32[]{:S(2)}, u32[]{:S(2)}) collective-permute-start(bf16[2,2,192,1024]{3,2,1,0:T(8,128)(2,1)} %pad_maximum_fusion.6), channel_id=1, source_target_pairs={{0,1},{1,0},{2,3},{3,2},{4,5},{5,4},{6,7},{7,6},{8,9},{9,8},{10,11... | collective-permute-start | bytes 4718600 | tf_op jit(solution)/shard_map/ppermute | solution.py:465
  87.1 24.1 %collective-permute-start.12 = (bf16[32,4096]{1,0:T(8,128)(2,1)}, bf16[32,4096]{1,0:T(8,128)(2,1)}, u32[]{:S(2)}, u32[]{:S(2)}) collective-permute-start(bf16[32,4096]{1,0:T(8,128)(2,1)} %param.28), channel_id=1, source_target_pairs={{0,4},{4,0},{1,5},{5,1},{2,6},{6,2},{3,7},{7,3},{8,12},{12,8},{9,1... | collective-permute-start | bytes 786440 | tf_op jit(solution)/shard_map/ppermute | solution.py:465
  90.7 640.3 %all-gather.5.cloned.1.call-start = ((), (), s32[]{:S(2)}) async-start(), calls=%async_computation.1 | async-start | bytes 4325376 | tf_op jit(solution)/shard_map/all_gather | solution.py:1019
  132.2 23.0 %collective-permute-start.14 = (bf16[2,2,32,2560]{3,2,1,0:T(8,128)(2,1)S(1)}, bf16[2,2,32,2560]{3,2,1,0:T(8,128)(2,1)S(1)}, u32[]{:S(2)}, u32[]{:S(2)}) collective-permute-start(bf16[2,2,32,2560]{3,2,1,0:T(8,128)(2,1)S(1)} %get-tuple-element.270), channel_id=1, source_target_pairs={{0,1},{1,0},{2,3},{3,2},{4,5},{5,4},{6,7},{7,6},{8,9},{9,8},{10,11... | collective-permute-start | bytes 1966088 | tf_op jit(solution)/shard_map/ppermute | solution.py:465
  132.8 24.8 %collective-permute-start.15 = (bf16[2,2,32,2560]{3,2,1,0:T(8,128)(2,1)S(1)}, bf16[2,2,32,2560]{3,2,1,0:T(8,128)(2,1)S(1)}, u32[]{:S(2)}, u32[]{:S(2)}) collective-permute-start(bf16[2,2,32,2560]{3,2,1,0:T(8,128)(2,1)S(1)} %get-tuple-element.271), channel_id=1, source_target_pairs={{0,16},{16,0},{1,17},{17,1},{2,18},{18,2},{3,19},{19,3},{4,20},{20... | collective-permute-start | bytes 1966088 | tf_op jit(solution)/shard_map/ppermute | solution.py:465
  158.9 37.9 %collective-permute-start.16 = (bf16[2,2,2,32,2560]{4,3,2,1,0:T(8,128)(2,1)}, bf16[2,2,2,32,2560]{4,3,2,1,0:T(8,128)(2,1)}, u32[]{:S(2)}, u32[]{:S(2)}) collective-permute-start(bf16[2,2,2,32,2560]{4,3,2,1,0:T(8,128)(2,1)} %pad_maximum_fusion.9), channel_id=1, source_target_pairs={{0,16},{16,0},{1,17},{17,1},{2,18},{18,2},{3,19},{19,3},{4,20},{20... | collective-permute-start | bytes 3932168 | tf_op jit(solution)/shard_map/ppermute | solution.py:465
  161.4 35.5 %collective-permute-start.17 = (bf16[2,2,2,32,2560]{4,3,2,1,0:T(8,128)(2,1)S(1)}, bf16[2,2,2,32,2560]{4,3,2,1,0:T(8,128)(2,1)}, u32[]{:S(2)}, u32[]{:S(2)}) collective-permute-start(bf16[2,2,2,32,2560]{4,3,2,1,0:T(8,128)(2,1)S(1)} %pad_maximum_fusion.10), channel_id=1, source_target_pairs={{0,1},{1,0},{2,3},{3,2},{4,5},{5,4},{6,7},{7,6},{8,9},{9,8},{10,11... | collective-permute-start | bytes 3932168 | tf_op jit(solution)/shard_map/ppermute | solution.py:465
  162.7 34.2 %collective-permute-start.18 = (bf16[2,32,4096]{2,1,0:T(8,128)(2,1)}, bf16[2,32,4096]{2,1,0:T(8,128)(2,1)S(1)}, u32[]{:S(2)}, u32[]{:S(2)}) collective-permute-start(bf16[2,32,4096]{2,1,0:T(8,128)(2,1)} %pad_maximum_fusion.20), channel_id=1, source_target_pairs={{0,2},{2,0},{1,3},{3,1},{4,6},{6,4},{5,7},{7,5},{8,10},{10,8},{9,1... | collective-permute-start | bytes 1572872 | tf_op jit(solution)/shard_map/ppermute | solution.py:465
  202.5 23.1 %collective-permute-start.21 = (bf16[2,2,32,2048]{3,2,1,0:T(8,128)(2,1)S(1)}, bf16[2,2,32,2048]{3,2,1,0:T(8,128)(2,1)}, u32[]{:S(2)}, u32[]{:S(2)}) collective-permute-start(bf16[2,2,32,2048]{3,2,1,0:T(8,128)(2,1)S(1)} %pad_maximum_fusion.21), channel_id=1, source_target_pairs={{0,1},{1,0},{2,3},{3,2},{4,5},{5,4},{6,7},{7,6},{8,9},{9,8},{10,11... | collective-permute-start | bytes 1572872 | tf_op jit(solution)/shard_map/ppermute | solution.py:465
  204.5 21.1 %collective-permute-start.22 = (bf16[2,2,32,2048]{3,2,1,0:T(8,128)(2,1)S(1)}, bf16[2,2,32,2048]{3,2,1,0:T(8,128)(2,1)}, u32[]{:S(2)}, u32[]{:S(2)}) collective-permute-start(bf16[2,2,32,2048]{3,2,1,0:T(8,128)(2,1)S(1)} %pad_maximum_fusion.22), channel_id=1, source_target_pairs={{0,16},{16,0},{1,17},{17,1},{2,18},{18,2},{3,19},{19,3},{4,20},{20... | collective-permute-start | bytes 1572872 | tf_op jit(solution)/shard_map/ppermute | solution.py:465
  228.6 25.3 %collective-permute-start.23 = (bf16[2,2,2,32,2048]{4,3,2,1,0:T(8,128)(2,1)S(1)}, bf16[2,2,2,32,2048]{4,3,2,1,0:T(8,128)(2,1)S(1)}, u32[]{:S(2)}, u32[]{:S(2)}) collective-permute-start(bf16[2,2,2,32,2048]{4,3,2,1,0:T(8,128)(2,1)S(1)} %pad_maximum_fusion.12), channel_id=1, source_target_pairs={{0,16},{16,0},{1,17},{17,1},{2,18},{18,2},{3,19},{19,3},{4,20},{20... | collective-permute-start | bytes 3145736 | tf_op jit(solution)/shard_map/ppermute | solution.py:465
  228.7 25.5 %collective-permute-start.24 = (bf16[2,2,2,32,2048]{4,3,2,1,0:T(8,128)(2,1)S(1)}, bf16[2,2,2,32,2048]{4,3,2,1,0:T(8,128)(2,1)S(1)}, u32[]{:S(2)}, u32[]{:S(2)}) collective-permute-start(bf16[2,2,2,32,2048]{4,3,2,1,0:T(8,128)(2,1)S(1)} %pad_maximum_fusion.13), channel_id=1, source_target_pairs={{0,1},{1,0},{2,3},{3,2},{4,5},{5,4},{6,7},{7,6},{8,9},{9,8},{10,11... | collective-permute-start | bytes 3145736 | tf_op jit(solution)/shard_map/ppermute | solution.py:465
  344.1 55.7 %collective-permute-start.30 = (bf16[1,512,4096]{2,1,0:T(8,128)(2,1)}, bf16[1,512,4096]{2,1,0:T(8,128)(2,1)}, u32[]{:S(2)}, u32[]{:S(2)}) collective-permute-start(bf16[1,512,4096]{2,1,0:T(8,128)(2,1)} %bitcast.450), channel_id=1, source_target_pairs={{0,8},{8,0},{1,9},{9,1},{2,10},{10,2},{3,11},{11,3},{4,12},{12,4},... | collective-permute-start | bytes 12582920 | tf_op jit(solution)/shard_map/ppermute | solution.py:465
  367.5 32.3 %collective-permute-start.28 = (bf16[1,2,2,2,128,512]{5,4,1,2,3,0:T(8,128)(2,1)}, bf16[1,2,2,2,128,512]{5,4,1,2,3,0:T(8,128)(2,1)}, u32[]{:S(2)}, u32[]{:S(2)}) collective-permute-start(bf16[1,2,2,2,128,512]{5,4,1,2,3,0:T(8,128)(2,1)} %bitcast.365), channel_id=1, source_target_pairs={{0,16},{16,0},{1,17},{17,1},{2,18},{18,2},{3,19},{19,3},{4,20},{20... | collective-permute-start | bytes 3145736 | tf_op jit(solution)/shard_map/ppermute | solution.py:465
  369.3 30.5 %collective-permute-start.29 = (bf16[1,2,2,2,128,512]{5,4,2,3,1,0:T(8,128)(2,1)}, bf16[1,2,2,2,128,512]{5,4,2,3,1,0:T(8,128)(2,1)}, u32[]{:S(2)}, u32[]{:S(2)}) collective-permute-start(bf16[1,2,2,2,128,512]{5,4,2,3,1,0:T(8,128)(2,1)} %bitcast.364), channel_id=1, source_target_pairs={{0,1},{1,0},{2,3},{3,2},{4,5},{5,4},{6,7},{7,6},{8,9},{9,8},{10,11... | collective-permute-start | bytes 3145736 | tf_op jit(solution)/shard_map/ppermute | solution.py:465
  429.6 50.0 %collective-permute-start.35 = (bf16[5,512,1024]{2,1,0:T(8,128)(2,1)}, bf16[5,512,1024]{2,1,0:T(8,128)(2,1)}, u32[]{:S(2)}, u32[]{:S(2)}) collective-permute-start(bf16[5,512,1024]{2,1,0:T(8,128)(2,1)} %half_products.4), channel_id=1, source_target_pairs={{0,8},{8,0},{1,9},{9,1},{2,10},{10,2},{3,11},{11,3},{4,12},{12,4},... | collective-permute-start | bytes 15728648 | tf_op jit(solution)/shard_map/ppermute | solution.py:465
  429.6 37.4 %collective-permute-start.33 = (bf16[1,2,2,2,32,2048]{5,4,1,2,3,0:T(8,128)(2,1)}, bf16[1,2,2,2,32,2048]{5,4,1,2,3,0:T(8,128)(2,1)}, u32[]{:S(2)}, u32[]{:S(2)}) collective-permute-start(bf16[1,2,2,2,32,2048]{5,4,1,2,3,0:T(8,128)(2,1)} %bitcast.405), channel_id=1, source_target_pairs={{0,16},{16,0},{1,17},{17,1},{2,18},{18,2},{3,19},{19,3},{4,20},{20... | collective-permute-start | bytes 3145736 | tf_op jit(solution)/shard_map/ppermute | solution.py:465
  429.8 37.2 %collective-permute-start.34 = (bf16[1,2,2,2,32,2048]{5,4,2,3,1,0:T(8,128)(2,1)}, bf16[1,2,2,2,32,2048]{5,4,2,3,1,0:T(8,128)(2,1)}, u32[]{:S(2)}, u32[]{:S(2)}) collective-permute-start(bf16[1,2,2,2,32,2048]{5,4,2,3,1,0:T(8,128)(2,1)} %bitcast.404), channel_id=1, source_target_pairs={{0,1},{1,0},{2,3},{3,2},{4,5},{5,4},{6,7},{7,6},{8,9},{9,8},{10,11... | collective-permute-start | bytes 3145736 | tf_op jit(solution)/shard_map/ppermute | solution.py:465
  437.3 29.4 %collective-permute-start.31 = (bf16[1,2,2,128,512]{4,3,1,2,0:T(8,128)(2,1)}, bf16[1,2,2,128,512]{4,3,1,2,0:T(8,128)(2,1)}, u32[]{:S(2)}, u32[]{:S(2)}) collective-permute-start(bf16[1,2,2,128,512]{4,3,1,2,0:T(8,128)(2,1)} %dynamic-slice_bitcast_fusion.7), channel_id=1, source_target_pairs={{0,1},{1,0},{2,3},{3,2},{4,5},{5,4},{6,7},{7,6},{8,9},{9,8},{10,11... | collective-permute-start | bytes 1572872 | tf_op jit(solution)/shard_map/ppermute | solution.py:465
  439.0 27.9 %collective-permute-start.32 = (bf16[1,2,2,128,512]{4,3,1,2,0:T(8,128)(2,1)}, bf16[1,2,2,128,512]{4,3,1,2,0:T(8,128)(2,1)}, u32[]{:S(2)}, u32[]{:S(2)}) collective-permute-start(bf16[1,2,2,128,512]{4,3,1,2,0:T(8,128)(2,1)} %dynamic-slice_bitcast_fusion.6), channel_id=1, source_target_pairs={{0,16},{16,0},{1,17},{17,1},{2,18},{18,2},{3,19},{19,3},{4,20},{20... | collective-permute-start | bytes 1572872 | tf_op jit(solution)/shard_map/ppermute | solution.py:465
  466.7 70.8 %collective-permute-start.40 = (bf16[2,2,64,1024]{3,2,0,1:T(8,128)(2,1)}, bf16[2,2,64,1024]{3,2,0,1:T(8,128)(2,1)}, u32[]{:S(2)}, u32[]{:S(2)}) collective-permute-start(bf16[2,2,64,1024]{3,2,0,1:T(8,128)(2,1)} %bitcast.369), channel_id=1, source_target_pairs={{0,1},{1,0},{2,3},{3,2},{4,5},{5,4},{6,7},{7,6},{8,9},{9,8},{10,11... | collective-permute-start | bytes 1572872 | tf_op jit(solution)/shard_map/ppermute | solution.py:465
  476.1 67.1 %collective-permute-start.36 = (bf16[1,2,2,32,2048]{4,3,1,2,0:T(8,128)(2,1)}, bf16[1,2,2,32,2048]{4,3,1,2,0:T(8,128)(2,1)}, u32[]{:S(2)}, u32[]{:S(2)}) collective-permute-start(bf16[1,2,2,32,2048]{4,3,1,2,0:T(8,128)(2,1)} %dynamic-slice_bitcast_fusion.5), channel_id=1, source_target_pairs={{0,1},{1,0},{2,3},{3,2},{4,5},{5,4},{6,7},{7,6},{8,9},{9,8},{10,11... | collective-permute-start | bytes 1572872 | tf_op jit(solution)/shard_map/ppermute | solution.py:465
  477.9 65.3 %collective-permute-start.37 = (bf16[1,2,2,32,2048]{4,3,1,2,0:T(8,128)(2,1)}, bf16[1,2,2,32,2048]{4,3,1,2,0:T(8,128)(2,1)}, u32[]{:S(2)}, u32[]{:S(2)}) collective-permute-start(bf16[1,2,2,32,2048]{4,3,1,2,0:T(8,128)(2,1)} %dynamic-slice_bitcast_fusion.4), channel_id=1, source_target_pairs={{0,16},{16,0},{1,17},{17,1},{2,18},{18,2},{3,19},{19,3},{4,20},{20... | collective-permute-start | bytes 1572872 | tf_op jit(solution)/shard_map/ppermute | solution.py:465
  496.2 53.8 %collective-permute-start.38 = (bf16[5,2,2,2,32,512]{5,4,0,1,2,3:T(8,128)(2,1)}, bf16[5,2,2,2,32,512]{5,4,0,1,2,3:T(8,128)(2,1)}, u32[]{:S(2)}, u32[]{:S(2)}) collective-permute-start(bf16[5,2,2,2,32,512]{5,4,0,1,2,3:T(8,128)(2,1)} %bitcast.361), channel_id=1, source_target_pairs={{0,16},{16,0},{1,17},{17,1},{2,18},{18,2},{3,19},{19,3},{4,20},{20... | collective-permute-start | bytes 3932168 | tf_op jit(solution)/shard_map/ppermute | solution.py:465
  496.5 53.5 %collective-permute-start.39 = (bf16[5,2,2,2,32,512]{5,4,0,2,3,1:T(8,128)(2,1)}, bf16[5,2,2,2,32,512]{5,4,0,2,3,1:T(8,128)(2,1)}, u32[]{:S(2)}, u32[]{:S(2)}) collective-permute-start(bf16[5,2,2,2,32,512]{5,4,0,2,3,1:T(8,128)(2,1)} %bitcast.360), channel_id=1, source_target_pairs={{0,1},{1,0},{2,3},{3,2},{4,5},{5,4},{6,7},{7,6},{8,9},{9,8},{10,11... | collective-permute-start | bytes 3932168 | tf_op jit(solution)/shard_map/ppermute | solution.py:465
  561.3 37.0 %collective-permute-start.46 = (bf16[2,2,128,1024]{3,2,0,1:T(8,128)(2,1)}, bf16[2,2,128,1024]{3,2,0,1:T(8,128)(2,1)S(1)}, u32[]{:S(2)}, u32[]{:S(2)}) collective-permute-start(bf16[2,2,128,1024]{3,2,0,1:T(8,128)(2,1)} %bitcast.366), channel_id=1, source_target_pairs={{0,1},{1,0},{2,3},{3,2},{4,5},{5,4},{6,7},{7,6},{8,9},{9,8},{10,11... | collective-permute-start | bytes 3145736 | tf_op jit(solution)/shard_map/ppermute | solution.py:465
  562.2 36.1 %collective-permute-start.44 = (bf16[5,2,2,32,512]{4,3,0,1,2:T(8,128)(2,1)}, bf16[5,2,2,32,512]{4,3,0,1,2:T(8,128)(2,1)S(1)}, u32[]{:S(2)}, u32[]{:S(2)}) collective-permute-start(bf16[5,2,2,32,512]{4,3,0,1,2:T(8,128)(2,1)} %dynamic-slice_bitcast_fusion.2), channel_id=1, source_target_pairs={{0,1},{1,0},{2,3},{3,2},{4,5},{5,4},{6,7},{7,6},{8,9},{9,8},{10,11... | collective-permute-start | bytes 1966088 | tf_op jit(solution)/shard_map/ppermute | solution.py:465
  563.3 35.0 %collective-permute-start.45 = (bf16[5,2,2,32,512]{4,3,0,1,2:T(8,128)(2,1)}, bf16[5,2,2,32,512]{4,3,0,1,2:T(8,128)(2,1)}, u32[]{:S(2)}, u32[]{:S(2)}) collective-permute-start(bf16[5,2,2,32,512]{4,3,0,1,2:T(8,128)(2,1)} %dynamic-slice_bitcast_fusion.1), channel_id=1, source_target_pairs={{0,16},{16,0},{1,17},{17,1},{2,18},{18,2},{3,19},{19,3},{4,20},{20... | collective-permute-start | bytes 1966088 | tf_op jit(solution)/shard_map/ppermute | solution.py:465
  567.6 27.3 %collective-permute-start.43 = (bf16[1,2,32,4096]{3,2,1,0:T(8,128)(2,1)}, bf16[1,2,32,4096]{3,2,1,0:T(8,128)(2,1)}, u32[]{:S(2)}, u32[]{:S(2)}) collective-permute-start(bf16[1,2,32,4096]{3,2,1,0:T(8,128)(2,1)} %fusion.80), channel_id=1, source_target_pairs={{0,2},{2,0},{1,3},{3,1},{4,6},{6,4},{5,7},{7,5},{8,10},{10,8},{9,1... | collective-permute-start | bytes 1572872 | tf_op jit(solution)/shard_map/ppermute | solution.py:465
  576.3 18.5 %collective-permute-start.47 = (bf16[2,64,1024]{2,1,0:T(8,128)(2,1)}, bf16[2,64,1024]{2,1,0:T(8,128)(2,1)S(1)}, u32[]{:S(2)}, u32[]{:S(2)}) collective-permute-start(bf16[2,64,1024]{2,1,0:T(8,128)(2,1)} %dynamic-slice_bitcast_fusion.14), channel_id=1, source_target_pairs={{0,2},{2,0},{1,3},{3,1},{4,6},{6,4},{5,7},{7,5},{8,10},{10,8},{9,1... | collective-permute-start | bytes 786440 | tf_op jit(solution)/shard_map/ppermute | solution.py:465
  624.5 42.5 %collective-permute-start.49 = (bf16[5,2,32,1024]{3,2,0,1:T(8,128)(2,1)S(1)}, bf16[5,2,32,1024]{3,2,0,1:T(8,128)(2,1)S(1)}, u32[]{:S(2)}, u32[]{:S(2)}) collective-permute-start(bf16[5,2,32,1024]{3,2,0,1:T(8,128)(2,1)S(1)} %copy-done.91), channel_id=1, source_target_pairs={{0,2},{2,0},{1,3},{3,1},{4,6},{6,4},{5,7},{7,5},{8,10},{10,8},{9,1... | collective-permute-start | bytes 1966088 | tf_op jit(solution)/shard_map/ppermute | solution.py:465
  625.0 42.0 %collective-permute-start.50 = (bf16[2,128,1024]{2,1,0:T(8,128)(2,1)S(1)}, bf16[2,128,1024]{2,1,0:T(8,128)(2,1)S(1)}, u32[]{:S(2)}, u32[]{:S(2)}) collective-permute-start(bf16[2,128,1024]{2,1,0:T(8,128)(2,1)S(1)} %copy-done.95), channel_id=1, source_target_pairs={{0,2},{2,0},{1,3},{3,1},{4,6},{6,4},{5,7},{7,5},{8,10},{10,8},{9,1... | collective-permute-start | bytes 1572872 | tf_op jit(solution)/shard_map/ppermute | solution.py:465
  647.5 23.2 %collective-permute-start.51 = (bf16[3,2,2,2,32,512]{5,4,0,1,2,3:T(8,128)(2,1)S(1)}, bf16[3,2,2,2,32,512]{5,4,0,1,2,3:T(8,128)(2,1)S(1)}, u32[]{:S(2)}, u32[]{:S(2)}) collective-permute-start(bf16[3,2,2,2,32,512]{5,4,0,1,2,3:T(8,128)(2,1)S(1)} %bitcast.412), channel_id=1, source_target_pairs={{0,16},{16,0},{1,17},{17,1},{2,18},{18,2},{3,19},{19,3},{4,20},{20... | collective-permute-start | bytes 2359304 | tf_op jit(solution)/shard_map/ppermute | solution.py:465
  647.8 22.8 %collective-permute-start.52 = (bf16[3,2,2,2,32,512]{5,4,0,2,3,1:T(8,128)(2,1)S(1)}, bf16[3,2,2,2,32,512]{5,4,0,2,3,1:T(8,128)(2,1)S(1)}, u32[]{:S(2)}, u32[]{:S(2)}) collective-permute-start(bf16[3,2,2,2,32,512]{5,4,0,2,3,1:T(8,128)(2,1)S(1)} %bitcast.411), channel_id=1, source_target_pairs={{0,1},{1,0},{2,3},{3,2},{4,5},{5,4},{6,7},{7,6},{8,9},{9,8},{10,11... | collective-permute-start | bytes 2359304 | tf_op jit(solution)/shard_map/ppermute | solution.py:465
  671.4 18.2 %collective-permute-start.54 = (bf16[3,2,2,32,512]{4,3,0,1,2:T(8,128)(2,1)S(1)}, bf16[3,2,2,32,512]{4,3,0,1,2:T(8,128)(2,1)S(1)}, u32[]{:S(2)}, u32[]{:S(2)}) collective-permute-start(bf16[3,2,2,32,512]{4,3,0,1,2:T(8,128)(2,1)S(1)} %dynamic-slice_bitcast_fusion.9), channel_id=1, source_target_pairs={{0,1},{1,0},{2,3},{3,2},{4,5},{5,4},{6,7},{7,6},{8,9},{9,8},{10,11... | collective-permute-start | bytes 1179656 | tf_op jit(solution)/shard_map/ppermute | solution.py:465
  671.9 17.9 %collective-permute-start.55 = (bf16[3,2,2,32,512]{4,3,0,1,2:T(8,128)(2,1)S(1)}, bf16[3,2,2,32,512]{4,3,0,1,2:T(8,128)(2,1)S(1)}, u32[]{:S(2)}, u32[]{:S(2)}) collective-permute-start(bf16[3,2,2,32,512]{4,3,0,1,2:T(8,128)(2,1)S(1)} %dynamic-slice_bitcast_fusion.8), channel_id=1, source_target_pairs={{0,16},{16,0},{1,17},{17,1},{2,18},{18,2},{3,19},{19,3},{4,20},{20... | collective-permute-start | bytes 1179656 | tf_op jit(solution)/shard_map/ppermute | solution.py:465
  674.1 29.6 %collective-permute-start.59 = (bf16[64,1024]{1,0:T(8,128)(2,1)S(1)}, bf16[64,1024]{1,0:T(8,128)(2,1)S(1)}, u32[]{:S(2)}, u32[]{:S(2)}) collective-permute-start(bf16[64,1024]{1,0:T(8,128)(2,1)S(1)} %copy-done.102), channel_id=1, source_target_pairs={{0,4},{4,0},{1,5},{5,1},{2,6},{6,2},{3,7},{7,3},{8,12},{12,8},{9,1... | collective-permute-start | bytes 393224 | tf_op jit(solution)/shard_map/ppermute | solution.py:465
  677.9 40.3 %collective-permute-start.57 = (bf16[5,32,1024]{2,1,0:T(8,128)(2,1)S(1)}, bf16[5,32,1024]{2,1,0:T(8,128)(2,1)S(1)}, u32[]{:S(2)}, u32[]{:S(2)}) collective-permute-start(bf16[5,32,1024]{2,1,0:T(8,128)(2,1)S(1)} %dynamic-slice_bitcast_fusion.10), channel_id=1, source_target_pairs={{0,4},{4,0},{1,5},{5,1},{2,6},{6,2},{3,7},{7,3},{8,12},{12,8},{9,1... | collective-permute-start | bytes 983048 | tf_op jit(solution)/shard_map/ppermute | solution.py:465
  677.9 40.3 %collective-permute-start.58 = (bf16[128,1024]{1,0:T(8,128)(2,1)S(1)}, bf16[128,1024]{1,0:T(8,128)(2,1)S(1)}, u32[]{:S(2)}, u32[]{:S(2)}) collective-permute-start(bf16[128,1024]{1,0:T(8,128)(2,1)S(1)} %dynamic-slice_bitcast_fusion.11), channel_id=1, source_target_pairs={{0,4},{4,0},{1,5},{5,1},{2,6},{6,2},{3,7},{7,3},{8,12},{12,8},{9,1... | collective-permute-start | bytes 786440 | tf_op jit(solution)/shard_map/ppermute | solution.py:465
  690.1 28.1 %collective-permute-start.56 = (bf16[3,2,32,1024]{3,2,0,1:T(8,128)(2,1)S(1)}, bf16[3,2,32,1024]{3,2,0,1:T(8,128)(2,1)S(1)}, u32[]{:S(2)}, u32[]{:S(2)}) collective-permute-start(bf16[3,2,32,1024]{3,2,0,1:T(8,128)(2,1)S(1)} %fusion.92), channel_id=1, source_target_pairs={{0,2},{2,0},{1,3},{3,1},{4,6},{6,4},{5,7},{7,5},{8,10},{10,8},{9,1... | collective-permute-start | bytes 1179656 | tf_op jit(solution)/shard_map/ppermute | solution.py:465
  (131 other events, 1233.8 us)
Sparse Core Ops, SparseCore 0:
  90.9 91.3 all-gather.2
  621.3 88.1 all-gather.4

commit v3 on v2

--- a/solution.py
+++ b/solution.py
@@ -291,6 +291,57 @@
         name="attend_backward",
     )(*([scalars] if masked else []), queries, grads, mixed, lse, *kv_list, *kv_list, *given)
     return outs[0], outs[1 : 1 + n_seg], outs[1 + n_seg :]
+def ffn_forward_kernel(h_ref, up_ref, bias_ref, down_ref, act_ref, slope_ref, out_ref):
+    step = pl.program_id(0)
+    rows = h_ref.shape[0]
+    half = rows // 2
+    for at in (0, half):
+        part = slice(at, at + half)
+        pre = product(h_ref[part, :], up_ref[...]) + bias_ref[...]
+        cdf = 0.5 * (1.0 + lax.erf(pre * (0.5**0.5)))
+        act = (pre * cdf).astype(jnp.bfloat16)
+        act_ref[part, :] = act
+        slope = cdf + pre * jnp.exp(-0.5 * pre * pre) * 0.3989422804014327
+        slope_ref[part, :] = slope.astype(jnp.bfloat16)
+        add = product(act, down_ref[...])
+
+        @pl.when(step == 0)
+        def _(part=part, add=add):
+            out_ref[part, :] = add
+
+        @pl.when(step > 0)
+        def _(part=part, add=add):
+            out_ref[part, :] += add
+
+
+def ffn_forward(hidden_two, w_up, up_bias, w_down, step=1024):
+    rows, width = hidden_two.shape
+    units = w_up.shape[1]
+    whole = pl.BlockSpec((rows, width), lambda i: (0, 0))
+    block = pl.BlockSpec((rows, step), lambda i: (0, i))
+    return pl.pallas_call(
+        ffn_forward_kernel,
+        grid=(units // step,),
+        in_specs=[
+            whole,
+            pl.BlockSpec((width, step), lambda i: (0, i)),
+            pl.BlockSpec((1, step), lambda i: (0, i)),
+            pl.BlockSpec((step, width), lambda i: (i, 0)),
+        ],
+        out_specs=[block, block, whole],
+        out_shape=[
+            jax.ShapeDtypeStruct((rows, units), jnp.bfloat16),
+            jax.ShapeDtypeStruct((rows, units), jnp.bfloat16),
+            jax.ShapeDtypeStruct((rows, width), jnp.float32),
+        ],
+        compiler_params=pltpu.CompilerParams(
+            dimension_semantics=("arbitrary",), vmem_limit_bytes=VMEM_LIMIT
+        ),
+        cost_estimate=pl.CostEstimate(flops=1, bytes_accessed=1, transcendentals=0),
+        name="ffn_forward",
+    )(hidden_two, w_up, up_bias.reshape(1, units), w_down)
+
+
 def ffn_backward_kernel(
     core_ref,
     g_ref,
@@ -333,8 +384,9 @@
     def _():
         out_ref[...] += add
 
-    up_other[...] = product(turned[: 2 * quarter, :], pre).astype(jnp.bfloat16)
-    up_mine[...] = product(turned[2 * quarter :, :], pre).astype(jnp.bfloat16)
+    up = product(turned[...], pre).astype(jnp.bfloat16)
+    up_other[...] = up[: 2 * quarter]
+    up_mine[...] = up[2 * quarter :]
     down = product_tn(act_ref[...], grad).astype(jnp.bfloat16)
 
     @pl.when(step < steps // 2)
@@ -402,38 +454,67 @@
 
 
 def half_products_kernel(counts, has_came, core_ref, *refs):
-    out_ref = refs[-1]
-    came_ref = refs[-2] if has_came else None
+    n_in = 2 * sum(counts) + has_came
+    given, out_ref = refs[:n_in], refs[n_in]
+    held, out_held, in_sems, out_sems = refs[n_in + 1 : 2 * n_in + 1], *refs[2 * n_in + 1 :]
+    coming = [
+        pltpu.make_async_copy(source, target, in_sems.at[i])
+        for i, (source, target) in enumerate(zip(given, held))
+    ]
+    if has_came:
+        coming[-1].start()
+    for copy in coming[: n_in - has_came]:
+        copy.start()
+    going = []
     at = 0
     for term, count in enumerate(counts):
-        pairs = [(refs[at + 2 * i], refs[at + 2 * i + 1]) for i in range(count)]
-        at += 2 * count
-        quarter = pairs[0][0].shape[1] // 4
-        for x in (0, 1):
-            rows = slice(x * quarter, (x + 1) * quarter)
-            first = pl.multiple_of((2 * x + core_ref[0]) * quarter, quarter)
-            total = sum(product_tn(left[:, pl.ds(first, quarter)], right[...]) for left, right in pairs)
-            if has_came:
-                total = total + came_ref[term, rows, :].astype(jnp.float32)
-            out_ref[term, rows, :] = total.astype(jnp.bfloat16)
+        total = 0.0
+        for pair in range(count):
+            for copy in coming[at : at + 2]:
+                copy.wait()
+            left, right = held[at], held[at + 1]
+            at += 2
+            quarter = left.shape[1] // 4
+            spots = [
+                pl.ds(pl.multiple_of((2 * x + core_ref[0]) * quarter, quarter), quarter)
+                for x in (0, 1)
+            ]
+            picked = jnp.concatenate([left[:, spot] for spot in spots], 1)
+            total = total + product_tn(picked, right[...])
+        if has_came:
+            if term == 0:
+                coming[-1].wait()
+            total = total + held[-1][term].astype(jnp.float32)
+        out_held[term] = total.astype(jnp.bfloat16)
+        copy = pltpu.make_async_copy(out_held.at[term], out_ref.at[term], out_sems.at[term])
+        copy.start()
+        going.append(copy)
+    for copy in going:
+        copy.wait()
 
 
 def half_products(core, terms, came=None):
     arrays = [matrix for pairs in terms for pair in pairs for matrix in pair]
     shape = (len(terms), arrays[0].shape[1] // 2, arrays[1].shape[1])
-    given = [] if came is None else [came]
+    given = arrays if came is None else [*arrays, came]
     return pl.pallas_call(
         functools.partial(
             half_products_kernel, tuple(len(pairs) for pairs in terms), came is not None
         ),
         in_specs=[pl.BlockSpec(memory_space=pltpu.SMEM)]
-        + [pl.BlockSpec(memory_space=pltpu.VMEM)] * (len(arrays) + len(given)),
-        out_specs=pl.BlockSpec(memory_space=pltpu.VMEM),
+        + [pl.BlockSpec(memory_space=pl.ANY)] * len(given),
+        out_specs=pl.BlockSpec(memory_space=pl.ANY),
         out_shape=jax.ShapeDtypeStruct(shape, jnp.bfloat16),
+        scratch_shapes=[pltpu.VMEM(array.shape, jnp.bfloat16) for array in given]
+        + [
+            pltpu.VMEM(shape, jnp.bfloat16),
+            pltpu.SemaphoreType.DMA((len(given),)),
+            pltpu.SemaphoreType.DMA((len(terms),)),
+        ],
         compiler_params=pltpu.CompilerParams(vmem_limit_bytes=VMEM_LIMIT),
         cost_estimate=pl.CostEstimate(flops=1, bytes_accessed=1, transcendentals=0),
         name="half_products",
-    )(core, *arrays, *given)
+    )(core, *given)
 
 
 def column_sum(matrix):
@@ -476,13 +557,15 @@
         )
 
     def operands(self):
-        return [self.pick(1)]
+        part = self.pick(1)
+        return [part.reshape(-1, part.shape[-1])]
 
     def launch(self, operands):
         self.coming = swap(operands[0], self.names[0])
 
     def add(self):
-        total = self.pick(0).astype(jnp.float32) + self.coming.astype(jnp.float32)
+        part = self.pick(0)
+        total = part.astype(jnp.float32) + self.coming.reshape(part.shape).astype(jnp.float32)
         self.names.pop(0)
         self.part = total.astype(jnp.bfloat16) if self.names else total
         self.coming = None
@@ -503,7 +586,8 @@
     def operands(self):
         if self.names[0] == "c":
             return [self.other]
-        return [self.pick(side, 1) for side in range(len(self.sides))]
+        parts = [self.pick(side, 1) for side in range(len(self.sides))]
+        return [part.reshape(-1, part.shape[-1]) for part in parts]
 
     def pick(self, side, flip):
         stage = self.names[0]
@@ -523,9 +607,10 @@
             total = total.reshape(terms, 2, 2, 2, 2, rows // 16, width)
             self.sides = [total[..., : width // 2], total[..., width // 2 :]]
         else:
+            kept = [self.pick(side, 0) for side in range(len(coming))]
             self.sides = [
-                self.pick(side, 0).astype(f32) + came.astype(f32)
-                for side, came in enumerate(coming)
+                part.astype(f32) + came.reshape(part.shape).astype(f32)
+                for part, came in zip(kept, coming)
             ]
             if stage != "w":
                 self.sides = [side.astype(bf16) for side in self.sides]
@@ -838,13 +923,13 @@
     tokens = jnp.concatenate([prompt_in[0], cont_in[0, 0]], 0)
     tokens = begin(tokens, first, rows_in)
     tokens = advance(tokens, first)
-    tokens = advance(tokens, first, rows_in)
+    tokens = advance(tokens, rows_in)
+    tokens = advance(tokens, first)
     tokens = begin(tokens, second)
     tokens = advance(tokens, first)
     tokens = advance(tokens, rows_in, second)
     tokens = advance(tokens, first)
-    tokens, down_proj = begin((tokens, down_proj), up)
-    w_down = lax.all_gather(down_proj, links.every, axis=0, tiled=True)
+    tokens = begin(tokens, up)
     tokens = advance(tokens, first)
     self_w, small = first.finish(place)
     w_q, w_kv = self_w[:, :width], self_w[:, width:]
@@ -878,10 +963,11 @@
     prompt_all, enc_all = rows_in.finish(place)
     prompt_kv = (product(prompt_all, w_kv) + kv_bias).astype(bf16)
     plan = self_plan(prompt_rows, prompt_len, slot_len)
-    prompt_kv = advance(prompt_kv, second)
+    prompt_kv, down_proj = advance((prompt_kv, down_proj), second, up)
+    w_down = lax.all_gather(down_proj, links.every, axis=0, tiled=True)
     attn, self_log = attend_forward(scalars, queries, [prompt_kv, cont_kv], plan, prompt_rows)
+    attn = advance(attn, second)
     attn = advance(attn, second, up)
-    attn = advance(attn, second)
     w_so, w_cq, w_ckv, w_co = second.finish(place)
     branch_self = product(attn, w_so) + biases[2]
     resid_one = tokens.astype(f32) + branch_self
@@ -891,21 +977,18 @@
     enc_kv = (product(enc_all, w_ckv) + enc_bias).astype(bf16)
     cross_queries = ((product(hidden_one, w_cq) + biases[3]) * scale).astype(bf16)
     enc_len = enc_all.shape[0]
-    cross_queries = advance(cross_queries, up)
     cross_attn, cross_log = attend_forward(
         None, cross_queries, [enc_kv], cross_plan(row_total, enc_len, 320), 0
     )
     cross_attn = advance(cross_attn, up)
-    (w_up,) = up.finish(place)
     branch_cross = product(cross_attn, w_co) + biases[5]
     resid_two = hidden_one.astype(f32) + branch_cross
     hidden_two = layer_norm(resid_two, gains[1], shifts[1]).astype(bf16)
-
-    pre_act = product(hidden_two, w_up) + hidden_bias
-    half = 0.5 * (1.0 + lax.erf(pre_act * (0.5**0.5)))
-    act = (pre_act * half).astype(bf16)
-    slope = (half + pre_act * jnp.exp(-0.5 * pre_act * pre_act) * 0.3989422804014327).astype(bf16)
-    branch_ffn = product(act, w_down) + biases[6]
+    hidden_two = advance(hidden_two, up)
+    (w_up,) = up.finish(place)
+
+    act, slope, branch_ffn = ffn_forward(hidden_two, w_up, hidden_bias, w_down)
+    branch_ffn = branch_ffn + biases[6]
     resid_three = hidden_two.astype(f32) + branch_ffn
     output = layer_norm(resid_three, gains[2], shifts[2]).astype(bf16)
 
@@ -958,7 +1041,6 @@
         cross_gv[0], w_ckv[:, width:]
     )
     enc_sum = links.row_sum(enc_back)
-    grad_cq = begin(grad_cq, enc_sum)
     grad_hidden_one = grad_two + product_nt(grad_cq, w_cq)
     grad_one, gain_one, shift_one = layer_norm_back(resid_one, gains[0], grad_hidden_one)
     grad_self = grad_one.astype(bf16)
@@ -971,6 +1053,8 @@
             [(enc_all, cross_gv[0])],
         ]
     )
+    if links.fast:
+        grad_self, mid_sum.other = advance((grad_self, mid_sum.other), down_sum, up_sum)
     grad_self = begin(grad_self, mid_sum)
     grad_attn = product_nt(grad_self, w_so).astype(bf16)
     small_part = jnp.concatenate(
@@ -998,18 +1082,18 @@
         0,
     )
     grad_attn, small_part = lax.optimization_barrier((grad_attn, small_part))
-    grad_attn = advance(grad_attn, down_sum, up_sum)
     grad_attn = advance(grad_attn, mid_sum)
     self_args = (queries, grad_attn, attn, self_log, [prompt_kv, cont_kv], plan, prompt_rows)
     part_gq, prompt_gk, prompt_gv = attend_backward(scalars, *self_args, 1024, (0,))
     prompt_gk, prompt_gv = prompt_gk[0], prompt_gv[0]
     w_k, w_v = w_kv[:, :width], w_kv[:, width:]
-    part_gq = advance(part_gq, up_sum, mid_sum, enc_sum, down_sum)
+    part_gq = advance(part_gq, up_sum, mid_sum, down_sum)
     prompt_sum = links.row_sum(product_nt(prompt_gk, w_k) + product_nt(prompt_gv, w_v))
     part_gq = begin(part_gq, prompt_sum)
     self_gq, cont_gk, cont_gv = attend_backward(scalars, *self_args, 512, (1,), part_gq)
     cont_gk, cont_gv = cont_gk[0], cont_gv[0]
-    self_gq = advance(self_gq, down_sum, up_sum, mid_sum, prompt_sum, enc_sum)
+    self_gq = advance(self_gq, down_sum, up_sum, mid_sum, prompt_sum)
+    self_gq = begin(self_gq, enc_sum)
     grad_q = (self_gq.astype(f32) * scale).astype(bf16)
 
     last_part = jnp.stack([column_sum(grad_q), column_sum(prompt_gv) + column_sum(cont_gv)])
@@ -1024,14 +1108,18 @@
             [(prompt_all, prompt_gv), (cont_rows, cont_gv)],
         ]
     )
-    grad_q = begin(grad_q, self_sum)
     input_grad = grad_one + product_nt(grad_q, w_q)
     cont_grad = input_grad[prompt_rows:] + product_nt(cont_gk, w_k) + product_nt(cont_gv, w_v)
-    cont_grad = advance(cont_grad, self_sum)
-    cont_grad = advance(cont_grad, mid_sum, prompt_sum)
-    cont_grad = advance(cont_grad, self_sum, up_sum)
-    cont_grad = advance(cont_grad, self_sum)
-    cont_grad = advance(cont_grad, self_sum, mid_sum, prompt_sum, enc_sum)[None, None]
+    if links.fast:
+        cont_grad, self_sum.other = advance(
+            (cont_grad, self_sum.other), mid_sum, prompt_sum, up_sum
+        )
+    cont_grad = begin(cont_grad, self_sum)
+    cont_grad = advance(cont_grad, self_sum, enc_sum)
+    cont_grad = advance(cont_grad, self_sum, mid_sum, prompt_sum)
+    cont_grad = advance(cont_grad, self_sum, enc_sum)
+    cont_grad = advance(cont_grad, self_sum, enc_sum)
+    cont_grad = cont_grad[None, None]
     prompt_grad = (input_grad[:prompt_rows] + prompt_sum.finish())[None]
     encoder_grad = enc_sum.finish()[None]
     up_total, down_total = up_sum.finish()[0], down_sum.finish()[0]

time: 748 us -> 721 us (0.964)
  matrix products: 82.3 us -> 51.3 us
  Pallas kernels: 213 us -> 224 us
  waiting for transfers between devices: 198 us -> 189 us
    dot_general x9 -> x7, matrix products: 51.1 us -> 23.6 us  [product(): return jnp.dot(first_mat, second_mat, preferred_element_type=jnp.float32)]
    pallas_call x0 -> x1, Pallas kernels: none -> 18.5 us  [ffn_forward(): pl.pallas_call(ffn_forward_kernel, grid=(units // step,), in_specs=[whole...]
    ppermute x61, waiting for transfers between devices: 198 us -> 189 us  [swap(): return lax.ppermute(value, axis, SWAP)]
    dynamic_slice x8 -> x18, local copies, waits for them, and re-layouts: 5.69 us -> 13.5 us  [pick(): return lax.dynamic_index_in_dim(self.sides[side], here, dim, keepdims=False)]
  transfers between devices with their start and end apart: 63 -> 63, of which waited for: 28 -> 28; matrix products, arithmetic and copies ran while one was open for 22% -> 19% of each run, Pallas kernels for 22% -> 24%
where the time goes in v3:
time: 721 us; the launch traced here: 716 us
  Pallas kernels  224 us (31%)
  waiting for transfers between devices  189 us (26%)
  other arithmetic  101 us (14%)
  starting transfers between devices  67.6 us (9%)
  local copies, waits for them, and re-layouts  64.4 us (9%)
  matrix products  51.3 us (7%)
  between operations  17.7 us (2%)
    ppermute x61, waiting for transfers between devices, swap(): return lax.ppermute(value, axis, SWAP)  189 us
    pallas_call x3, Pallas kernels, attend_backward(): pl.pallas_call(functools.partial(bwd_kernel, plan, masked, slot_at, key_s...  74 us
    ppermute x61, starting transfers between devices, swap(): return lax.ppermute(value, axis, SWAP)  67.5 us
    pallas_call x2, Pallas kernels, attend_forward(): pl.pallas_call(functools.partial(fwd_kernel, plan, masked, slot_at), grid...  40.9 us
    pallas_call x1, Pallas kernels, ffn_backward(): pl.pallas_call(ffn_backward_kernel, grid_spec=pltpu.PrefetchScalarGridSpe...  33.9 us
    pallas_call x4, Pallas kernels, half_products(): pl.pallas_call(functools.partial(half_products_kernel, tuple((len(pairs)...  32 us
    dot_general x10, matrix products, product_nt(): lax.dot_general(first_mat, second_mat, (((1,), (1,)), ((), ())), preferre...  27.7 us
    dot_general x7, matrix products, product(): return jnp.dot(first_mat, second_mat, preferred_element_type=jnp.float32)  23.6 us
  transfers between devices with their start and end apart: 63, of which 28 were waited for; matrix products, arithmetic and copies ran while one was open for 19% of the time, Pallas kernels for 24%

profile of v3, /device:TPU:0, one launch (start us, length us, event | category | flops | bytes accessed | tf_op | source)
XLA Modules:
  0.0 715.7 jit_solution(16294664957097765389)
XLA Ops:
  9.5 4.1 collective-permute-start
  13.7 18.6 %collective-permute-done = bf16[32,3200]{1,0:T(8,128)(2,1)S(1)} collective-permute-done((bf16[32,3200]{1,0:T(8,128)(2,1)S(1)}, bf16[32,3200]{1,0:T(8,128)(2,1)S(1)}, u32[]{:S(2)}, u32[]{:S(2)}) %collective-permute-start) | collective-permute-done | bytes 204832 | tf_op jit(solution)/shard_map/ppermute | solution.py:546
  32.6 7.5 %collective-permute-done.1 = bf16[192,1024]{1,0:T(8,128)(2,1)S(1)} collective-permute-done((bf16[192,1024]{1,0:T(8,128)(2,1)S(1)}, bf16[192,1024]{1,0:T(8,128)(2,1)S(1)}, u32[]{:S(2)}, u32[]{:S(2)}) %collective-permute-start.1) | collective-permute-done | bytes 393248 | tf_op jit(solution)/shard_map/ppermute | solution.py:546
  40.9 8.0 %collective-permute-done.2 = bf16[2,32,3200]{2,1,0:T(8,128)(2,1)S(1)} collective-permute-done((bf16[2,32,3200]{2,1,0:T(8,128)(2,1)S(1)}, bf16[2,32,3200]{2,1,0:T(8,128)(2,1)S(1)}, u32[]{:S(2)}, u32[]{:S(2)}) %collective-permute-start.2) | collective-permute-done | bytes 409632 | tf_op jit(solution)/shard_map/ppermute | solution.py:546
  53.8 7.5 %collective-permute-done.4 = bf16[2,2,32,1536]{3,2,1,0:T(8,128)(2,1)S(1)} collective-permute-done((bf16[2,2,32,1536]{3,2,1,0:T(8,128)(2,1)S(1)}, bf16[2,2,32,1536]{3,2,1,0:T(8,128)(2,1)S(1)}, u32[]{:S(2)}, u32[]{:S(2)}) %collective-permute-start.4) | collective-permute-done | bytes 393248 | tf_op jit(solution)/shard_map/ppermute | solution.py:546
  64.0 5.3 collective-permute-done.6
  69.3 3.3 collective-permute-done.5
  74.8 6.1 collective-permute-done.8
  85.7 4.0 collective-permute-start.12
  89.8 7.0 assemble.3
  96.8 3.5 slice_reduce_fusion.1
  107.0 12.9 %collective-permute-done.13 = bf16[2,2,192,1024]{3,2,1,0:T(8,128)(2,1)S(1)} collective-permute-done((bf16[2,2,192,1024]{3,2,1,0:T(8,128)(2,1)}, bf16[2,2,192,1024]{3,2,1,0:T(8,128)(2,1)S(1)}, u32[]{:S(2)}, u32[]{:S(2)}) %collective-permute-start.13) | collective-permute-done | bytes 1572896 | tf_op jit(solution)/shard_map/ppermute | solution.py:546
  128.5 6.1 add_convert_fusion.refs_2_.refs_4_.refs_5_.refs_6_
  134.6 4.7 collective-permute-done.16
  150.7 29.8 %attend_forward.2 = (bf16[640,1024]{1,0:T(8,128)(2,1)S(1)}, f32[640,128]{1,0:T(8,128)S(1)}) custom-call(s32[3]{0:T(128)S(1)} %pad_add_fusion.refs_0_, bf16[640,1024]{1,0:T(8,128)(2,1)S(1)} %copy-done.16, bf16[1024,2048]{1,0:T(8,128)(2,1)} %add_convert_fusion.refs_2_.refs_4_.refs_5_.refs_6_, bf16[512,2048]{1,0:T(8,128)(2,1)S(1)} %add_convert_fusion.3.refs_3_.refs_5_.refs_6_, ...), custom_call_target="tpu_custom_call" | custom-call | flops 1 | bytes 1 | tf_op jit(solution)/shard_map/attend_forward/pallas_call | solution.py:227
  188.3 15.7 %collective-permute-done.21 = bf16[2,2,32,2048]{3,2,1,0:T(8,128)(2,1)S(1)} collective-permute-done((bf16[2,2,32,2048]{3,2,1,0:T(8,128)(2,1)S(1)}, bf16[2,2,32,2048]{3,2,1,0:T(8,128)(2,1)S(1)}, u32[]{:S(2)}, u32[]{:S(2)}) %collective-permute-start.21) | collective-permute-done | bytes 524320 | tf_op jit(solution)/shard_map/ppermute | solution.py:546
  210.6 8.2 %assemble.4 = (bf16[1024,1024]{1,0:T(8,128)(2,1)S(1)}, bf16[1024,1024]{1,0:T(8,128)(2,1)S(1)}, bf16[1024,2048]{1,0:T(8,128)(2,1)}, bf16[1024,1024]{1,0:T(8,128)(2,1)}) custom-call(s32[5]{0:T(128)S(1)} %stack.333.place_ref, bf16[2,2,2,2,32,2560]{5,4,3,2,1,0:T(8,128)(2,1)} %copy-done.47, bf16[2,2,2,2,32,2560]{5,4,3,2,1,0:T(8,128)(2,1)} %copy-done.46, ...), custom_call_target="tpu_custom_call" | custom-call | bytes 20971520 | tf_op jit(solution)/shard_map/assemble/pallas_call | solution.py:745
  229.8 11.1 %attend_forward.3 = (bf16[640,1024]{1,0:T(8,128)(2,1)S(1)}, f32[640,128]{1,0:T(8,128)S(1)}) custom-call(bf16[640,1024]{1,0:T(8,128)(2,1)S(1)} %multiply_convert_fusion.2.refs_0_, bf16[512,2048]{1,0:T(8,128)(2,1)S(1)} %add_convert_fusion.2.refs_1_.refs_2_.refs_4_.refs_5_, bf16[512,2048]{1,0:T(8,128)(2,1)S(1)} %add_convert_fusion.2.refs_1_.refs_2_.refs_4_.refs_5_), custom_call_target="tpu_custom_call" | custom-call | flops 1 | bytes 1 | tf_op jit(solution)/shard_map/attend_forward/pallas_call | solution.py:227
  249.2 5.5 fusion.99
  256.2 8.0 %assemble.5.up_ref = bf16[1024,4096]{1,0:T(8,128)(2,1)} custom-call(s32[5]{0:T(128)S(1)} %stack.333.place_ref, bf16[2,2,2,2,32,2048]{5,4,3,2,1,0:T(8,128)(2,1)} %pad_maximum_fusion.3.left_own, bf16[2,2,2,2,32,2048]{5,4,3,2,1,0:T(8,128)(2,1)} %pad_maximum_fusion.4.right_own, bf16[2,2,2,2,32,2048]{5,4,3,2,1,0:T(8,128)(2,1)} %collective-permute-done.25.left_came, ...), custom_call_target="tpu_custom_call" | custom-call | bytes 16777216 | tf_op jit(solution)/shard_map/assemble/pallas_call | solution.py:745
  264.2 18.5 %ffn_forward.1 = (bf16[640,4096]{1,0:T(8,128)(2,1)}, bf16[640,4096]{1,0:T(8,128)(2,1)}, f32[640,1024]{1,0:T(8,128)S(1)}) custom-call(bf16[640,1024]{1,0:T(8,128)(2,1)S(1)} %add_convert_fusion.5.h_ref, bf16[1024,4096]{1,0:T(8,128)(2,1)} %assemble.5.up_ref, f32[1,4096]{1,0:T(1,128)S(1)} %reshape_reshape.3.bias_ref, ...), custom_call_target="tpu_custom_call" | custom-call | flops 1 | bytes 1 | tf_op jit(solution)/shard_map/ffn_forward/pallas_call | solution.py:322
  282.7 5.0 multiply_reduce_fusion.2
  293.4 33.9 %ffn_backward.1 = (bf16[2048,1024]{1,0:T(8,128)(2,1)}, bf16[2048,1024]{1,0:T(8,128)(2,1)}, bf16[512,4096]{1,0:T(8,128)(2,1)}, bf16[512,4096]{1,0:T(8,128)(2,1)},...) custom-call(s32[1]{0:T(128)} %bitcast.30.core_ref, bf16[640,1024]{1,0:T(8,128)(2,1)S(1)} %get-tuple-element.481.g_ref, ...), custom_call_target="tpu_custom_call" | custom-call | flops 1 | bytes 1 | tf_op jit(solution)/shard_map/ffn_backward/pallas_call | solution.py:417
  329.2 7.8 %multiply_reduce_fusion = (f32[1024]{0:T(1024)}, f32[640]{0:T(1024)S(1)}, f32[640]{0:T(1024)S(1)}, f32[1024]{0:T(1024)}, f32[640,1024]{1,0:T(8,128)S(1)}, /*index=5*/bf16[640,1024]{1,0:T(8,128)(2,1)}) fusion(f32[640,1024]{1,0:T(8,128)} %copy-done.41, f32[640]{0:T(1024)S(1)} %add_rsqrt_fusion.1, f32[640]{0:T(1024)S(1)} %broadcast_multiply_fusion.7, ...), kind=kLoop, calls=%fused_computation.43 | loop fusion | flops 15725312 | bytes 13148160 | tf_op jit(solution)/shard_map/reduce_sum | solution.py:539
  343.0 4.3 fusion.1
  355.9 21.0 %attend_backward.3 = (bf16[640,1024]{1,0:T(8,128)(2,1)S(1)}, bf16[512,1024]{1,0:T(8,128)(2,1)S(1)}, bf16[512,1024]{1,0:T(8,128)(2,1)S(1)}) custom-call(bf16[640,1024]{1,0:T(8,128)(2,1)S(1)} %copy-done.24, bf16[640,1024]{1,0:T(8,128)(2,1)S(1)} %copy-done.28, bf16[640,1024]{1,0:T(8,128)(2,1)} %copy-done.8, f32[8,2,640]{2,1,0:T(2,128)S(1)} %reshape.763.refs_3_, ...), custom_call_target="tpu_custom_call" | custom-call | flops 1 | bytes 1 | tf_op jit(solution)/shard_map/attend_backward/pallas_call | solution.py:272
  377.7 5.3 fusion
  404.7 6.7 half_products.4
  411.4 17.5 %collective-permute-done.31 = bf16[512,512]{1,0:T(8,128)(2,1)S(1)} collective-permute-done((bf16[512,512]{1,0:T(8,128)(2,1)}, bf16[512,512]{1,0:T(8,128)(2,1)S(1)}, u32[]{:S(2)}, u32[]{:S(2)}) %collective-permute-start.31) | collective-permute-done | bytes 524320 | tf_op jit(solution)/shard_map/ppermute | solution.py:546
  444.7 4.1 concatenate.60
  448.8 3.7 convolution_convert_fusion.refs_2_
  456.4 8.2 %half_products.5 = bf16[5,512,1024]{2,1,0:T(8,128)(2,1)} custom-call(s32[1]{0:T(128)} %bitcast.30.core_ref, bf16[640,1024]{1,0:T(8,128)(2,1)S(1)} %copy-done.10, bf16[640,1024]{1,0:T(8,128)(2,1)S(1)} %copy-done.13, bf16[640,1024]{1,0:T(8,128)(2,1)} %copy-done.45, bf16[640,1024]{1,0:T(8,128)(2,1)} %get-tuple-element.514.refs_3_, bf16[640,1024]{1,0:T(8,128)(2,1)} %copy-done.3, ...), custom_call_target="tpu_custom_call" | custom-call | flops 1 | bytes 1 | tf_op jit(solution)/shard_map/half_products/pallas_call | solution.py:500
  464.6 3.4 fusion.101
  472.0 35.5 %attend_backward.4 = (f32[640,1024]{1,0:T(8,128)}, bf16[1024,1024]{1,0:T(8,128)(2,1)S(1)}, bf16[1024,1024]{1,0:T(8,128)(2,1)}) custom-call(s32[3]{0:T(128)S(1)} %pad_add_fusion.refs_0_, bf16[640,1024]{1,0:T(8,128)(2,1)S(1)} %copy-done.17, bf16[640,1024]{1,0:T(8,128)(2,1)S(1)} %convolution_convert_fusion.refs_2_, bf16[640,1024]{1,0:T(8,128)(2,1)S(1)} %copy-done.4, ...), custom_call_target="tpu_custom_call" | custom-call | flops 1 | bytes 1 | tf_op jit(solution)/shard_map/attend_backward/pallas_call | solution.py:272
  507.5 4.8 fusion.37
  512.2 4.0 add_convert_fusion.1
  537.2 17.5 %attend_backward.5 = (bf16[640,1024]{1,0:T(8,128)(2,1)S(1)}, bf16[512,1024]{1,0:T(8,128)(2,1)S(1)}, bf16[512,1024]{1,0:T(8,128)(2,1)S(1)}) custom-call(s32[3]{0:T(128)S(1)} %pad_add_fusion.refs_0_, bf16[640,1024]{1,0:T(8,128)(2,1)S(1)} %copy-done.17, bf16[640,1024]{1,0:T(8,128)(2,1)S(1)} %convolution_convert_fusion.refs_2_, bf16[640,1024]{1,0:T(8,128)(2,1)} %copy-done.3, ...), custom_call_target="tpu_custom_call" | custom-call | flops 1 | bytes 1 | tf_op jit(solution)/shard_map/attend_backward/pallas_call | solution.py:272
  554.7 4.3 collective-permute-start.41
  562.1 6.8 collective-permute-done.41
  583.7 8.4 %half_products.6 = bf16[3,512,1024]{2,1,0:T(8,128)(2,1)} custom-call(s32[1]{0:T(128)S(6)} %sub.98.core_ref, bf16[640,1024]{1,0:T(8,128)(2,1)S(1)} %pad_maximum_fusion.8.refs_0_, bf16[640,1024]{1,0:T(8,128)(2,1)S(1)} %get-tuple-element.512.refs_1_, bf16[1024,1024]{1,0:T(8,128)(2,1)} %copy-done.1, bf16[1024,1024]{1,0:T(8,128)(2,1)} %copy-done.22, ...), custom_call_target="tpu_custom_call" | custom-call | flops 1 | bytes 1 | tf_op jit(solution)/shard_map/half_products/pallas_call | solution.py:500
  592.2 14.1 %collective-permute-done.48 = bf16[32,4096]{1,0:T(8,128)(2,1)S(1)} collective-permute-done((bf16[32,4096]{1,0:T(8,128)(2,1)S(1)}, bf16[32,4096]{1,0:T(8,128)(2,1)S(1)}, u32[]{:S(2)}, u32[]{:S(2)}) %collective-permute-start.48) | collective-permute-done | bytes 262176 | tf_op jit(solution)/shard_map/ppermute | solution.py:546
  623.5 5.5 collective-permute-done.50
  629.1 8.7 %half_products.7 = bf16[3,512,1024]{2,1,0:T(8,128)(2,1)} custom-call(s32[1]{0:T(128)} %bitcast.30.core_ref, bf16[640,1024]{1,0:T(8,128)(2,1)S(1)} %pad_maximum_fusion.8.refs_0_, bf16[640,1024]{1,0:T(8,128)(2,1)S(1)} %copy-done.15, bf16[1024,1024]{1,0:T(8,128)(2,1)} %copy-done.1, bf16[1024,1024]{1,0:T(8,128)(2,1)} %copy-done.22, ...), custom_call_target="tpu_custom_call" | custom-call | flops 1 | bytes 1 | tf_op jit(solution)/shard_map/half_products/pallas_call | solution.py:500
  644.9 8.9 %collective-permute-done.54 = bf16[128,1024]{1,0:T(8,128)(2,1)S(1)} collective-permute-done((bf16[128,1024]{1,0:T(8,128)(2,1)S(1)}, bf16[128,1024]{1,0:T(8,128)(2,1)S(1)}, u32[]{:S(2)}, u32[]{:S(2)}) %collective-permute-start.54) | collective-permute-done | bytes 262176 | tf_op jit(solution)/shard_map/ppermute | solution.py:546
  653.9 9.6 %collective-permute-done.51 = bf16[768,512]{1,0:T(8,128)(2,1)S(1)} collective-permute-done((bf16[768,512]{1,0:T(8,128)(2,1)S(1)}, bf16[768,512]{1,0:T(8,128)(2,1)S(1)}, u32[]{:S(2)}, u32[]{:S(2)}) %collective-permute-start.51) | collective-permute-done | bytes 786464 | tf_op jit(solution)/shard_map/ppermute | solution.py:546
  668.0 12.0 %collective-permute-done.55 = bf16[384,512]{1,0:T(8,128)(2,1)S(1)} collective-permute-done((bf16[384,512]{1,0:T(8,128)(2,1)S(1)}, bf16[384,512]{1,0:T(8,128)(2,1)S(1)}, u32[]{:S(2)}, u32[]{:S(2)}) %collective-permute-start.55) | collective-permute-done | bytes 393248 | tf_op jit(solution)/shard_map/ppermute | solution.py:546
  685.1 8.8 %collective-permute-done.59 = bf16[64,1024]{1,0:T(8,128)(2,1)S(1)} collective-permute-done((bf16[64,1024]{1,0:T(8,128)(2,1)S(1)}, bf16[64,1024]{1,0:T(8,128)(2,1)S(1)}, u32[]{:S(2)}, u32[]{:S(2)}) %collective-permute-start.59) | collective-permute-done | bytes 131104 | tf_op jit(solution)/shard_map/ppermute | solution.py:546
  698.3 4.2 collective-permute-done.60
  (534 shorter events, 228.8 us)
Async XLA Ops:
  7.3 256.9 %all-gather.3.cloned.1.call-start = ((), (), s32[]{:S(2)}) async-start(), calls=%async_computation | async-start | bytes 8650752 | tf_op jit(solution)/shard_map/all_gather | solution.py:967
  9.5 22.8 %collective-permute-start = (bf16[32,3200]{1,0:T(8,128)(2,1)S(1)}, bf16[32,3200]{1,0:T(8,128)(2,1)S(1)}, u32[]{:S(2)}, u32[]{:S(2)}) collective-permute-start(bf16[32,3200]{1,0:T(8,128)(2,1)S(1)} %pad_maximum_fusion.30), channel_id=1, source_target_pairs={{0,4},{4,0},{1,5},{5,1},{2,6},{6,2},{3,7},{7,3},{8,12},{12,8},{9,1... | collective-permute-start | bytes 614408 | tf_op jit(solution)/shard_map/ppermute | solution.py:546
  13.6 26.4 %collective-permute-start.1 = (bf16[192,1024]{1,0:T(8,128)(2,1)S(1)}, bf16[192,1024]{1,0:T(8,128)(2,1)S(1)}, u32[]{:S(2)}, u32[]{:S(2)}) collective-permute-start(bf16[192,1024]{1,0:T(8,128)(2,1)S(1)} %pad_maximum_fusion.25), channel_id=1, source_target_pairs={{0,4},{4,0},{1,5},{5,1},{2,6},{6,2},{3,7},{7,3},{8,12},{12,8},{9,1... | collective-permute-start | bytes 1179656 | tf_op jit(solution)/shard_map/ppermute | solution.py:546
  32.5 16.4 %collective-permute-start.2 = (bf16[2,32,3200]{2,1,0:T(8,128)(2,1)S(1)}, bf16[2,32,3200]{2,1,0:T(8,128)(2,1)S(1)}, u32[]{:S(2)}, u32[]{:S(2)}) collective-permute-start(bf16[2,32,3200]{2,1,0:T(8,128)(2,1)S(1)} %pad_maximum_fusion.24), channel_id=1, source_target_pairs={{0,2},{2,0},{1,3},{3,1},{4,6},{6,4},{5,7},{7,5},{8,10},{10,8},{9,1... | collective-permute-start | bytes 1228808 | tf_op jit(solution)/shard_map/ppermute | solution.py:546
  40.1 32.5 %collective-permute-start.5 = (bf16[2,192,1024]{2,1,0:T(8,128)(2,1)S(1)}, bf16[2,192,1024]{2,1,0:T(8,128)(2,1)S(1)}, u32[]{:S(2)}, u32[]{:S(2)}) collective-permute-start(bf16[2,192,1024]{2,1,0:T(8,128)(2,1)S(1)} %pad_maximum_fusion.15), channel_id=1, source_target_pairs={{0,2},{2,0},{1,3},{3,1},{4,6},{6,4},{5,7},{7,5},{8,10},{10,8},{9,1... | collective-permute-start | bytes 2359304 | tf_op jit(solution)/shard_map/ppermute | solution.py:546
  52.1 17.1 %collective-permute-start.6 = (bf16[32,5120]{1,0:T(8,128)(2,1)S(1)}, bf16[32,5120]{1,0:T(8,128)(2,1)S(1)}, u32[]{:S(2)}, u32[]{:S(2)}) collective-permute-start(bf16[32,5120]{1,0:T(8,128)(2,1)S(1)} %pad_maximum_fusion.28), channel_id=1, source_target_pairs={{0,4},{4,0},{1,5},{5,1},{2,6},{6,2},{3,7},{7,3},{8,12},{12,8},{9,1... | collective-permute-start | bytes 983048 | tf_op jit(solution)/shard_map/ppermute | solution.py:546
  61.5 19.7 %collective-permute-start.7 = (bf16[2,2,2,32,1664]{4,3,2,1,0:T(8,128)(2,1)S(1)}, bf16[2,2,2,32,1664]{4,3,2,1,0:T(8,128)(2,1)S(1)}, u32[]{:S(2)}, u32[]{:S(2)}) collective-permute-start(bf16[2,2,2,32,1664]{4,3,2,1,0:T(8,128)(2,1)S(1)} %pad_maximum_fusion.14), channel_id=1, source_target_pairs={{0,16},{16,0},{1,17},{17,1},{2,18},{18,2},{3,19},{19,3},{4,20},{20... | collective-permute-start | bytes 2555912 | tf_op jit(solution)/shard_map/ppermute | solution.py:546
  63.0 17.9 %collective-permute-start.8 = (bf16[2,2,2,32,1536]{4,3,2,1,0:T(8,128)(2,1)S(1)}, bf16[2,2,2,32,1536]{4,3,2,1,0:T(8,128)(2,1)S(1)}, u32[]{:S(2)}, u32[]{:S(2)}) collective-permute-start(bf16[2,2,2,32,1536]{4,3,2,1,0:T(8,128)(2,1)S(1)} %pad_maximum_fusion.16), channel_id=1, source_target_pairs={{0,1},{1,0},{2,3},{3,2},{4,5},{5,4},{6,7},{7,6},{8,9},{9,8},{10,11... | collective-permute-start | bytes 2359304 | tf_op jit(solution)/shard_map/ppermute | solution.py:546
  83.2 22.5 %collective-permute-start.11 = (bf16[2,32,5120]{2,1,0:T(8,128)(2,1)}, bf16[2,32,5120]{2,1,0:T(8,128)(2,1)S(1)}, u32[]{:S(2)}, u32[]{:S(2)}) collective-permute-start(bf16[2,32,5120]{2,1,0:T(8,128)(2,1)} %pad_maximum_fusion.17), channel_id=1, source_target_pairs={{0,2},{2,0},{1,3},{3,1},{4,6},{6,4},{5,7},{7,5},{8,10},{10,8},{9,1... | collective-permute-start | bytes 1966088 | tf_op jit(solution)/shard_map/ppermute | solution.py:546
  83.2 36.7 %collective-permute-start.13 = (bf16[2,2,192,1024]{3,2,1,0:T(8,128)(2,1)}, bf16[2,2,192,1024]{3,2,1,0:T(8,128)(2,1)S(1)}, u32[]{:S(2)}, u32[]{:S(2)}) collective-permute-start(bf16[2,2,192,1024]{3,2,1,0:T(8,128)(2,1)} %pad_maximum_fusion.6), channel_id=1, source_target_pairs={{0,1},{1,0},{2,3},{3,2},{4,5},{5,4},{6,7},{7,6},{8,9},{9,8},{10,11... | collective-permute-start | bytes 4718600 | tf_op jit(solution)/shard_map/ppermute | solution.py:546
  85.7 20.1 %collective-permute-start.12 = (bf16[32,4096]{1,0:T(8,128)(2,1)}, bf16[32,4096]{1,0:T(8,128)(2,1)S(1)}, u32[]{:S(2)}, u32[]{:S(2)}) collective-permute-start(bf16[32,4096]{1,0:T(8,128)(2,1)} %param.28), channel_id=1, source_target_pairs={{0,4},{4,0},{1,5},{5,1},{2,6},{6,2},{3,7},{7,3},{8,12},{12,8},{9,1... | collective-permute-start | bytes 786440 | tf_op jit(solution)/shard_map/ppermute | solution.py:546
  123.9 15.9 %collective-permute-start.14 = (bf16[2,2,32,2560]{3,2,1,0:T(8,128)(2,1)S(1)}, bf16[2,2,32,2560]{3,2,1,0:T(8,128)(2,1)S(1)}, u32[]{:S(2)}, u32[]{:S(2)}) collective-permute-start(bf16[2,2,32,2560]{3,2,1,0:T(8,128)(2,1)S(1)} %get-tuple-element.284), channel_id=1, source_target_pairs={{0,1},{1,0},{2,3},{3,2},{4,5},{5,4},{6,7},{7,6},{8,9},{9,8},{10,11... | collective-permute-start | bytes 1966088 | tf_op jit(solution)/shard_map/ppermute | solution.py:546
  145.0 558.3 %all-gather.5.cloned.1.call-start = ((), (), s32[]{:S(2)}) async-start(), calls=%async_computation.1 | async-start | bytes 4325376 | tf_op jit(solution)/shard_map/all_gather | solution.py:1103
  145.1 36.1 %collective-permute-start.17 = (bf16[2,2,2,32,2560]{4,3,2,1,0:T(8,128)(2,1)}, bf16[2,2,2,32,2560]{4,3,2,1,0:T(8,128)(2,1)}, u32[]{:S(2)}, u32[]{:S(2)}) collective-permute-start(bf16[2,2,2,32,2560]{4,3,2,1,0:T(8,128)(2,1)} %pad_maximum_fusion.9), channel_id=1, source_target_pairs={{0,16},{16,0},{1,17},{17,1},{2,18},{18,2},{3,19},{19,3},{4,20},{20... | collective-permute-start | bytes 3932168 | tf_op jit(solution)/shard_map/ppermute | solution.py:546
  146.7 34.5 %collective-permute-start.18 = (bf16[2,2,2,32,2560]{4,3,2,1,0:T(8,128)(2,1)}, bf16[2,2,2,32,2560]{4,3,2,1,0:T(8,128)(2,1)}, u32[]{:S(2)}, u32[]{:S(2)}) collective-permute-start(bf16[2,2,2,32,2560]{4,3,2,1,0:T(8,128)(2,1)} %pad_maximum_fusion.10), channel_id=1, source_target_pairs={{0,1},{1,0},{2,3},{3,2},{4,5},{5,4},{6,7},{7,6},{8,9},{9,8},{10,11... | collective-permute-start | bytes 3932168 | tf_op jit(solution)/shard_map/ppermute | solution.py:546
  185.8 20.7 %collective-permute-start.19 = (bf16[2,2,2,2,32,2560]{5,4,3,2,1,0:T(8,128)(2,1)S(1)}, bf16[2,2,2,2,32,2560]{5,4,3,2,1,0:T(8,128)(2,1)S(1)}, u32[]{:S(2)}, u32[]{:S(2)}) collective-permute-start(bf16[2,2,2,2,32,2560]{5,4,3,2,1,0:T(8,128)(2,1)S(1)} %pad_maximum_fusion.1.left_own), channel_id=1, source_target_pairs={{0,8},{8,0},{1,9},{9,1},{2,10},{10,2},{3,11},{11,3},{4,12},{12,4},... | collective-permute-start | bytes 7864328 | tf_op jit(solution)/shard_map/ppermute | solution.py:546
  185.9 20.6 %collective-permute-start.20 = (bf16[2,2,2,2,32,2560]{5,4,3,2,1,0:T(8,128)(2,1)S(1)}, bf16[2,2,2,2,32,2560]{5,4,3,2,1,0:T(8,128)(2,1)S(1)}, u32[]{:S(2)}, u32[]{:S(2)}) collective-permute-start(bf16[2,2,2,2,32,2560]{5,4,3,2,1,0:T(8,128)(2,1)S(1)} %pad_maximum_fusion.2.right_own), channel_id=1, source_target_pairs={{0,8},{8,0},{1,9},{9,1},{2,10},{10,2},{3,11},{11,3},{4,12},{12,4},... | collective-permute-start | bytes 7864328 | tf_op jit(solution)/shard_map/ppermute | solution.py:546
  186.4 17.5 %collective-permute-start.21 = (bf16[2,2,32,2048]{3,2,1,0:T(8,128)(2,1)S(1)}, bf16[2,2,32,2048]{3,2,1,0:T(8,128)(2,1)S(1)}, u32[]{:S(2)}, u32[]{:S(2)}) collective-permute-start(bf16[2,2,32,2048]{3,2,1,0:T(8,128)(2,1)S(1)} %copy-done.87), channel_id=1, source_target_pairs={{0,1},{1,0},{2,3},{3,2},{4,5},{5,4},{6,7},{7,6},{8,9},{9,8},{10,11... | collective-permute-start | bytes 1572872 | tf_op jit(solution)/shard_map/ppermute | solution.py:546
  187.9 18.7 %collective-permute-start.22 = (bf16[2,2,32,2048]{3,2,1,0:T(8,128)(2,1)S(1)}, bf16[2,2,32,2048]{3,2,1,0:T(8,128)(2,1)S(1)}, u32[]{:S(2)}, u32[]{:S(2)}) collective-permute-start(bf16[2,2,32,2048]{3,2,1,0:T(8,128)(2,1)S(1)} %copy-done.86), channel_id=1, source_target_pairs={{0,16},{16,0},{1,17},{17,1},{2,18},{18,2},{3,19},{19,3},{4,20},{20... | collective-permute-start | bytes 1572872 | tf_op jit(solution)/shard_map/ppermute | solution.py:546
  210.1 30.8 %collective-permute-start.23 = (bf16[2,2,2,32,2048]{4,3,2,1,0:T(8,128)(2,1)}, bf16[2,2,2,32,2048]{4,3,2,1,0:T(8,128)(2,1)}, u32[]{:S(2)}, u32[]{:S(2)}) collective-permute-start(bf16[2,2,2,32,2048]{4,3,2,1,0:T(8,128)(2,1)} %pad_maximum_fusion.12), channel_id=1, source_target_pairs={{0,16},{16,0},{1,17},{17,1},{2,18},{18,2},{3,19},{19,3},{4,20},{20... | collective-permute-start | bytes 3145736 | tf_op jit(solution)/shard_map/ppermute | solution.py:546
  210.6 30.3 %collective-permute-start.24 = (bf16[2,2,2,32,2048]{4,3,2,1,0:T(8,128)(2,1)S(1)}, bf16[2,2,2,32,2048]{4,3,2,1,0:T(8,128)(2,1)}, u32[]{:S(2)}, u32[]{:S(2)}) collective-permute-start(bf16[2,2,2,32,2048]{4,3,2,1,0:T(8,128)(2,1)S(1)} %pad_maximum_fusion.13), channel_id=1, source_target_pairs={{0,1},{1,0},{2,3},{3,2},{4,5},{5,4},{6,7},{7,6},{8,9},{9,8},{10,11... | collective-permute-start | bytes 3145736 | tf_op jit(solution)/shard_map/ppermute | solution.py:546
  328.8 48.2 %collective-permute-start.30 = (bf16[1,512,4096]{2,1,0:T(8,128)(2,1)}, bf16[1,512,4096]{2,1,0:T(8,128)(2,1)}, u32[]{:S(2)}, u32[]{:S(2)}) collective-permute-start(bf16[1,512,4096]{2,1,0:T(8,128)(2,1)} %bitcast.492), channel_id=1, source_target_pairs={{0,8},{8,0},{1,9},{9,1},{2,10},{10,2},{3,11},{11,3},{4,12},{12,4},... | collective-permute-start | bytes 12582920 | tf_op jit(solution)/shard_map/ppermute | solution.py:546
  350.7 26.3 %collective-permute-start.28 = (bf16[1024,512]{1,0:T(8,128)(2,1)}, bf16[1024,512]{1,0:T(8,128)(2,1)}, u32[]{:S(2)}, u32[]{:S(2)}) collective-permute-start(bf16[1024,512]{1,0:T(8,128)(2,1)} %bitcast.73), channel_id=1, source_target_pairs={{0,16},{16,0},{1,17},{17,1},{2,18},{18,2},{3,19},{19,3},{4,20},{20... | collective-permute-start | bytes 3145736 | tf_op jit(solution)/shard_map/ppermute | solution.py:546
  352.3 25.4 %collective-permute-start.29 = (bf16[1024,512]{1,0:T(8,128)(2,1)}, bf16[1024,512]{1,0:T(8,128)(2,1)}, u32[]{:S(2)}, u32[]{:S(2)}) collective-permute-start(bf16[1024,512]{1,0:T(8,128)(2,1)} %bitcast.74), channel_id=1, source_target_pairs={{0,1},{1,0},{2,3},{3,2},{4,5},{5,4},{6,7},{7,6},{8,9},{9,8},{10,11... | collective-permute-start | bytes 3145736 | tf_op jit(solution)/shard_map/ppermute | solution.py:546
  393.0 36.0 %collective-permute-start.33 = (bf16[256,2048]{1,0:T(8,128)(2,1)}, bf16[256,2048]{1,0:T(8,128)(2,1)}, u32[]{:S(2)}, u32[]{:S(2)}) collective-permute-start(bf16[256,2048]{1,0:T(8,128)(2,1)} %bitcast.84), channel_id=1, source_target_pairs={{0,16},{16,0},{1,17},{17,1},{2,18},{18,2},{3,19},{19,3},{4,20},{20... | collective-permute-start | bytes 3145736 | tf_op jit(solution)/shard_map/ppermute | solution.py:546
  393.3 35.6 %collective-permute-start.34 = (bf16[256,2048]{1,0:T(8,128)(2,1)}, bf16[256,2048]{1,0:T(8,128)(2,1)}, u32[]{:S(2)}, u32[]{:S(2)}) collective-permute-start(bf16[256,2048]{1,0:T(8,128)(2,1)} %bitcast.85), channel_id=1, source_target_pairs={{0,1},{1,0},{2,3},{3,2},{4,5},{5,4},{6,7},{7,6},{8,9},{9,8},{10,11... | collective-permute-start | bytes 3145736 | tf_op jit(solution)/shard_map/ppermute | solution.py:546
  397.8 31.1 %collective-permute-start.31 = (bf16[512,512]{1,0:T(8,128)(2,1)}, bf16[512,512]{1,0:T(8,128)(2,1)S(1)}, u32[]{:S(2)}, u32[]{:S(2)}) collective-permute-start(bf16[512,512]{1,0:T(8,128)(2,1)} %bitcast.78), channel_id=1, source_target_pairs={{0,1},{1,0},{2,3},{3,2},{4,5},{5,4},{6,7},{7,6},{8,9},{9,8},{10,11... | collective-permute-start | bytes 1572872 | tf_op jit(solution)/shard_map/ppermute | solution.py:546
  398.1 30.8 %collective-permute-start.32 = (bf16[512,512]{1,0:T(8,128)(2,1)}, bf16[512,512]{1,0:T(8,128)(2,1)S(1)}, u32[]{:S(2)}, u32[]{:S(2)}) collective-permute-start(bf16[512,512]{1,0:T(8,128)(2,1)} %bitcast.81), channel_id=1, source_target_pairs={{0,16},{16,0},{1,17},{17,1},{2,18},{18,2},{3,19},{19,3},{4,20},{20... | collective-permute-start | bytes 1572872 | tf_op jit(solution)/shard_map/ppermute | solution.py:546
  435.9 20.4 %collective-permute-start.35 = (bf16[5,512,1024]{2,1,0:T(8,128)(2,1)}, bf16[5,512,1024]{2,1,0:T(8,128)(2,1)}, u32[]{:S(2)}, u32[]{:S(2)}) collective-permute-start(bf16[5,512,1024]{2,1,0:T(8,128)(2,1)} %half_products.4), channel_id=1, source_target_pairs={{0,8},{8,0},{1,9},{9,1},{2,10},{10,2},{3,11},{11,3},{4,12},{12,4},... | collective-permute-start | bytes 15728648 | tf_op jit(solution)/shard_map/ppermute | solution.py:546
  452.5 65.3 %collective-permute-start.36 = (bf16[128,2048]{1,0:T(8,128)(2,1)}, bf16[128,2048]{1,0:T(8,128)(2,1)}, u32[]{:S(2)}, u32[]{:S(2)}) collective-permute-start(bf16[128,2048]{1,0:T(8,128)(2,1)} %bitcast.93), channel_id=1, source_target_pairs={{0,1},{1,0},{2,3},{3,2},{4,5},{5,4},{6,7},{7,6},{8,9},{9,8},{10,11... | collective-permute-start | bytes 1572872 | tf_op jit(solution)/shard_map/ppermute | solution.py:546
  454.0 63.8 %collective-permute-start.37 = (bf16[128,2048]{1,0:T(8,128)(2,1)}, bf16[128,2048]{1,0:T(8,128)(2,1)}, u32[]{:S(2)}, u32[]{:S(2)}) collective-permute-start(bf16[128,2048]{1,0:T(8,128)(2,1)} %bitcast.96), channel_id=1, source_target_pairs={{0,16},{16,0},{1,17},{17,1},{2,18},{18,2},{3,19},{19,3},{4,20},{20... | collective-permute-start | bytes 1572872 | tf_op jit(solution)/shard_map/ppermute | solution.py:546
  455.5 62.3 %collective-permute-start.40 = (bf16[256,1024]{1,0:T(8,128)(2,1)}, bf16[256,1024]{1,0:T(8,128)(2,1)}, u32[]{:S(2)}, u32[]{:S(2)}) collective-permute-start(bf16[256,1024]{1,0:T(8,128)(2,1)} %bitcast.90), channel_id=1, source_target_pairs={{0,2},{2,0},{1,3},{3,1},{4,6},{6,4},{5,7},{7,5},{8,10},{10,8},{9,1... | collective-permute-start | bytes 1572872 | tf_op jit(solution)/shard_map/ppermute | solution.py:546
  470.6 47.2 %collective-permute-start.38 = (bf16[1280,512]{1,0:T(8,128)(2,1)}, bf16[1280,512]{1,0:T(8,128)(2,1)}, u32[]{:S(2)}, u32[]{:S(2)}) collective-permute-start(bf16[1280,512]{1,0:T(8,128)(2,1)} %bitcast.118), channel_id=1, source_target_pairs={{0,16},{16,0},{1,17},{17,1},{2,18},{18,2},{3,19},{19,3},{4,20},{20... | collective-permute-start | bytes 3932168 | tf_op jit(solution)/shard_map/ppermute | solution.py:546
  471.3 46.6 %collective-permute-start.39 = (bf16[1280,512]{1,0:T(8,128)(2,1)}, bf16[1280,512]{1,0:T(8,128)(2,1)}, u32[]{:S(2)}, u32[]{:S(2)}) collective-permute-start(bf16[1280,512]{1,0:T(8,128)(2,1)} %bitcast.119), channel_id=1, source_target_pairs={{0,1},{1,0},{2,3},{3,2},{4,5},{5,4},{6,7},{7,6},{8,9},{9,8},{10,11... | collective-permute-start | bytes 3932168 | tf_op jit(solution)/shard_map/ppermute | solution.py:546
  528.9 40.0 %collective-permute-start.45 = (bf16[512,1024]{1,0:T(8,128)(2,1)}, bf16[512,1024]{1,0:T(8,128)(2,1)}, u32[]{:S(2)}, u32[]{:S(2)}) collective-permute-start(bf16[512,1024]{1,0:T(8,128)(2,1)} %bitcast.136), channel_id=1, source_target_pairs={{0,1},{1,0},{2,3},{3,2},{4,5},{5,4},{6,7},{7,6},{8,9},{9,8},{10,11... | collective-permute-start | bytes 3145736 | tf_op jit(solution)/shard_map/ppermute | solution.py:546
  531.5 37.3 %collective-permute-start.43 = (bf16[640,512]{1,0:T(8,128)(2,1)}, bf16[640,512]{1,0:T(8,128)(2,1)S(1)}, u32[]{:S(2)}, u32[]{:S(2)}) collective-permute-start(bf16[640,512]{1,0:T(8,128)(2,1)} %bitcast.128), channel_id=1, source_target_pairs={{0,1},{1,0},{2,3},{3,2},{4,5},{5,4},{6,7},{7,6},{8,9},{9,8},{10,11... | collective-permute-start | bytes 1966088 | tf_op jit(solution)/shard_map/ppermute | solution.py:546
  532.3 36.6 %collective-permute-start.44 = (bf16[640,512]{1,0:T(8,128)(2,1)}, bf16[640,512]{1,0:T(8,128)(2,1)S(1)}, u32[]{:S(2)}, u32[]{:S(2)}) collective-permute-start(bf16[640,512]{1,0:T(8,128)(2,1)} %bitcast.131), channel_id=1, source_target_pairs={{0,16},{16,0},{1,17},{17,1},{2,18},{18,2},{3,19},{19,3},{4,20},{20... | collective-permute-start | bytes 1966088 | tf_op jit(solution)/shard_map/ppermute | solution.py:546
  533.8 35.0 %collective-permute-start.42 = (bf16[64,4096]{1,0:T(8,128)(2,1)}, bf16[64,4096]{1,0:T(8,128)(2,1)S(1)}, u32[]{:S(2)}, u32[]{:S(2)}) collective-permute-start(bf16[64,4096]{1,0:T(8,128)(2,1)} %bitcast.125), channel_id=1, source_target_pairs={{0,2},{2,0},{1,3},{3,1},{4,6},{6,4},{5,7},{7,5},{8,10},{10,8},{9,1... | collective-permute-start | bytes 1572872 | tf_op jit(solution)/shard_map/ppermute | solution.py:546
  574.9 33.6 %collective-permute-start.46 = (bf16[320,1024]{1,0:T(8,128)(2,1)S(1)}, bf16[320,1024]{1,0:T(8,128)(2,1)S(1)}, u32[]{:S(2)}, u32[]{:S(2)}) collective-permute-start(bf16[320,1024]{1,0:T(8,128)(2,1)S(1)} %bitcast.435), channel_id=1, source_target_pairs={{0,2},{2,0},{1,3},{3,1},{4,6},{6,4},{5,7},{7,5},{8,10},{10,8},{9,1... | collective-permute-start | bytes 1966088 | tf_op jit(solution)/shard_map/ppermute | solution.py:546
  575.0 33.5 %collective-permute-start.47 = (bf16[256,1024]{1,0:T(8,128)(2,1)S(1)}, bf16[256,1024]{1,0:T(8,128)(2,1)S(1)}, u32[]{:S(2)}, u32[]{:S(2)}) collective-permute-start(bf16[256,1024]{1,0:T(8,128)(2,1)S(1)} %bitcast.445), channel_id=1, source_target_pairs={{0,2},{2,0},{1,3},{3,1},{4,6},{6,4},{5,7},{7,5},{8,10},{10,8},{9,1... | collective-permute-start | bytes 1572872 | tf_op jit(solution)/shard_map/ppermute | solution.py:546
  577.0 29.3 %collective-permute-start.48 = (bf16[32,4096]{1,0:T(8,128)(2,1)S(1)}, bf16[32,4096]{1,0:T(8,128)(2,1)S(1)}, u32[]{:S(2)}, u32[]{:S(2)}) collective-permute-start(bf16[32,4096]{1,0:T(8,128)(2,1)S(1)} %dynamic-slice_bitcast_fusion.2), channel_id=1, source_target_pairs={{0,4},{4,0},{1,5},{5,1},{2,6},{6,2},{3,7},{7,3},{8,12},{12,8},{9,1... | collective-permute-start | bytes 786440 | tf_op jit(solution)/shard_map/ppermute | solution.py:546
  610.7 18.3 %collective-permute-start.49 = (bf16[3,512,1024]{2,1,0:T(8,128)(2,1)}, bf16[3,512,1024]{2,1,0:T(8,128)(2,1)}, u32[]{:S(2)}, u32[]{:S(2)}) collective-permute-start(bf16[3,512,1024]{2,1,0:T(8,128)(2,1)} %half_products.6), channel_id=1, source_target_pairs={{0,8},{8,0},{1,9},{9,1},{2,10},{10,2},{3,11},{11,3},{4,12},{12,4},... | collective-permute-start | bytes 9437192 | tf_op jit(solution)/shard_map/ppermute | solution.py:546
  620.6 33.3 %collective-permute-start.53 = (bf16[160,1024]{1,0:T(8,128)(2,1)S(1)}, bf16[160,1024]{1,0:T(8,128)(2,1)S(1)}, u32[]{:S(2)}, u32[]{:S(2)}) collective-permute-start(bf16[160,1024]{1,0:T(8,128)(2,1)S(1)} %bitcast.458), channel_id=1, source_target_pairs={{0,4},{4,0},{1,5},{5,1},{2,6},{6,2},{3,7},{7,3},{8,12},{12,8},{9,1... | collective-permute-start | bytes 983048 | tf_op jit(solution)/shard_map/ppermute | solution.py:546
  622.5 31.4 %collective-permute-start.54 = (bf16[128,1024]{1,0:T(8,128)(2,1)S(1)}, bf16[128,1024]{1,0:T(8,128)(2,1)S(1)}, u32[]{:S(2)}, u32[]{:S(2)}) collective-permute-start(bf16[128,1024]{1,0:T(8,128)(2,1)S(1)} %copy-done.98), channel_id=1, source_target_pairs={{0,4},{4,0},{1,5},{5,1},{2,6},{6,2},{3,7},{7,3},{8,12},{12,8},{9,1... | collective-permute-start | bytes 786440 | tf_op jit(solution)/shard_map/ppermute | solution.py:546
  640.4 23.0 %collective-permute-start.51 = (bf16[768,512]{1,0:T(8,128)(2,1)S(1)}, bf16[768,512]{1,0:T(8,128)(2,1)S(1)}, u32[]{:S(2)}, u32[]{:S(2)}) collective-permute-start(bf16[768,512]{1,0:T(8,128)(2,1)S(1)} %bitcast.424), channel_id=1, source_target_pairs={{0,16},{16,0},{1,17},{17,1},{2,18},{18,2},{3,19},{19,3},{4,20},{20... | collective-permute-start | bytes 2359304 | tf_op jit(solution)/shard_map/ppermute | solution.py:546
  641.2 22.3 %collective-permute-start.52 = (bf16[768,512]{1,0:T(8,128)(2,1)S(1)}, bf16[768,512]{1,0:T(8,128)(2,1)S(1)}, u32[]{:S(2)}, u32[]{:S(2)}) collective-permute-start(bf16[768,512]{1,0:T(8,128)(2,1)S(1)} %bitcast.426), channel_id=1, source_target_pairs={{0,1},{1,0},{2,3},{3,2},{4,5},{5,4},{6,7},{7,6},{8,9},{9,8},{10,11... | collective-permute-start | bytes 2359304 | tf_op jit(solution)/shard_map/ppermute | solution.py:546
  643.1 24.8 %collective-permute-start.57 = (bf16[128,1024]{1,0:T(8,128)(2,1)S(1)}, bf16[128,1024]{1,0:T(8,128)(2,1)S(1)}, u32[]{:S(2)}, u32[]{:S(2)}) collective-permute-start(bf16[128,1024]{1,0:T(8,128)(2,1)S(1)} %bitcast.461), channel_id=1, source_target_pairs={{0,2},{2,0},{1,3},{3,1},{4,6},{6,4},{5,7},{7,5},{8,10},{10,8},{9,1... | collective-permute-start | bytes 786440 | tf_op jit(solution)/shard_map/ppermute | solution.py:546
  665.4 16.8 %collective-permute-start.56 = (bf16[384,512]{1,0:T(8,128)(2,1)S(1)}, bf16[384,512]{1,0:T(8,128)(2,1)S(1)}, u32[]{:S(2)}, u32[]{:S(2)}) collective-permute-start(bf16[384,512]{1,0:T(8,128)(2,1)S(1)} %bitcast.450), channel_id=1, source_target_pairs={{0,16},{16,0},{1,17},{17,1},{2,18},{18,2},{3,19},{19,3},{4,20},{20... | collective-permute-start | bytes 1179656 | tf_op jit(solution)/shard_map/ppermute | solution.py:546
  (135 other events, 1091.3 us)
Sparse Core Ops, SparseCore 0:
  145.1 89.6 all-gather.2
  612.3 81.8 all-gather.4

commit v4 on v3

--- a/solution.py
+++ b/solution.py
@@ -1022,7 +1022,7 @@
     grad_two, gain_two, shift_two = layer_norm_back(resid_two, gains[1], grad_hidden_two)
     grad_cross = grad_two.astype(bf16)
     grad_cattn = product_nt(grad_cross, w_co).astype(bf16)
-    grad_cattn = advance(grad_cattn, down_sum)
+    grad_cattn = advance(grad_cattn, down_sum, up_sum)
     cross_gq, cross_gk, cross_gv = attend_backward(
         None,
         cross_queries,
@@ -1035,7 +1035,6 @@
         512,
         (0,),
     )
-    cross_gq = advance(cross_gq, down_sum, up_sum)
     grad_cq = (cross_gq.astype(f32) * scale).astype(bf16)
     enc_back = product_nt(cross_gk[0], w_ckv[:, :width]) + product_nt(
         cross_gv[0], w_ckv[:, width:]
@@ -1082,7 +1081,7 @@
         0,
     )
     grad_attn, small_part = lax.optimization_barrier((grad_attn, small_part))
-    grad_attn = advance(grad_attn, mid_sum)
+    grad_attn = advance(grad_attn, mid_sum, down_sum, up_sum)
     self_args = (queries, grad_attn, attn, self_log, [prompt_kv, cont_kv], plan, prompt_rows)
     part_gq, prompt_gk, prompt_gv = attend_backward(scalars, *self_args, 1024, (0,))
     prompt_gk, prompt_gv = prompt_gk[0], prompt_gv[0]
@@ -1090,9 +1089,10 @@
     part_gq = advance(part_gq, up_sum, mid_sum, down_sum)
     prompt_sum = links.row_sum(product_nt(prompt_gk, w_k) + product_nt(prompt_gv, w_v))
     part_gq = begin(part_gq, prompt_sum)
+    part_gq = advance(part_gq, down_sum, up_sum)
     self_gq, cont_gk, cont_gv = attend_backward(scalars, *self_args, 512, (1,), part_gq)
     cont_gk, cont_gv = cont_gk[0], cont_gv[0]
-    self_gq = advance(self_gq, down_sum, up_sum, mid_sum, prompt_sum)
+    self_gq = advance(self_gq, mid_sum, prompt_sum)
     self_gq = begin(self_gq, enc_sum)
     grad_q = (self_gq.astype(f32) * scale).astype(bf16)
 
@@ -1112,12 +1112,12 @@
     cont_grad = input_grad[prompt_rows:] + product_nt(cont_gk, w_k) + product_nt(cont_gv, w_v)
     if links.fast:
         cont_grad, self_sum.other = advance(
-            (cont_grad, self_sum.other), mid_sum, prompt_sum, up_sum
+            (cont_grad, self_sum.other), mid_sum, prompt_sum, enc_sum
         )
     cont_grad = begin(cont_grad, self_sum)
-    cont_grad = advance(cont_grad, self_sum, enc_sum)
-    cont_grad = advance(cont_grad, self_sum, mid_sum, prompt_sum)
-    cont_grad = advance(cont_grad, self_sum, enc_sum)
+    cont_grad = advance(cont_grad, self_sum)
+    cont_grad = advance(cont_grad, self_sum, mid_sum, prompt_sum, enc_sum)
+    cont_grad = advance(cont_grad, self_sum)
     cont_grad = advance(cont_grad, self_sum, enc_sum)
     cont_grad = cont_grad[None, None]
     prompt_grad = (input_grad[:prompt_rows] + prompt_sum.finish())[None]

time: 721 us -> 716 us (level)
    unnamed x243 -> x251, local copies, waits for them, and re-layouts: 17.4 us -> 17.3 us
  transfers between devices with their start and end apart: 63 -> 63, of which waited for: 28 -> 33; matrix products, arithmetic and copies ran while one was open for 19% -> 18% of each run, Pallas kernels for 24% -> 23%
where the time goes in v4:
time: 716 us; the launch traced here: 711 us
  Pallas kernels  224 us (31%)
  waiting for transfers between devices  185 us (26%)
  other arithmetic  97.2 us (14%)
  starting transfers between devices  65.6 us (9%)
  local copies, waits for them, and re-layouts  65.1 us (9%)
  matrix products  56 us (8%)
  between operations  17.7 us (2%)
    ppermute x61, waiting for transfers between devices, swap(): return lax.ppermute(value, axis, SWAP)  185 us
    pallas_call x3, Pallas kernels, attend_backward(): pl.pallas_call(functools.partial(bwd_kernel, plan, masked, slot_at, key_s...  74 us
    ppermute x61, starting transfers between devices, swap(): return lax.ppermute(value, axis, SWAP)  65.5 us
    pallas_call x2, Pallas kernels, attend_forward(): pl.pallas_call(functools.partial(fwd_kernel, plan, masked, slot_at), grid...  40.3 us
    pallas_call x1, Pallas kernels, ffn_backward(): pl.pallas_call(ffn_backward_kernel, grid_spec=pltpu.PrefetchScalarGridSpe...  33.9 us
    dot_general x10, matrix products, product_nt(): lax.dot_general(first_mat, second_mat, (((1,), (1,)), ((), ())), preferre...  32.5 us
    pallas_call x4, Pallas kernels, half_products(): pl.pallas_call(functools.partial(half_products_kernel, tuple((len(pairs)...  31.6 us
    dot_general x7, matrix products, product(): return jnp.dot(first_mat, second_mat, preferred_element_type=jnp.float32)  23.6 us
  transfers between devices with their start and end apart: 63, of which 33 were waited for; matrix products, arithmetic and copies ran while one was open for 18% of the time, Pallas kernels for 23%

profile of v4, /device:TPU:0, one launch (start us, length us, event | category | flops | bytes accessed | tf_op | source)
XLA Modules:
  0.0 710.9 jit_solution(14338363446053642688)
XLA Ops:
  9.5 4.1 collective-permute-start
  13.7 18.6 %collective-permute-done = bf16[32,3200]{1,0:T(8,128)(2,1)S(1)} collective-permute-done((bf16[32,3200]{1,0:T(8,128)(2,1)S(1)}, bf16[32,3200]{1,0:T(8,128)(2,1)S(1)}, u32[]{:S(2)}, u32[]{:S(2)}) %collective-permute-start) | collective-permute-done | bytes 204832 | tf_op jit(solution)/shard_map/ppermute | solution.py:546
  32.6 7.5 %collective-permute-done.1 = bf16[192,1024]{1,0:T(8,128)(2,1)S(1)} collective-permute-done((bf16[192,1024]{1,0:T(8,128)(2,1)S(1)}, bf16[192,1024]{1,0:T(8,128)(2,1)S(1)}, u32[]{:S(2)}, u32[]{:S(2)}) %collective-permute-start.1) | collective-permute-done | bytes 393248 | tf_op jit(solution)/shard_map/ppermute | solution.py:546
  40.9 8.0 %collective-permute-done.2 = bf16[2,32,3200]{2,1,0:T(8,128)(2,1)S(1)} collective-permute-done((bf16[2,32,3200]{2,1,0:T(8,128)(2,1)S(1)}, bf16[2,32,3200]{2,1,0:T(8,128)(2,1)S(1)}, u32[]{:S(2)}, u32[]{:S(2)}) %collective-permute-start.2) | collective-permute-done | bytes 409632 | tf_op jit(solution)/shard_map/ppermute | solution.py:546
  53.8 7.5 %collective-permute-done.4 = bf16[2,2,32,1536]{3,2,1,0:T(8,128)(2,1)S(1)} collective-permute-done((bf16[2,2,32,1536]{3,2,1,0:T(8,128)(2,1)S(1)}, bf16[2,2,32,1536]{3,2,1,0:T(8,128)(2,1)S(1)}, u32[]{:S(2)}, u32[]{:S(2)}) %collective-permute-start.4) | collective-permute-done | bytes 393248 | tf_op jit(solution)/shard_map/ppermute | solution.py:546
  64.0 5.3 collective-permute-done.6
  74.8 6.1 collective-permute-done.8
  85.7 4.0 collective-permute-start.12
  89.8 7.3 %assemble.3 = (bf16[1024,3072]{1,0:T(8,128)(2,1)}, bf16[1024,128]{1,0:T(8,128)(2,1)S(1)}) custom-call(s32[5]{0:T(128)S(1)} %stack.333.place_ref, bf16[2,2,2,2,32,1664]{5,4,3,2,1,0:T(8,128)(2,1)S(1)} %pad_maximum_fusion.5.left_own, bf16[2,2,2,2,32,1536]{5,4,3,2,1,0:T(8,128)(2,1)} %pad_maximum_fusion.7.right_own, ...), custom_call_target="tpu_custom_call" | custom-call | bytes 13107200 | tf_op jit(solution)/shard_map/assemble/pallas_call | solution.py:745
  97.1 3.5 slice_reduce_fusion.1
  107.1 12.8 %collective-permute-done.13 = bf16[2,2,192,1024]{3,2,1,0:T(8,128)(2,1)S(1)} collective-permute-done((bf16[2,2,192,1024]{3,2,1,0:T(8,128)(2,1)}, bf16[2,2,192,1024]{3,2,1,0:T(8,128)(2,1)S(1)}, u32[]{:S(2)}, u32[]{:S(2)}) %collective-permute-start.13) | collective-permute-done | bytes 1572896 | tf_op jit(solution)/shard_map/ppermute | solution.py:546
  129.0 6.1 add_convert_fusion.refs_2_.refs_4_.refs_5_.refs_6_
  135.1 4.7 collective-permute-done.16
  151.1 29.5 %attend_forward.2 = (bf16[640,1024]{1,0:T(8,128)(2,1)S(1)}, f32[640,128]{1,0:T(8,128)S(1)}) custom-call(s32[3]{0:T(128)S(1)} %pad_add_fusion.refs_0_, bf16[640,1024]{1,0:T(8,128)(2,1)S(1)} %copy-done.15, bf16[1024,2048]{1,0:T(8,128)(2,1)} %add_convert_fusion.refs_2_.refs_4_.refs_5_.refs_6_, bf16[512,2048]{1,0:T(8,128)(2,1)S(1)} %add_convert_fusion.3.refs_3_.refs_5_.refs_6_, ...), custom_call_target="tpu_custom_call" | custom-call | flops 1 | bytes 1 | tf_op jit(solution)/shard_map/attend_forward/pallas_call | solution.py:227
  187.8 14.7 %collective-permute-done.21 = bf16[2,2,32,2048]{3,2,1,0:T(8,128)(2,1)S(1)} collective-permute-done((bf16[2,2,32,2048]{3,2,1,0:T(8,128)(2,1)S(1)}, bf16[2,2,32,2048]{3,2,1,0:T(8,128)(2,1)S(1)}, u32[]{:S(2)}, u32[]{:S(2)}) %collective-permute-start.21) | collective-permute-done | bytes 524320 | tf_op jit(solution)/shard_map/ppermute | solution.py:546
  207.5 8.2 %assemble.4 = (bf16[1024,1024]{1,0:T(8,128)(2,1)S(1)}, bf16[1024,1024]{1,0:T(8,128)(2,1)S(1)}, bf16[1024,2048]{1,0:T(8,128)(2,1)}, bf16[1024,1024]{1,0:T(8,128)(2,1)}) custom-call(s32[5]{0:T(128)S(1)} %stack.333.place_ref, bf16[2,2,2,2,32,2560]{5,4,3,2,1,0:T(8,128)(2,1)} %copy-done.43, bf16[2,2,2,2,32,2560]{5,4,3,2,1,0:T(8,128)(2,1)} %copy-done.42, ...), custom_call_target="tpu_custom_call" | custom-call | bytes 20971520 | tf_op jit(solution)/shard_map/assemble/pallas_call | solution.py:745
  226.7 10.8 %attend_forward.3 = (bf16[640,1024]{1,0:T(8,128)(2,1)S(1)}, f32[640,128]{1,0:T(8,128)S(1)}) custom-call(bf16[640,1024]{1,0:T(8,128)(2,1)S(1)} %multiply_convert_fusion.2.refs_0_, bf16[512,2048]{1,0:T(8,128)(2,1)S(1)} %add_convert_fusion.2.refs_1_.refs_2_.refs_4_.refs_5_, bf16[512,2048]{1,0:T(8,128)(2,1)S(1)} %add_convert_fusion.2.refs_1_.refs_2_.refs_4_.refs_5_), custom_call_target="tpu_custom_call" | custom-call | flops 1 | bytes 1 | tf_op jit(solution)/shard_map/attend_forward/pallas_call | solution.py:227
  245.8 5.5 fusion.99
  252.8 8.0 %assemble.5.up_ref = bf16[1024,4096]{1,0:T(8,128)(2,1)} custom-call(s32[5]{0:T(128)S(1)} %stack.333.place_ref, bf16[2,2,2,2,32,2048]{5,4,3,2,1,0:T(8,128)(2,1)} %pad_maximum_fusion.3.left_own, bf16[2,2,2,2,32,2048]{5,4,3,2,1,0:T(8,128)(2,1)} %pad_maximum_fusion.4.right_own, bf16[2,2,2,2,32,2048]{5,4,3,2,1,0:T(8,128)(2,1)} %collective-permute-done.25.left_came, ...), custom_call_target="tpu_custom_call" | custom-call | bytes 16777216 | tf_op jit(solution)/shard_map/assemble/pallas_call | solution.py:745
  260.8 18.4 %ffn_forward.1 = (bf16[640,4096]{1,0:T(8,128)(2,1)}, bf16[640,4096]{1,0:T(8,128)(2,1)}, f32[640,1024]{1,0:T(8,128)S(1)}) custom-call(bf16[640,1024]{1,0:T(8,128)(2,1)S(1)} %add_convert_fusion.5.h_ref, bf16[1024,4096]{1,0:T(8,128)(2,1)} %assemble.5.up_ref, f32[1,4096]{1,0:T(1,128)S(1)} %reshape_reshape.3.bias_ref, ...), custom_call_target="tpu_custom_call" | custom-call | flops 1 | bytes 1 | tf_op jit(solution)/shard_map/ffn_forward/pallas_call | solution.py:322
  279.3 3.5 multiply_reduce_fusion.2
  288.6 33.9 %ffn_backward.1 = (bf16[2048,1024]{1,0:T(8,128)(2,1)}, bf16[2048,1024]{1,0:T(8,128)(2,1)}, bf16[512,4096]{1,0:T(8,128)(2,1)}, bf16[512,4096]{1,0:T(8,128)(2,1)},...) custom-call(s32[1]{0:T(128)} %bitcast.30.core_ref, bf16[640,1024]{1,0:T(8,128)(2,1)S(1)} %get-tuple-element.479.g_ref, ...), custom_call_target="tpu_custom_call" | custom-call | flops 1 | bytes 1 | tf_op jit(solution)/shard_map/ffn_backward/pallas_call | solution.py:417
  324.6 7.8 %multiply_reduce_fusion = (f32[1024]{0:T(1024)}, f32[640]{0:T(1024)S(1)}, f32[640]{0:T(1024)S(1)}, f32[1024]{0:T(1024)}, f32[640,1024]{1,0:T(8,128)S(1)}, /*index=5*/bf16[640,1024]{1,0:T(8,128)(2,1)}) fusion(f32[640,1024]{1,0:T(8,128)} %copy-done.37, f32[640]{0:T(1024)S(1)} %add_rsqrt_fusion.1, f32[640]{0:T(1024)S(1)} %broadcast_multiply_fusion.7, ...), kind=kLoop, calls=%fused_computation.43 | loop fusion | flops 15725312 | bytes 13148160 | tf_op jit(solution)/shard_map/reduce_sum | solution.py:539
  338.0 3.7 fusion
  345.4 4.3 fusion.1
  358.7 21.0 %attend_backward.3 = (bf16[640,1024]{1,0:T(8,128)(2,1)S(1)}, bf16[512,1024]{1,0:T(8,128)(2,1)S(1)}, bf16[512,1024]{1,0:T(8,128)(2,1)S(1)}) custom-call(bf16[640,1024]{1,0:T(8,128)(2,1)S(1)} %copy-done.23, bf16[640,1024]{1,0:T(8,128)(2,1)S(1)} %convolution_convert_fusion.1.refs_1_, bf16[640,1024]{1,0:T(8,128)(2,1)} %copy-done.8, ...), custom_call_target="tpu_custom_call" | custom-call | flops 1 | bytes 1 | tf_op jit(solution)/shard_map/attend_backward/pallas_call | solution.py:272
  379.8 5.3 multiply_reduce_fusion.1
  389.8 6.8 half_products.4
  396.7 5.8 collective-permute-done.31
  427.1 4.1 concatenate.59
  431.2 3.7 convolution_convert_fusion.refs_2_
  438.3 9.1 %collective-permute-done.36 = bf16[128,2048]{1,0:T(8,128)(2,1)} collective-permute-done((bf16[128,2048]{1,0:T(8,128)(2,1)}, bf16[128,2048]{1,0:T(8,128)(2,1)}, u32[]{:S(2)}, u32[]{:S(2)}) %collective-permute-start.36) | collective-permute-done | bytes 524320 | tf_op jit(solution)/shard_map/ppermute | solution.py:546
  454.6 8.4 %half_products.5 = bf16[5,512,1024]{2,1,0:T(8,128)(2,1)} custom-call(s32[1]{0:T(128)} %bitcast.30.core_ref, bf16[640,1024]{1,0:T(8,128)(2,1)S(1)} %copy-done.10, bf16[640,1024]{1,0:T(8,128)(2,1)S(1)} %copy-done.12, bf16[640,1024]{1,0:T(8,128)(2,1)} %copy-done.41, bf16[640,1024]{1,0:T(8,128)(2,1)} %get-tuple-element.512.refs_3_, bf16[640,1024]{1,0:T(8,128)(2,1)} %copy-done.3, ...), custom_call_target="tpu_custom_call" | custom-call | flops 1 | bytes 1 | tf_op jit(solution)/shard_map/half_products/pallas_call | solution.py:500
  474.1 35.5 %attend_backward.4 = (f32[640,1024]{1,0:T(8,128)}, bf16[1024,1024]{1,0:T(8,128)(2,1)S(1)}, bf16[1024,1024]{1,0:T(8,128)(2,1)}) custom-call(s32[3]{0:T(128)S(1)} %pad_add_fusion.refs_0_, bf16[640,1024]{1,0:T(8,128)(2,1)S(1)} %copy-done.16, bf16[640,1024]{1,0:T(8,128)(2,1)S(1)} %convolution_convert_fusion.refs_2_, bf16[640,1024]{1,0:T(8,128)(2,1)S(1)} %copy-done.4, ...), custom_call_target="tpu_custom_call" | custom-call | flops 1 | bytes 1 | tf_op jit(solution)/shard_map/attend_backward/pallas_call | solution.py:272
  509.6 4.8 fusion.37
  514.4 4.0 add_convert_fusion.1
  529.8 4.2 collective-permute-start.42
  539.5 10.6 %collective-permute-done.42 = bf16[128,1024]{1,0:T(8,128)(2,1)S(1)} collective-permute-done((bf16[128,1024]{1,0:T(8,128)(2,1)S(1)}, bf16[128,1024]{1,0:T(8,128)(2,1)S(1)}, u32[]{:S(2)}, u32[]{:S(2)}) %collective-permute-start.42) | collective-permute-done | bytes 262176 | tf_op jit(solution)/shard_map/ppermute | solution.py:546
  550.9 4.9 collective-permute-done.43
  555.8 17.5 %attend_backward.5 = (bf16[640,1024]{1,0:T(8,128)(2,1)S(1)}, bf16[512,1024]{1,0:T(8,128)(2,1)S(1)}, bf16[512,1024]{1,0:T(8,128)(2,1)S(1)}) custom-call(s32[3]{0:T(128)S(1)} %pad_add_fusion.refs_0_, bf16[640,1024]{1,0:T(8,128)(2,1)S(1)} %copy-done.16, bf16[640,1024]{1,0:T(8,128)(2,1)S(1)} %convolution_convert_fusion.refs_2_, bf16[640,1024]{1,0:T(8,128)(2,1)} %copy-done.3, ...), custom_call_target="tpu_custom_call" | custom-call | flops 1 | bytes 1 | tf_op jit(solution)/shard_map/attend_backward/pallas_call | solution.py:272
  588.9 7.8 %half_products.6 = bf16[3,512,1024]{2,1,0:T(8,128)(2,1)} custom-call(s32[1]{0:T(128)S(6)} %sub.98.core_ref, bf16[640,1024]{1,0:T(8,128)(2,1)S(1)} %pad_maximum_fusion.8.refs_0_, bf16[640,1024]{1,0:T(8,128)(2,1)S(1)} %get-tuple-element.510.refs_1_, bf16[1024,1024]{1,0:T(8,128)(2,1)} %copy-done.1, bf16[1024,1024]{1,0:T(8,128)(2,1)} %copy-done.21, ...), custom_call_target="tpu_custom_call" | custom-call | flops 1 | bytes 1 | tf_op jit(solution)/shard_map/half_products/pallas_call | solution.py:500
  596.7 4.2 fusion.22
  600.9 8.7 %collective-permute-done.48 = bf16[256,1024]{1,0:T(8,128)(2,1)S(1)} collective-permute-done((bf16[256,1024]{1,0:T(8,128)(2,1)}, bf16[256,1024]{1,0:T(8,128)(2,1)S(1)}, u32[]{:S(2)}, u32[]{:S(2)}) %collective-permute-start.48) | collective-permute-done | bytes 524320 | tf_op jit(solution)/shard_map/ppermute | solution.py:546
  624.1 8.7 %half_products.7 = bf16[3,512,1024]{2,1,0:T(8,128)(2,1)} custom-call(s32[1]{0:T(128)} %bitcast.30.core_ref, bf16[640,1024]{1,0:T(8,128)(2,1)S(1)} %pad_maximum_fusion.8.refs_0_, bf16[640,1024]{1,0:T(8,128)(2,1)S(1)} %copy-done.14, bf16[1024,1024]{1,0:T(8,128)(2,1)} %copy-done.1, bf16[1024,1024]{1,0:T(8,128)(2,1)} %copy-done.21, ...), custom_call_target="tpu_custom_call" | custom-call | flops 1 | bytes 1 | tf_op jit(solution)/shard_map/half_products/pallas_call | solution.py:500
  640.9 12.0 %collective-permute-done.54 = bf16[128,1024]{1,0:T(8,128)(2,1)S(1)} collective-permute-done((bf16[128,1024]{1,0:T(8,128)(2,1)}, bf16[128,1024]{1,0:T(8,128)(2,1)S(1)}, u32[]{:S(2)}, u32[]{:S(2)}) %collective-permute-start.54) | collective-permute-done | bytes 262176 | tf_op jit(solution)/shard_map/ppermute | solution.py:546
  652.9 4.1 collective-permute-done.51
  672.6 16.3 %collective-permute-done.58 = bf16[192,1024]{1,0:T(8,128)(2,1)S(1)} collective-permute-done((bf16[192,1024]{1,0:T(8,128)(2,1)S(1)}, bf16[192,1024]{1,0:T(8,128)(2,1)S(1)}, u32[]{:S(2)}, u32[]{:S(2)}) %collective-permute-start.58) | collective-permute-done | bytes 393248 | tf_op jit(solution)/shard_map/ppermute | solution.py:546
  689.9 7.9 %collective-permute-done.60 = bf16[96,1024]{1,0:T(8,128)(2,1)S(1)} collective-permute-done((bf16[96,1024]{1,0:T(8,128)(2,1)S(1)}, bf16[96,1024]{1,0:T(8,128)(2,1)S(1)}, u32[]{:S(2)}, u32[]{:S(2)}) %collective-permute-start.60) | collective-permute-done | bytes 196640 | tf_op jit(solution)/shard_map/ppermute | solution.py:546
  (542 shorter events, 234.0 us)
Async XLA Ops:
  7.3 253.6 %all-gather.3.cloned.1.call-start = ((), (), s32[]{:S(2)}) async-start(), calls=%async_computation | async-start | bytes 8650752 | tf_op jit(solution)/shard_map/all_gather | solution.py:967
  9.5 22.8 %collective-permute-start = (bf16[32,3200]{1,0:T(8,128)(2,1)S(1)}, bf16[32,3200]{1,0:T(8,128)(2,1)S(1)}, u32[]{:S(2)}, u32[]{:S(2)}) collective-permute-start(bf16[32,3200]{1,0:T(8,128)(2,1)S(1)} %pad_maximum_fusion.30), channel_id=1, source_target_pairs={{0,4},{4,0},{1,5},{5,1},{2,6},{6,2},{3,7},{7,3},{8,12},{12,8},{9,1... | collective-permute-start | bytes 614408 | tf_op jit(solution)/shard_map/ppermute | solution.py:546
  13.6 26.4 %collective-permute-start.1 = (bf16[192,1024]{1,0:T(8,128)(2,1)S(1)}, bf16[192,1024]{1,0:T(8,128)(2,1)S(1)}, u32[]{:S(2)}, u32[]{:S(2)}) collective-permute-start(bf16[192,1024]{1,0:T(8,128)(2,1)S(1)} %pad_maximum_fusion.25), channel_id=1, source_target_pairs={{0,4},{4,0},{1,5},{5,1},{2,6},{6,2},{3,7},{7,3},{8,12},{12,8},{9,1... | collective-permute-start | bytes 1179656 | tf_op jit(solution)/shard_map/ppermute | solution.py:546
  32.5 16.4 %collective-permute-start.2 = (bf16[2,32,3200]{2,1,0:T(8,128)(2,1)S(1)}, bf16[2,32,3200]{2,1,0:T(8,128)(2,1)S(1)}, u32[]{:S(2)}, u32[]{:S(2)}) collective-permute-start(bf16[2,32,3200]{2,1,0:T(8,128)(2,1)S(1)} %pad_maximum_fusion.24), channel_id=1, source_target_pairs={{0,2},{2,0},{1,3},{3,1},{4,6},{6,4},{5,7},{7,5},{8,10},{10,8},{9,1... | collective-permute-start | bytes 1228808 | tf_op jit(solution)/shard_map/ppermute | solution.py:546
  40.1 32.5 %collective-permute-start.5 = (bf16[2,192,1024]{2,1,0:T(8,128)(2,1)S(1)}, bf16[2,192,1024]{2,1,0:T(8,128)(2,1)S(1)}, u32[]{:S(2)}, u32[]{:S(2)}) collective-permute-start(bf16[2,192,1024]{2,1,0:T(8,128)(2,1)S(1)} %pad_maximum_fusion.15), channel_id=1, source_target_pairs={{0,2},{2,0},{1,3},{3,1},{4,6},{6,4},{5,7},{7,5},{8,10},{10,8},{9,1... | collective-permute-start | bytes 2359304 | tf_op jit(solution)/shard_map/ppermute | solution.py:546
  52.1 17.1 %collective-permute-start.6 = (bf16[32,5120]{1,0:T(8,128)(2,1)S(1)}, bf16[32,5120]{1,0:T(8,128)(2,1)S(1)}, u32[]{:S(2)}, u32[]{:S(2)}) collective-permute-start(bf16[32,5120]{1,0:T(8,128)(2,1)S(1)} %pad_maximum_fusion.28), channel_id=1, source_target_pairs={{0,4},{4,0},{1,5},{5,1},{2,6},{6,2},{3,7},{7,3},{8,12},{12,8},{9,1... | collective-permute-start | bytes 983048 | tf_op jit(solution)/shard_map/ppermute | solution.py:546
  61.5 19.7 %collective-permute-start.7 = (bf16[2,2,2,32,1664]{4,3,2,1,0:T(8,128)(2,1)S(1)}, bf16[2,2,2,32,1664]{4,3,2,1,0:T(8,128)(2,1)S(1)}, u32[]{:S(2)}, u32[]{:S(2)}) collective-permute-start(bf16[2,2,2,32,1664]{4,3,2,1,0:T(8,128)(2,1)S(1)} %pad_maximum_fusion.14), channel_id=1, source_target_pairs={{0,16},{16,0},{1,17},{17,1},{2,18},{18,2},{3,19},{19,3},{4,20},{20... | collective-permute-start | bytes 2555912 | tf_op jit(solution)/shard_map/ppermute | solution.py:546
  63.0 17.9 %collective-permute-start.8 = (bf16[2,2,2,32,1536]{4,3,2,1,0:T(8,128)(2,1)S(1)}, bf16[2,2,2,32,1536]{4,3,2,1,0:T(8,128)(2,1)S(1)}, u32[]{:S(2)}, u32[]{:S(2)}) collective-permute-start(bf16[2,2,2,32,1536]{4,3,2,1,0:T(8,128)(2,1)S(1)} %pad_maximum_fusion.16), channel_id=1, source_target_pairs={{0,1},{1,0},{2,3},{3,2},{4,5},{5,4},{6,7},{7,6},{8,9},{9,8},{10,11... | collective-permute-start | bytes 2359304 | tf_op jit(solution)/shard_map/ppermute | solution.py:546
  83.2 22.5 %collective-permute-start.11 = (bf16[2,32,5120]{2,1,0:T(8,128)(2,1)}, bf16[2,32,5120]{2,1,0:T(8,128)(2,1)S(1)}, u32[]{:S(2)}, u32[]{:S(2)}) collective-permute-start(bf16[2,32,5120]{2,1,0:T(8,128)(2,1)} %pad_maximum_fusion.17), channel_id=1, source_target_pairs={{0,2},{2,0},{1,3},{3,1},{4,6},{6,4},{5,7},{7,5},{8,10},{10,8},{9,1... | collective-permute-start | bytes 1966088 | tf_op jit(solution)/shard_map/ppermute | solution.py:546
  83.2 36.7 %collective-permute-start.13 = (bf16[2,2,192,1024]{3,2,1,0:T(8,128)(2,1)}, bf16[2,2,192,1024]{3,2,1,0:T(8,128)(2,1)S(1)}, u32[]{:S(2)}, u32[]{:S(2)}) collective-permute-start(bf16[2,2,192,1024]{3,2,1,0:T(8,128)(2,1)} %pad_maximum_fusion.6), channel_id=1, source_target_pairs={{0,1},{1,0},{2,3},{3,2},{4,5},{5,4},{6,7},{7,6},{8,9},{9,8},{10,11... | collective-permute-start | bytes 4718600 | tf_op jit(solution)/shard_map/ppermute | solution.py:546
  85.7 20.1 %collective-permute-start.12 = (bf16[32,4096]{1,0:T(8,128)(2,1)}, bf16[32,4096]{1,0:T(8,128)(2,1)S(1)}, u32[]{:S(2)}, u32[]{:S(2)}) collective-permute-start(bf16[32,4096]{1,0:T(8,128)(2,1)} %param.28), channel_id=1, source_target_pairs={{0,4},{4,0},{1,5},{5,1},{2,6},{6,2},{3,7},{7,3},{8,12},{12,8},{9,1... | collective-permute-start | bytes 786440 | tf_op jit(solution)/shard_map/ppermute | solution.py:546
  124.4 15.9 %collective-permute-start.14 = (bf16[2,2,32,2560]{3,2,1,0:T(8,128)(2,1)S(1)}, bf16[2,2,32,2560]{3,2,1,0:T(8,128)(2,1)S(1)}, u32[]{:S(2)}, u32[]{:S(2)}) collective-permute-start(bf16[2,2,32,2560]{3,2,1,0:T(8,128)(2,1)S(1)} %get-tuple-element.283), channel_id=1, source_target_pairs={{0,1},{1,0},{2,3},{3,2},{4,5},{5,4},{6,7},{7,6},{8,9},{9,8},{10,11... | collective-permute-start | bytes 1966088 | tf_op jit(solution)/shard_map/ppermute | solution.py:546
  125.8 15.6 %collective-permute-start.15 = (bf16[2,2,32,2560]{3,2,1,0:T(8,128)(2,1)S(1)}, bf16[2,2,32,2560]{3,2,1,0:T(8,128)(2,1)S(1)}, u32[]{:S(2)}, u32[]{:S(2)}) collective-permute-start(bf16[2,2,32,2560]{3,2,1,0:T(8,128)(2,1)S(1)} %get-tuple-element.284), channel_id=1, source_target_pairs={{0,16},{16,0},{1,17},{17,1},{2,18},{18,2},{3,19},{19,3},{4,20},{20... | collective-permute-start | bytes 1966088 | tf_op jit(solution)/shard_map/ppermute | solution.py:546
  145.5 553.2 %all-gather.5.cloned.1.call-start = ((), (), s32[]{:S(2)}) async-start(), calls=%async_computation.1 | async-start | bytes 4325376 | tf_op jit(solution)/shard_map/all_gather | solution.py:1103
  145.6 35.1 %collective-permute-start.17 = (bf16[2,2,2,32,2560]{4,3,2,1,0:T(8,128)(2,1)}, bf16[2,2,2,32,2560]{4,3,2,1,0:T(8,128)(2,1)}, u32[]{:S(2)}, u32[]{:S(2)}) collective-permute-start(bf16[2,2,2,32,2560]{4,3,2,1,0:T(8,128)(2,1)} %pad_maximum_fusion.9), channel_id=1, source_target_pairs={{0,16},{16,0},{1,17},{17,1},{2,18},{18,2},{3,19},{19,3},{4,20},{20... | collective-permute-start | bytes 3932168 | tf_op jit(solution)/shard_map/ppermute | solution.py:546
  147.1 33.5 %collective-permute-start.18 = (bf16[2,2,2,32,2560]{4,3,2,1,0:T(8,128)(2,1)}, bf16[2,2,2,32,2560]{4,3,2,1,0:T(8,128)(2,1)}, u32[]{:S(2)}, u32[]{:S(2)}) collective-permute-start(bf16[2,2,2,32,2560]{4,3,2,1,0:T(8,128)(2,1)} %pad_maximum_fusion.10), channel_id=1, source_target_pairs={{0,1},{1,0},{2,3},{3,2},{4,5},{5,4},{6,7},{7,6},{8,9},{9,8},{10,11... | collective-permute-start | bytes 3932168 | tf_op jit(solution)/shard_map/ppermute | solution.py:546
  185.4 19.6 %collective-permute-start.19 = (bf16[2,2,2,2,32,2560]{5,4,3,2,1,0:T(8,128)(2,1)S(1)}, bf16[2,2,2,2,32,2560]{5,4,3,2,1,0:T(8,128)(2,1)S(1)}, u32[]{:S(2)}, u32[]{:S(2)}) collective-permute-start(bf16[2,2,2,2,32,2560]{5,4,3,2,1,0:T(8,128)(2,1)S(1)} %pad_maximum_fusion.1.left_own), channel_id=1, source_target_pairs={{0,8},{8,0},{1,9},{9,1},{2,10},{10,2},{3,11},{11,3},{4,12},{12,4},... | collective-permute-start | bytes 7864328 | tf_op jit(solution)/shard_map/ppermute | solution.py:546
  185.5 19.5 %collective-permute-start.20 = (bf16[2,2,2,2,32,2560]{5,4,3,2,1,0:T(8,128)(2,1)S(1)}, bf16[2,2,2,2,32,2560]{5,4,3,2,1,0:T(8,128)(2,1)S(1)}, u32[]{:S(2)}, u32[]{:S(2)}) collective-permute-start(bf16[2,2,2,2,32,2560]{5,4,3,2,1,0:T(8,128)(2,1)S(1)} %pad_maximum_fusion.2.right_own), channel_id=1, source_target_pairs={{0,8},{8,0},{1,9},{9,1},{2,10},{10,2},{3,11},{11,3},{4,12},{12,4},... | collective-permute-start | bytes 7864328 | tf_op jit(solution)/shard_map/ppermute | solution.py:546
  186.0 16.6 %collective-permute-start.21 = (bf16[2,2,32,2048]{3,2,1,0:T(8,128)(2,1)S(1)}, bf16[2,2,32,2048]{3,2,1,0:T(8,128)(2,1)S(1)}, u32[]{:S(2)}, u32[]{:S(2)}) collective-permute-start(bf16[2,2,32,2048]{3,2,1,0:T(8,128)(2,1)S(1)} %copy-done.93), channel_id=1, source_target_pairs={{0,1},{1,0},{2,3},{3,2},{4,5},{5,4},{6,7},{7,6},{8,9},{9,8},{10,11... | collective-permute-start | bytes 1572872 | tf_op jit(solution)/shard_map/ppermute | solution.py:546
  187.3 17.7 %collective-permute-start.22 = (bf16[2,2,32,2048]{3,2,1,0:T(8,128)(2,1)S(1)}, bf16[2,2,32,2048]{3,2,1,0:T(8,128)(2,1)S(1)}, u32[]{:S(2)}, u32[]{:S(2)}) collective-permute-start(bf16[2,2,32,2048]{3,2,1,0:T(8,128)(2,1)S(1)} %copy-done.92), channel_id=1, source_target_pairs={{0,16},{16,0},{1,17},{17,1},{2,18},{18,2},{3,19},{19,3},{4,20},{20... | collective-permute-start | bytes 1572872 | tf_op jit(solution)/shard_map/ppermute | solution.py:546
  206.7 31.8 %collective-permute-start.23 = (bf16[2,2,2,32,2048]{4,3,2,1,0:T(8,128)(2,1)S(1)}, bf16[2,2,2,32,2048]{4,3,2,1,0:T(8,128)(2,1)}, u32[]{:S(2)}, u32[]{:S(2)}) collective-permute-start(bf16[2,2,2,32,2048]{4,3,2,1,0:T(8,128)(2,1)S(1)} %pad_maximum_fusion.12), channel_id=1, source_target_pairs={{0,16},{16,0},{1,17},{17,1},{2,18},{18,2},{3,19},{19,3},{4,20},{20... | collective-permute-start | bytes 3145736 | tf_op jit(solution)/shard_map/ppermute | solution.py:546
  207.5 31.0 %collective-permute-start.24 = (bf16[2,2,2,32,2048]{4,3,2,1,0:T(8,128)(2,1)S(1)}, bf16[2,2,2,32,2048]{4,3,2,1,0:T(8,128)(2,1)}, u32[]{:S(2)}, u32[]{:S(2)}) collective-permute-start(bf16[2,2,2,32,2048]{4,3,2,1,0:T(8,128)(2,1)S(1)} %pad_maximum_fusion.13), channel_id=1, source_target_pairs={{0,1},{1,0},{2,3},{3,2},{4,5},{5,4},{6,7},{7,6},{8,9},{9,8},{10,11... | collective-permute-start | bytes 3145736 | tf_op jit(solution)/shard_map/ppermute | solution.py:546
  354.6 42.0 %collective-permute-start.29 = (bf16[1024,512]{1,0:T(8,128)(2,1)}, bf16[1024,512]{1,0:T(8,128)(2,1)}, u32[]{:S(2)}, u32[]{:S(2)}) collective-permute-start(bf16[1024,512]{1,0:T(8,128)(2,1)} %bitcast.73), channel_id=1, source_target_pairs={{0,16},{16,0},{1,17},{17,1},{2,18},{18,2},{3,19},{19,3},{4,20},{20... | collective-permute-start | bytes 3145736 | tf_op jit(solution)/shard_map/ppermute | solution.py:546
  355.8 40.8 %collective-permute-start.30 = (bf16[1024,512]{1,0:T(8,128)(2,1)}, bf16[1024,512]{1,0:T(8,128)(2,1)}, u32[]{:S(2)}, u32[]{:S(2)}) collective-permute-start(bf16[1024,512]{1,0:T(8,128)(2,1)} %bitcast.74), channel_id=1, source_target_pairs={{0,1},{1,0},{2,3},{3,2},{4,5},{5,4},{6,7},{7,6},{8,9},{9,8},{10,11... | collective-permute-start | bytes 3145736 | tf_op jit(solution)/shard_map/ppermute | solution.py:546
  357.7 44.8 %collective-permute-start.31 = (bf16[256,2048]{1,0:T(8,128)(2,1)}, bf16[256,2048]{1,0:T(8,128)(2,1)}, u32[]{:S(2)}, u32[]{:S(2)}) collective-permute-start(bf16[256,2048]{1,0:T(8,128)(2,1)} %bitcast.77), channel_id=1, source_target_pairs={{0,16},{16,0},{1,17},{17,1},{2,18},{18,2},{3,19},{19,3},{4,20},{20... | collective-permute-start | bytes 3145736 | tf_op jit(solution)/shard_map/ppermute | solution.py:546
  358.3 45.3 %collective-permute-start.32 = (bf16[256,2048]{1,0:T(8,128)(2,1)}, bf16[256,2048]{1,0:T(8,128)(2,1)}, u32[]{:S(2)}, u32[]{:S(2)}) collective-permute-start(bf16[256,2048]{1,0:T(8,128)(2,1)} %bitcast.78), channel_id=1, source_target_pairs={{0,1},{1,0},{2,3},{3,2},{4,5},{5,4},{6,7},{7,6},{8,9},{9,8},{10,11... | collective-permute-start | bytes 3145736 | tf_op jit(solution)/shard_map/ppermute | solution.py:546
  414.2 34.6 %collective-permute-start.33 = (bf16[5,512,1024]{2,1,0:T(8,128)(2,1)}, bf16[5,512,1024]{2,1,0:T(8,128)(2,1)}, u32[]{:S(2)}, u32[]{:S(2)}) collective-permute-start(bf16[5,512,1024]{2,1,0:T(8,128)(2,1)} %half_products.4), channel_id=1, source_target_pairs={{0,8},{8,0},{1,9},{9,1},{2,10},{10,2},{3,11},{11,3},{4,12},{12,4},... | collective-permute-start | bytes 15728648 | tf_op jit(solution)/shard_map/ppermute | solution.py:546
  421.4 15.1 %collective-permute-start.34 = (bf16[512,512]{1,0:T(8,128)(2,1)}, bf16[512,512]{1,0:T(8,128)(2,1)}, u32[]{:S(2)}, u32[]{:S(2)}) collective-permute-start(bf16[512,512]{1,0:T(8,128)(2,1)} %bitcast.446), channel_id=1, source_target_pairs={{0,1},{1,0},{2,3},{3,2},{4,5},{5,4},{6,7},{7,6},{8,9},{9,8},{10,11... | collective-permute-start | bytes 1572872 | tf_op jit(solution)/shard_map/ppermute | solution.py:546
  423.8 23.5 %collective-permute-start.36 = (bf16[128,2048]{1,0:T(8,128)(2,1)}, bf16[128,2048]{1,0:T(8,128)(2,1)}, u32[]{:S(2)}, u32[]{:S(2)}) collective-permute-start(bf16[128,2048]{1,0:T(8,128)(2,1)} %bitcast.444), channel_id=1, source_target_pairs={{0,1},{1,0},{2,3},{3,2},{4,5},{5,4},{6,7},{7,6},{8,9},{9,8},{10,11... | collective-permute-start | bytes 1572872 | tf_op jit(solution)/shard_map/ppermute | solution.py:546
  424.2 24.6 %collective-permute-start.37 = (bf16[128,2048]{1,0:T(8,128)(2,1)}, bf16[128,2048]{1,0:T(8,128)(2,1)}, u32[]{:S(2)}, u32[]{:S(2)}) collective-permute-start(bf16[128,2048]{1,0:T(8,128)(2,1)} %bitcast.443), channel_id=1, source_target_pairs={{0,16},{16,0},{1,17},{17,1},{2,18},{18,2},{3,19},{19,3},{4,20},{20... | collective-permute-start | bytes 1572872 | tf_op jit(solution)/shard_map/ppermute | solution.py:546
  471.1 48.6 %collective-permute-start.39 = (bf16[1280,512]{1,0:T(8,128)(2,1)}, bf16[1280,512]{1,0:T(8,128)(2,1)}, u32[]{:S(2)}, u32[]{:S(2)}) collective-permute-start(bf16[1280,512]{1,0:T(8,128)(2,1)} %bitcast.113), channel_id=1, source_target_pairs={{0,16},{16,0},{1,17},{17,1},{2,18},{18,2},{3,19},{19,3},{4,20},{20... | collective-permute-start | bytes 3932168 | tf_op jit(solution)/shard_map/ppermute | solution.py:546
  471.7 48.0 %collective-permute-start.40 = (bf16[1280,512]{1,0:T(8,128)(2,1)}, bf16[1280,512]{1,0:T(8,128)(2,1)}, u32[]{:S(2)}, u32[]{:S(2)}) collective-permute-start(bf16[1280,512]{1,0:T(8,128)(2,1)} %bitcast.114), channel_id=1, source_target_pairs={{0,1},{1,0},{2,3},{3,2},{4,5},{5,4},{6,7},{7,6},{8,9},{9,8},{10,11... | collective-permute-start | bytes 3932168 | tf_op jit(solution)/shard_map/ppermute | solution.py:546
  472.1 47.5 %collective-permute-start.38 = (bf16[64,4096]{1,0:T(8,128)(2,1)}, bf16[64,4096]{1,0:T(8,128)(2,1)S(1)}, u32[]{:S(2)}, u32[]{:S(2)}) collective-permute-start(bf16[64,4096]{1,0:T(8,128)(2,1)} %bitcast.124), channel_id=1, source_target_pairs={{0,2},{2,0},{1,3},{3,1},{4,6},{6,4},{5,7},{7,5},{8,10},{10,8},{9,1... | collective-permute-start | bytes 1572872 | tf_op jit(solution)/shard_map/ppermute | solution.py:546
  473.5 46.2 %collective-permute-start.41 = (bf16[256,1024]{1,0:T(8,128)(2,1)}, bf16[256,1024]{1,0:T(8,128)(2,1)S(1)}, u32[]{:S(2)}, u32[]{:S(2)}) collective-permute-start(bf16[256,1024]{1,0:T(8,128)(2,1)} %bitcast.119), channel_id=1, source_target_pairs={{0,2},{2,0},{1,3},{3,1},{4,6},{6,4},{5,7},{7,5},{8,10},{10,8},{9,1... | collective-permute-start | bytes 1572872 | tf_op jit(solution)/shard_map/ppermute | solution.py:546
  526.7 49.9 %collective-permute-start.46 = (bf16[512,1024]{1,0:T(8,128)(2,1)}, bf16[512,1024]{1,0:T(8,128)(2,1)}, u32[]{:S(2)}, u32[]{:S(2)}) collective-permute-start(bf16[512,1024]{1,0:T(8,128)(2,1)} %bitcast.139), channel_id=1, source_target_pairs={{0,1},{1,0},{2,3},{3,2},{4,5},{5,4},{6,7},{7,6},{8,9},{9,8},{10,11... | collective-permute-start | bytes 3145736 | tf_op jit(solution)/shard_map/ppermute | solution.py:546
  529.8 20.4 %collective-permute-start.42 = (bf16[128,1024]{1,0:T(8,128)(2,1)S(1)}, bf16[128,1024]{1,0:T(8,128)(2,1)S(1)}, u32[]{:S(2)}, u32[]{:S(2)}) collective-permute-start(bf16[128,1024]{1,0:T(8,128)(2,1)S(1)} %dynamic-slice_bitcast_fusion.2), channel_id=1, source_target_pairs={{0,4},{4,0},{1,5},{5,1},{2,6},{6,2},{3,7},{7,3},{8,12},{12,8},{9,1... | collective-permute-start | bytes 786440 | tf_op jit(solution)/shard_map/ppermute | solution.py:546
  534.0 21.8 %collective-permute-start.43 = (bf16[32,4096]{1,0:T(8,128)(2,1)S(1)}, bf16[32,4096]{1,0:T(8,128)(2,1)}, u32[]{:S(2)}, u32[]{:S(2)}) collective-permute-start(bf16[32,4096]{1,0:T(8,128)(2,1)S(1)} %dynamic-slice_bitcast_fusion.3), channel_id=1, source_target_pairs={{0,4},{4,0},{1,5},{5,1},{2,6},{6,2},{3,7},{7,3},{8,12},{12,8},{9,1... | collective-permute-start | bytes 786440 | tf_op jit(solution)/shard_map/ppermute | solution.py:546
  534.1 42.4 %collective-permute-start.44 = (bf16[640,512]{1,0:T(8,128)(2,1)}, bf16[640,512]{1,0:T(8,128)(2,1)S(1)}, u32[]{:S(2)}, u32[]{:S(2)}) collective-permute-start(bf16[640,512]{1,0:T(8,128)(2,1)} %bitcast.131), channel_id=1, source_target_pairs={{0,1},{1,0},{2,3},{3,2},{4,5},{5,4},{6,7},{7,6},{8,9},{9,8},{10,11... | collective-permute-start | bytes 1966088 | tf_op jit(solution)/shard_map/ppermute | solution.py:546
  535.8 40.8 %collective-permute-start.45 = (bf16[640,512]{1,0:T(8,128)(2,1)}, bf16[640,512]{1,0:T(8,128)(2,1)}, u32[]{:S(2)}, u32[]{:S(2)}) collective-permute-start(bf16[640,512]{1,0:T(8,128)(2,1)} %bitcast.134), channel_id=1, source_target_pairs={{0,16},{16,0},{1,17},{17,1},{2,18},{18,2},{3,19},{19,3},{4,20},{20... | collective-permute-start | bytes 1966088 | tf_op jit(solution)/shard_map/ppermute | solution.py:546
  581.7 28.0 %collective-permute-start.47 = (bf16[320,1024]{1,0:T(8,128)(2,1)S(1)}, bf16[320,1024]{1,0:T(8,128)(2,1)S(1)}, u32[]{:S(2)}, u32[]{:S(2)}) collective-permute-start(bf16[320,1024]{1,0:T(8,128)(2,1)S(1)} %bitcast.435), channel_id=1, source_target_pairs={{0,2},{2,0},{1,3},{3,1},{4,6},{6,4},{5,7},{7,5},{8,10},{10,8},{9,1... | collective-permute-start | bytes 1966088 | tf_op jit(solution)/shard_map/ppermute | solution.py:546
  585.5 15.4 %collective-permute-start.49 = (bf16[256,1024]{1,0:T(8,128)(2,1)}, bf16[256,1024]{1,0:T(8,128)(2,1)S(1)}, u32[]{:S(2)}, u32[]{:S(2)}) collective-permute-start(bf16[256,1024]{1,0:T(8,128)(2,1)} %bitcast.149), channel_id=1, source_target_pairs={{0,1},{1,0},{2,3},{3,2},{4,5},{5,4},{6,7},{7,6},{8,9},{9,8},{10,11... | collective-permute-start | bytes 1572872 | tf_op jit(solution)/shard_map/ppermute | solution.py:546
  587.0 22.7 %collective-permute-start.48 = (bf16[256,1024]{1,0:T(8,128)(2,1)}, bf16[256,1024]{1,0:T(8,128)(2,1)S(1)}, u32[]{:S(2)}, u32[]{:S(2)}) collective-permute-start(bf16[256,1024]{1,0:T(8,128)(2,1)} %bitcast.147), channel_id=1, source_target_pairs={{0,2},{2,0},{1,3},{3,1},{4,6},{6,4},{5,7},{7,5},{8,10},{10,8},{9,1... | collective-permute-start | bytes 1572872 | tf_op jit(solution)/shard_map/ppermute | solution.py:546
  620.9 32.0 %collective-permute-start.53 = (bf16[160,1024]{1,0:T(8,128)(2,1)}, bf16[160,1024]{1,0:T(8,128)(2,1)S(1)}, u32[]{:S(2)}, u32[]{:S(2)}) collective-permute-start(bf16[160,1024]{1,0:T(8,128)(2,1)} %bitcast.459), channel_id=1, source_target_pairs={{0,4},{4,0},{1,5},{5,1},{2,6},{6,2},{3,7},{7,3},{8,12},{12,8},{9,1... | collective-permute-start | bytes 983048 | tf_op jit(solution)/shard_map/ppermute | solution.py:546
  621.1 31.8 %collective-permute-start.54 = (bf16[128,1024]{1,0:T(8,128)(2,1)}, bf16[128,1024]{1,0:T(8,128)(2,1)S(1)}, u32[]{:S(2)}, u32[]{:S(2)}) collective-permute-start(bf16[128,1024]{1,0:T(8,128)(2,1)} %dynamic-slice_bitcast_fusion.1), channel_id=1, source_target_pairs={{0,4},{4,0},{1,5},{5,1},{2,6},{6,2},{3,7},{7,3},{8,12},{12,8},{9,1... | collective-permute-start | bytes 786440 | tf_op jit(solution)/shard_map/ppermute | solution.py:546
  623.8 29.1 %collective-permute-start.55 = (bf16[128,1024]{1,0:T(8,128)(2,1)S(1)}, bf16[128,1024]{1,0:T(8,128)(2,1)S(1)}, u32[]{:S(2)}, u32[]{:S(2)}) collective-permute-start(bf16[128,1024]{1,0:T(8,128)(2,1)S(1)} %bitcast.462), channel_id=1, source_target_pairs={{0,2},{2,0},{1,3},{3,1},{4,6},{6,4},{5,7},{7,5},{8,10},{10,8},{9,1... | collective-permute-start | bytes 786440 | tf_op jit(solution)/shard_map/ppermute | solution.py:546
  635.1 21.9 %collective-permute-start.51 = (bf16[768,512]{1,0:T(8,128)(2,1)S(1)}, bf16[768,512]{1,0:T(8,128)(2,1)S(1)}, u32[]{:S(2)}, u32[]{:S(2)}) collective-permute-start(bf16[768,512]{1,0:T(8,128)(2,1)S(1)} %bitcast.425), channel_id=1, source_target_pairs={{0,16},{16,0},{1,17},{17,1},{2,18},{18,2},{3,19},{19,3},{4,20},{20... | collective-permute-start | bytes 2359304 | tf_op jit(solution)/shard_map/ppermute | solution.py:546
  636.8 20.7 %collective-permute-start.52 = (bf16[768,512]{1,0:T(8,128)(2,1)S(1)}, bf16[768,512]{1,0:T(8,128)(2,1)S(1)}, u32[]{:S(2)}, u32[]{:S(2)}) collective-permute-start(bf16[768,512]{1,0:T(8,128)(2,1)S(1)} %bitcast.427), channel_id=1, source_target_pairs={{0,1},{1,0},{2,3},{3,2},{4,5},{5,4},{6,7},{7,6},{8,9},{9,8},{10,11... | collective-permute-start | bytes 2359304 | tf_op jit(solution)/shard_map/ppermute | solution.py:546
  669.4 19.6 %collective-permute-start.58 = (bf16[192,1024]{1,0:T(8,128)(2,1)S(1)}, bf16[192,1024]{1,0:T(8,128)(2,1)S(1)}, u32[]{:S(2)}, u32[]{:S(2)}) collective-permute-start(bf16[192,1024]{1,0:T(8,128)(2,1)S(1)} %bitcast.455), channel_id=1, source_target_pairs={{0,2},{2,0},{1,3},{3,1},{4,6},{6,4},{5,7},{7,5},{8,10},{10,8},{9,1... | collective-permute-start | bytes 1179656 | tf_op jit(solution)/shard_map/ppermute | solution.py:546
  (139 other events, 1194.2 us)
Sparse Core Ops, SparseCore 0:
  145.6 91.8 all-gather.2
  615.6 77.7 all-gather.4
